TPU v7x, 256 devices: a whole 4x4x8 slice. The times are simulated.
256 devices in a mesh: tile: 8 (over z), text: 32 (over y, x, core).
Axes of the slice: x: 4, y: 4, z: 8, core: 2. Of those that a mesh axis runs over, the one named last changes fastest.
Arguments:
- grad_seq: bfloat16 [10240, 8192], P('text', 'tile'), may hold values from -6 to 6
- positions: int32 [10240], replicated, may hold values from 0 to 10239, each once
- pre_act: bfloat16 [10240, 5120], P('tile', 'text'), may hold values from -6 to 6
- w_out: bfloat16 [5120, 8192], P('text', 'tile'), may hold values from -0.078125 to 0.078125
Outputs:
- grad_pre: float32 [10240, 5120], P('tile', 'text')
- grad_w_out: float32 [5120, 8192], P('text', 'tile')
- grad_bias: float32 [8192], P('tile')
Inputs may be any that keep to these rules, and one draw needn't show every extreme that they name: positions names every place 0 to 10239 once.
All inputs are finite; a program needn't handle non-finite values.
Results may differ from a plain program's by a relative error of at most 0.003.
Values may be sent and summed in bfloat16 or wider, within the bound.
No kernel may reach another device: no remote copies, remote signals or barrier semaphores. Data moves between devices by JAX's collectives and lax.ppermute only.
A program may use at most 128 MiB of HBM per device.

v0:
```python
import functools

import jax
import jax.numpy as jnp
from jax import lax
from jax.experimental import pallas as pl
from jax.experimental.pallas import tpu as pltpu
from jax.sharding import PartitionSpec as P

SIDE = 4
N_TEXT = 2 * SIDE * SIDE
N_TILE = 8
ROWS = 320
HID = 160
BLOCK = 1280
SLOTS = 10240
WIDTH = 1024
HALF = HID // 2
LANES = 128
GROUPS = 4
GROUP_ROWS = 4 * ROWS
UNROLL = 32
F32 = jnp.float32
BF16 = jnp.bfloat16


def plane_perm(step0, step1):
    pairs = []
    for y in range(SIDE):
        for x in range(SIDE):
            for core, (dy, dx) in ((0, step0), (1, step1)):
                target = (((y + dy) % SIDE) * SIDE + (x + dx) % SIDE) * 2 + core
                pairs.append(((y * SIDE + x) * 2 + core, target))
    return pairs


FIRST_UP = plane_perm((0, 1), (1, 0))
FIRST_DOWN = plane_perm((0, -1), (-1, 0))
SECOND_UP = plane_perm((1, 0), (0, 1))
SECOND_DOWN = plane_perm((-1, 0), (0, -1))
ARRIVAL = [(0, 0), (1, 0), (3, 0), (0, 1), (0, 3), (1, 1), (2, 0), (3, 1), (1, 3), (3, 3), (0, 2), (2, 1), (2, 3), (1, 2), (3, 2), (2, 2)]
SWAP = [(i, i ^ 1) for i in range(N_TEXT)]
TILE_UP = [(i, (i + 1) % N_TILE) for i in range(N_TILE)]
TILE_DOWN = [(i, (i - 1) % N_TILE) for i in range(N_TILE)]


def arrival_place(device, me):
    core, x, y = device & 1, (device >> 1) & 3, device >> 3
    my_core, my_x, my_y = me & 1, (me >> 1) & 3, me >> 3
    dx, dy = (my_x - x) & 3, (my_y - y) & 3
    first = jnp.where(core == 0, dx, dy)
    second = jnp.where(core == 0, dy, dx)
    codes = [sum(ARRIVAL.index((i, j)) << (4 * i) for i in range(SIDE)) for j in range(SIDE)]
    code = jnp.where(second == 0, codes[0], jnp.where(second == 1, codes[1], jnp.where(second == 2, codes[2], codes[3])))
    return (core ^ my_core) * 16 + ((code >> (4 * first)) & 15)


def store_rows(ref, start, value):
    count = value.shape[0]
    ref[pl.ds(start, count, stride=2), :] = value[:, :LANES]
    ref[pl.ds(start + 1, count, stride=2), 0:HID - LANES] = value[:, LANES:]


def load_turned(ref, start, count):
    left = ref[pl.ds(start, count, stride=2), :].T
    right = ref[pl.ds(start + 1, count, stride=2), :].T
    return left, right[0:HID - LANES]


def act_kernel(place_ref, act_ref, mine_ref, theirs_ref, rows, turned):
    block = pl.program_id(0)
    store_rows(turned, 0, act_ref[0].astype(F32).T)

    @pl.loop(0, BLOCK, step=UNROLL)
    def _(start):
        held = [turned[pl.ds(pl.multiple_of(2 * start, 2) + 2 * i, 2), :] for i in range(UNROLL)]
        for i in range(UNROLL):
            where = pl.multiple_of(place_ref[block * BLOCK + start + i], 2)
            rows[pl.ds(where, 2), :] = held[i]

    @pl.when(block == N_TILE - 1)
    def _():
        for group in range(2 * GROUPS):
            left, right = load_turned(rows, group * 2 * GROUP_ROWS, GROUP_ROWS)
            out_ref = (mine_ref, theirs_ref)[group // GROUPS]
            out_ref[group % GROUPS, 0:LANES, :] = left.astype(BF16)
            out_ref[group % GROUPS, LANES:HID, :] = right.astype(BF16)


def act_in_arrival_order(place, act):
    return pl.pallas_call(
        act_kernel,
        out_shape=[jax.ShapeDtypeStruct((GROUPS, HID, GROUP_ROWS), BF16)] * 2,
        grid_spec=pltpu.PrefetchScalarGridSpec(
            num_scalar_prefetch=1,
            grid=(N_TILE,),
            in_specs=[pl.BlockSpec((1, HID, BLOCK), lambda i, place: (i, 0, 0))],
            out_specs=[pl.BlockSpec((GROUPS, HID, GROUP_ROWS), lambda i, place: (0, 0, 0), pipeline_mode=pl.Buffered(1))] * 2,
            scratch_shapes=[pltpu.VMEM((2 * SLOTS, LANES), F32), pltpu.VMEM((2 * BLOCK, LANES), F32)],
        ),
        compiler_params=pltpu.CompilerParams(vmem_limit_bytes=17 * 2**20),
        cost_estimate=pl.CostEstimate(flops=0, bytes_accessed=70_000_000, transcendentals=0),
        name="act_rows",
    )(place, act)


def product_kernel(hand_on, weight_ref, *refs):
    pieces = refs[:4]
    if hand_on is None:
        mine_ref, theirs_ref, sums_ref = refs[-3:]
    else:
        mine_ref, theirs_ref, sums_ref, next_ref, sem = refs[-5:]
        copy = pltpu.make_async_copy(pieces[hand_on], next_ref, sem)
        copy.start()
    for k in range(4):
        piece = pieces[k][...]
        term = lax.dot_general(piece, weight_ref[...], (((1,), (1,)), ((), ())), preferred_element_type=F32)
        store_rows(mine_ref, 2 * k * ROWS, term[:, :HID])
        store_rows(theirs_ref, 2 * k * ROWS, term[:, HID:])
        sums_ref[k:k + 1, :] = jnp.sum(piece.astype(F32), axis=0, keepdims=True)
    if hand_on is not None:
        copy.wait()


def products_of(weight, pieces, after, hand_on=None):
    vmem, anywhere = pl.BlockSpec(memory_space=pltpu.VMEM), pl.BlockSpec(memory_space=pl.ANY)
    half = jax.ShapeDtypeStruct((2 * GROUP_ROWS, LANES), F32)
    out = [pltpu.VMEM(half.shape, F32), half, jax.ShapeDtypeStruct((4, WIDTH), F32)]
    return pl.pallas_call(
        functools.partial(product_kernel, hand_on),
        out_shape=out + [jax.ShapeDtypeStruct((ROWS, WIDTH), BF16)] * (hand_on is not None),
        in_specs=[vmem] * 5 + [anywhere] * len(after),
        out_specs=[vmem] * 3 + [anywhere] * (hand_on is not None),
        scratch_shapes=[pltpu.SemaphoreType.DMA(())] * (hand_on is not None),
        compiler_params=pltpu.CompilerParams(vmem_limit_bytes=6 * 2**20),
        cost_estimate=pl.CostEstimate(flops=1_300_000_000, bytes_accessed=8_000_000, transcendentals=0),
        name="products",
    )(weight, *pieces, *after)


def slot_kernel(count, place_ref, blocks_ref, *refs):
    if len(refs) == 3:
        rows_ref, out_ref, picked = refs
    else:
        rows_ref, out_ref, picked, sems = refs[8:]
        copies = [
            pltpu.make_async_copy(refs[k], rows_ref.at[pl.ds(k * 2 * GROUP_ROWS, 2 * GROUP_ROWS), :], sems.at[k])
            for k in range(8)
        ]
        for copy in copies:
            copy.start()
        for copy in copies:
            copy.wait()

    @pl.loop(0, count)
    def _(b):
        base = blocks_ref[b] * BLOCK

        @pl.loop(0, BLOCK, step=UNROLL)
        def _(start):
            held = []
            for i in range(UNROLL):
                where = pl.multiple_of(place_ref[base + start + i], 2)
                held.append(rows_ref[pl.ds(where, 2), :])
            for i in range(UNROLL):
                picked[pl.ds(pl.multiple_of(2 * start, 2) + 2 * i, 2), :] = held[i]

        left, right = load_turned(picked, 0, BLOCK)
        out_ref[b, 0:LANES, :] = left
        out_ref[b, LANES:HID, :] = right


def to_slot_order(place, blocks, rows):
    count = blocks.shape[0]
    vmem = pl.BlockSpec(memory_space=pltpu.VMEM)
    out = [pltpu.VMEM((count, HID, BLOCK), F32)]
    whole = len(rows) == 1
    if not whole:
        out.insert(0, pltpu.VMEM((2 * SLOTS, LANES), F32))
    return pl.pallas_call(
        functools.partial(slot_kernel, count),
        out_shape=out,
        in_specs=[pl.BlockSpec(memory_space=pltpu.SMEM)] * 2
        + ([vmem] if whole else [pl.BlockSpec(memory_space=pl.ANY)] * len(rows)),
        out_specs=[vmem] * len(out),
        scratch_shapes=[pltpu.VMEM((2 * BLOCK, LANES), F32)] + [pltpu.SemaphoreType.DMA((8,))] * (not whole),
        compiler_params=pltpu.CompilerParams(vmem_limit_bytes=(5 if whole else 46) * 2**20),
        cost_estimate=pl.CostEstimate(flops=0, bytes_accessed=8_000_000 * count, transcendentals=0),
        name="slot_rows",
    )(place, blocks, *rows)


def weight_kernel(first, mine_ref, theirs_ref, *refs):
    pieces = refs[:4]
    out_mine, out_theirs, held, sems = refs[-4:]
    copies = [
        pltpu.make_async_copy(piece, held.at[pl.ds(k * ROWS, ROWS), :], sems.at[k]) for k, piece in enumerate(pieces)
    ]
    for copy in copies:
        copy.start()
    for copy in copies:
        copy.wait()
    act = jnp.concatenate([mine_ref[...], theirs_ref[...]], axis=0)
    for n in range(0, WIDTH, 256):
        columns = slice(n, n + 256)
        term = jnp.dot(act, held[:, columns], preferred_element_type=F32)
        out_mine[:, columns] = term[:HID] if first else refs[4][:, columns] + term[:HID]
        out_theirs[:, columns] = term[HID:] if first else refs[5][:, columns] + term[HID:]


def weight_term(mine, theirs, pieces, totals):
    vmem = pl.BlockSpec(memory_space=pltpu.VMEM)
    return pl.pallas_call(
        functools.partial(weight_kernel, not totals),
        out_shape=[jax.ShapeDtypeStruct((HID, WIDTH), F32)] * 2,
        in_specs=[vmem] * 2 + [pl.BlockSpec(memory_space=pl.ANY)] * 4 + [vmem] * len(totals),
        out_specs=[vmem] * 2,
        scratch_shapes=[pltpu.VMEM((GROUP_ROWS, WIDTH), BF16), pltpu.SemaphoreType.DMA((4,))],
        compiler_params=pltpu.CompilerParams(vmem_limit_bytes=6 * 2**20),
        cost_estimate=pl.CostEstimate(flops=1_300_000_000, bytes_accessed=8_000_000, transcendentals=0),
        name="weight_term",
    )(mine, theirs, *pieces, *totals)


def gelu_parts(pre):
    value = pre.astype(F32)
    cdf = 0.5 * (1.0 + jax.scipy.special.erf(value * 0.7071067811865476))
    activated = value * cdf
    slope = cdf + value * jnp.exp(-0.5 * value * value) * 0.3989422804014327
    return activated, slope


def body(grad_seq, positions, pre_act, w_out):
    me = lax.axis_index("text")
    place = 2 * (arrival_place(positions // ROWS, me) * ROWS + positions % ROWS)
    piece_of = arrival_place(jnp.arange(N_TEXT, dtype=jnp.int32), me)

    activated, slope = gelu_parts(pre_act.T)
    act_all = lax.all_gather(activated.astype(BF16), "tile", axis=0)
    swap = lambda value: lax.ppermute(value, "text", SWAP)
    send = lambda value, perm: lax.ppermute(value, "text", perm)
    weight = jnp.concatenate([w_out, swap(w_out)], axis=0)
    act_mine, act_theirs = act_in_arrival_order(place, act_all)
    act_theirs = swap(act_theirs)

    got = {(0, 0): grad_seq, (1, 0): send(grad_seq, FIRST_UP), (3, 0): send(grad_seq, FIRST_DOWN)}
    got[0, 1], got[0, 3] = send(grad_seq, SECOND_UP), send(grad_seq, SECOND_DOWN)
    got[2, 0] = send(got[1, 0], FIRST_UP)
    for first in (1, 3, 2):
        got[first, 1], got[first, 3] = send(got[first, 0], SECOND_UP), send(got[first, 0], SECOND_DOWN)
    mine, theirs, sums = [], [], []
    for g in range(GROUPS):
        pieces = [got[key] for key in ARRIVAL[4 * g:4 * g + 4]]
        after = [act_mine] if g == GROUPS - 1 else []
        kept, sent, part, *handed = products_of(weight, pieces, after, {0: 3, 1: 1}.get(g))
        if g == 0:
            got[0, 2] = send(handed[0], SECOND_UP)
        if g == 1:
            got[1, 2] = send(handed[0], SECOND_UP)
            got[3, 2], got[2, 2] = send(got[3, 3], SECOND_DOWN), send(got[2, 3], SECOND_DOWN)
        mine.append(kept)
        theirs.append(swap(sent))
        sums.append(part)
    groups = [[got[key] for key in ARRIVAL[4 * g:4 * g + 4]] for g in range(GROUPS)]
    tile = lax.axis_index("tile")
    rows, early = to_slot_order(place, (tile + jnp.array([4, 3, 5], jnp.int32)) % N_TILE, mine + theirs)
    (late,) = to_slot_order(place, (tile + jnp.array([2, 6, 1, 7, 0], jnp.int32)) % N_TILE, [rows])
    up = lambda value: lax.ppermute(value.astype(BF16), "tile", TILE_UP).astype(F32)
    down = lambda value: lax.ppermute(value.astype(BF16), "tile", TILE_DOWN).astype(F32)
    rise, fall = up(early[0, :HALF]), down(early[0, HALF:])
    rise = up(jnp.concatenate([rise + early[1, :HALF], early[1, HALF:]], axis=0))
    fall = down(jnp.concatenate([early[2, :HALF], fall + early[2, HALF:]], axis=0))
    rise, fall = up(rise + late[0]), down(fall + late[1])
    rise, fall = up(rise + late[2]), down(fall + late[3])
    grad_pre = (late[4] + rise + fall) * slope
    totals = []
    for g in range(GROUPS):
        totals = weight_term(act_mine[g], act_theirs[g], groups[g], totals)
    grad_w = totals[0] + swap(totals[1])
    sums = jnp.concatenate(sums, axis=0)
    sums = jnp.concatenate([sums, swap(sums)], axis=0)
    grad_bias = jnp.sum(sums[piece_of], axis=0)
    return grad_pre.T, grad_w, grad_bias


def solution(mesh):
    in_specs = (P("text", "tile"), P(), P("tile", "text"), P("text", "tile"))
    out_specs = (P("tile", "text"), P("text", "tile"), P("tile"))
    return jax.shard_map(body, mesh=mesh, in_specs=in_specs, out_specs=out_specs, check_vma=False)
```

profile of v0, /device:TPU:1, one launch (start us, length us, event | category | flops | bytes accessed | tf_op | source)
XLA Modules:
  0.0 179.7 jit_solution(6583989393717699120)
XLA Ops:
  15.7 6.6 %collective-permute-done.1.refs_1_ = bf16[320,1024]{1,0:T(8,128)(2,1)S(1)} collective-permute-done((bf16[320,1024]{1,0:T(8,128)(2,1)}, bf16[320,1024]{1,0:T(8,128)(2,1)S(1)}, u32[]{:S(2)}, u32[]{:S(2)}) %collective-permute-start.1) | collective-permute-done | bytes 655392 | tf_op jit(solution)/shard_map/ppermute | solution.py:241
  23.8 7.8 %collective-permute-start = (bf16[160,1024]{1,0:T(8,128)(2,1)}, bf16[160,1024]{1,0:T(8,128)(2,1)S(1)}, u32[]{:S(2)}, u32[]{:S(2)}) collective-permute-start(bf16[160,1024]{1,0:T(8,128)(2,1)} %param.9), channel_id=1, source_target_pairs={{0,1},{1,0},{2,3},{3,2},{4,5},{5,4},{6,7},{7,6},{8,9},{9,8},{10,11... | collective-permute-start | bytes 983048 | tf_op jit(solution)/shard_map/ppermute | solution.py:240
  31.6 3.0 %collective-permute-start.9 = (bf16[320,1024]{1,0:T(8,128)(2,1)S(1)}, bf16[320,1024]{1,0:T(8,128)(2,1)}, u32[]{:S(2)}, u32[]{:S(2)}) collective-permute-start(bf16[320,1024]{1,0:T(8,128)(2,1)S(1)} %collective-permute-done.2.refs_2_), channel_id=1, source_target_pairs={{0,24},{1,7},{2,26},{3,1},{4,28},{5,3},{6,30},{7,5},{8,0},{9,15},{... | collective-permute-start | bytes 1966088 | tf_op jit(solution)/shard_map/ppermute | solution.py:241
  34.7 2.7 %collective-permute-start.8 = (bf16[320,1024]{1,0:T(8,128)(2,1)S(1)}, bf16[320,1024]{1,0:T(8,128)(2,1)S(1)}, u32[]{:S(2)}, u32[]{:S(2)}) collective-permute-start(bf16[320,1024]{1,0:T(8,128)(2,1)S(1)} %collective-permute-done.1.refs_1_), channel_id=1, source_target_pairs={{0,24},{1,7},{2,26},{3,1},{4,28},{5,3},{6,30},{7,5},{8,0},{9,15},{... | collective-permute-start | bytes 1966088 | tf_op jit(solution)/shard_map/ppermute | solution.py:241
  38.8 2.7 %products.4 = (f32[2560,128]{1,0:T(8,128)S(1)}, f32[2560,128]{1,0:T(8,128)}, f32[4,1024]{1,0:T(4,128)S(1)}, bf16[320,1024]{1,0:T(8,128)(2,1)}) custom-call(bf16[320,1024]{1,0:T(8,128)(2,1)S(1)} %constant_dynamic-update-slice_fusion.weight_ref, bf16[320,1024]{1,0:T(8,128)(2,1)S(1)} %copy-done.9, bf16[320,1024]{1,0:T(8,128)(2,1)S(1)} %collective-permute-done.1.refs_1_, ...), custom_call_target="tpu_custom_call" | custom-call | flops 1300000000 | bytes 8000000 | tf_op jit(solution)/shard_map/products/pallas_call | solution.py:129
  42.8 7.4 %collective-permute-done.7.refs_3_ = bf16[320,1024]{1,0:T(8,128)(2,1)S(1)} collective-permute-done((bf16[320,1024]{1,0:T(8,128)(2,1)S(1)}, bf16[320,1024]{1,0:T(8,128)(2,1)S(1)}, u32[]{:S(2)}, u32[]{:S(2)}) %collective-permute-start.7) | collective-permute-done | bytes 655392 | tf_op jit(solution)/shard_map/ppermute | solution.py:241
  50.1 7.0 %collective-permute-done.5.refs_1_ = bf16[320,1024]{1,0:T(8,128)(2,1)S(1)} collective-permute-done((bf16[320,1024]{1,0:T(8,128)(2,1)S(1)}, bf16[320,1024]{1,0:T(8,128)(2,1)S(1)}, u32[]{:S(2)}, u32[]{:S(2)}) %collective-permute-start.5) | collective-permute-done | bytes 655392 | tf_op jit(solution)/shard_map/ppermute | solution.py:241
  57.2 2.7 %products.5 = (f32[2560,128]{1,0:T(8,128)S(1)}, f32[2560,128]{1,0:T(8,128)}, f32[4,1024]{1,0:T(4,128)S(1)}, bf16[320,1024]{1,0:T(8,128)(2,1)}) custom-call(bf16[320,1024]{1,0:T(8,128)(2,1)S(1)} %constant_dynamic-update-slice_fusion.weight_ref, bf16[320,1024]{1,0:T(8,128)(2,1)S(1)} %collective-permute-done.4.refs_0_, ...), custom_call_target="tpu_custom_call" | custom-call | flops 1300000000 | bytes 8000000 | tf_op jit(solution)/shard_map/products/pallas_call | solution.py:129
  66.0 5.2 %collective-permute-done.11.refs_3_ = bf16[320,1024]{1,0:T(8,128)(2,1)} collective-permute-done((bf16[320,1024]{1,0:T(8,128)(2,1)S(1)}, bf16[320,1024]{1,0:T(8,128)(2,1)}, u32[]{:S(2)}, u32[]{:S(2)}) %collective-permute-start.11) | collective-permute-done | bytes 655392 | tf_op jit(solution)/shard_map/ppermute | solution.py:241
  74.1 3.9 %products.6 = (f32[2560,128]{1,0:T(8,128)S(1)}, f32[2560,128]{1,0:T(8,128)}, f32[4,1024]{1,0:T(4,128)S(1)}) custom-call(bf16[320,1024]{1,0:T(8,128)(2,1)S(1)} %constant_dynamic-update-slice_fusion.weight_ref, bf16[320,1024]{1,0:T(8,128)(2,1)S(1)} %copy-done.24, bf16[320,1024]{1,0:T(8,128)(2,1)} %collective-permute-done.9.refs_1_, ...), custom_call_target="tpu_custom_call" | custom-call | flops 1300000000 | bytes 8000000 | tf_op jit(solution)/shard_map/products/pallas_call | solution.py:129
  81.1 14.0 %act_rows.1 = (bf16[4,160,1280]{2,1,0:T(8,128)(2,1)S(1)}, bf16[4,160,1280]{2,1,0:T(8,128)(2,1)S(1)}) custom-call(s32[10240]{0:T(1024)S(1)} %fusion.23.place_ref, bf16[8,160,1280]{2,1,0:T(8,128)(2,1)S(1)} %bitcast.85), custom_call_target="tpu_custom_call" | custom-call | bytes 70000000 | tf_op jit(solution)/shard_map/act_rows/pallas_call | solution.py:91
  95.3 4.6 %products.7 = (f32[2560,128]{1,0:T(8,128)S(1)}, f32[2560,128]{1,0:T(8,128)}, f32[4,1024]{1,0:T(4,128)S(1)}) custom-call(bf16[320,1024]{1,0:T(8,128)(2,1)S(1)} %constant_dynamic-update-slice_fusion.weight_ref, bf16[320,1024]{1,0:T(8,128)(2,1)S(1)} %collective-permute-done.12.refs_0_, bf16[320,1024]{1,0:T(8,128)(2,1)} %collective-permute-done.13.refs_1_, ...), custom_call_target="tpu_custom_call" | custom-call | flops 1300000000 | bytes 8000000 | tf_op jit(solution)/shard_map/products/pallas_call | solution.py:129
  102.1 2.2 %collective-permute-done.19.refs_7_ = f32[2560,128]{1,0:T(8,128)} collective-permute-done((f32[2560,128]{1,0:T(8,128)}, f32[2560,128]{1,0:T(8,128)}, u32[]{:S(2)}, u32[]{:S(2)}) %collective-permute-start.19) | collective-permute-done | bytes 1310752 | tf_op jit(solution)/shard_map/ppermute | solution.py:240
  104.3 10.2 %slot_rows.2 = (f32[20480,128]{1,0:T(8,128)S(1)}, f32[3,160,1280]{2,1,0:T(8,128)S(1)}) custom-call(s32[10240]{0:T(1024)} %copy-done.6, s32[3]{0:T(128)} %and_select_fusion.blocks_ref, f32[2560,128]{1,0:T(8,128)} %copy-done.2, f32[2560,128]{1,0:T(8,128)} %copy-done.3, f32[2560,128]{1,0:T(8,128)} %copy-done.4, f32[2560,128]{1,0:T(8,128)} %copy-done.5, ...), custom_call_target="tpu_custom_call" | custom-call | bytes 24000000 | tf_op jit(solution)/shard_map/slot_rows/pallas_call | solution.py:180
  116.4 4.3 %collective-permute-start.24 = (bf16[80,1280]{1,0:T(8,128)(2,1)S(1)}, bf16[80,1280]{1,0:T(8,128)(2,1)S(1)}, u32[]{:S(2)}, u32[]{:S(2)}) collective-permute-start(bf16[80,1280]{1,0:T(8,128)(2,1)S(1)} %get-tuple-element.70), channel_id=1, source_target_pairs={{0,224},{32,0},{64,32},{96,64},{128,96},{160,128},{192,160},{224,1... | collective-permute-start | bytes 614408 | tf_op jit(solution)/shard_map/ppermute | solution.py:269
  120.8 9.2 %slot_rows.3 = f32[5,160,1280]{2,1,0:T(8,128)S(1)} custom-call(s32[10240]{0:T(1024)S(1)} %copy-done.7, s32[5]{0:T(128)S(1)} %and_select_fusion.1.blocks_ref, f32[20480,128]{1,0:T(8,128)S(1)} %get-tuple-element.40.refs_0_), custom_call_target="tpu_custom_call" | custom-call | bytes 40000000 | tf_op jit(solution)/shard_map/slot_rows/pallas_call | solution.py:180
  133.3 7.5 %collective-permute-done.25 = bf16[160,1280]{1,0:T(8,128)(2,1)S(1)} collective-permute-done((bf16[160,1280]{1,0:T(8,128)(2,1)S(1)}, bf16[160,1280]{1,0:T(8,128)(2,1)S(1)}, u32[]{:S(2)}, u32[]{:S(2)}) %collective-permute-start.25) | collective-permute-done | bytes 409632 | tf_op jit(solution)/shard_map/ppermute | solution.py:269
  142.9 2.7 %collective-permute-start.26 = (bf16[160,1280]{1,0:T(8,128)(2,1)S(1)}, bf16[160,1280]{1,0:T(8,128)(2,1)S(1)}, u32[]{:S(2)}, u32[]{:S(2)}) collective-permute-start(bf16[160,1280]{1,0:T(8,128)(2,1)S(1)} %get-tuple-element.58), channel_id=1, source_target_pairs={{0,224},{32,0},{64,32},{96,64},{128,96},{160,128},{192,160},{224,1... | collective-permute-start | bytes 1228808 | tf_op jit(solution)/shard_map/ppermute | solution.py:269
  149.5 2.6 %weight_term.6 = (f32[160,1024]{1,0:T(8,128)S(1)}, f32[160,1024]{1,0:T(8,128)S(1)}) custom-call(bf16[160,1280]{1,0:T(8,128)(2,1)S(1)} %get-tuple-element.67.mine_ref, bf16[160,1280]{1,0:T(8,128)(2,1)S(1)} %get-tuple-element.63.theirs_ref, bf16[320,1024]{1,0:T(8,128)(2,1)S(1)} %copy-done.25, bf16[320,1024]{1,0:T(8,128)(2,1)} %collective-permute-done.9.refs_1_, ...), custom_call_target="tpu_custom_call" | custom-call | flops 1300000000 | bytes 8000000 | tf_op jit(solution)/shard_map/weight_term/pallas_call | solution.py:213
  152.1 2.8 %weight_term.7 = (f32[160,1024]{1,0:T(8,128)S(1)}, f32[160,1024]{1,0:T(8,128)S(1)}) custom-call(bf16[160,1280]{1,0:T(8,128)(2,1)S(1)} %get-tuple-element.68.mine_ref, bf16[160,1280]{1,0:T(8,128)(2,1)S(1)} %get-tuple-element.64.theirs_ref, bf16[320,1024]{1,0:T(8,128)(2,1)S(1)} %collective-permute-done.12.refs_0_, ...), custom_call_target="tpu_custom_call" | custom-call | flops 1300000000 | bytes 8000000 | tf_op jit(solution)/shard_map/weight_term/pallas_call | solution.py:213
  154.9 2.6 %collective-permute-start.29 = (f32[160,1024]{1,0:T(8,128)S(1)}, f32[160,1024]{1,0:T(8,128)S(1)}, u32[]{:S(2)}, u32[]{:S(2)}) collective-permute-start(f32[160,1024]{1,0:T(8,128)S(1)} %get-tuple-element.50), channel_id=1, source_target_pairs={{0,1},{1,0},{2,3},{3,2},{4,5},{5,4},{6,7},{7,6},{8,9},{9,8},{10,11... | collective-permute-start | bytes 1966088 | tf_op jit(solution)/shard_map/ppermute | solution.py:240
  157.7 2.7 %collective-permute-start.27 = (bf16[160,1280]{1,0:T(8,128)(2,1)S(1)}, bf16[160,1280]{1,0:T(8,128)(2,1)}, u32[]{:S(2)}, u32[]{:S(2)}) collective-permute-start(bf16[160,1280]{1,0:T(8,128)(2,1)S(1)} %get-tuple-element.56), channel_id=1, source_target_pairs={{0,224},{32,0},{64,32},{96,64},{128,96},{160,128},{192,160},{224,1... | collective-permute-start | bytes 1228808 | tf_op jit(solution)/shard_map/ppermute | solution.py:269
  164.2 5.8 %collective-permute-done.23 = bf16[160,1280]{1,0:T(8,128)(2,1)} collective-permute-done((bf16[160,1280]{1,0:T(8,128)(2,1)S(1)}, bf16[160,1280]{1,0:T(8,128)(2,1)}, u32[]{:S(2)}, u32[]{:S(2)}) %collective-permute-start.23) | collective-permute-done | bytes 409632 | tf_op jit(solution)/shard_map/ppermute | solution.py:268
  170.1 2.7 %fusion.5 = f32[1280,160]{0,1:T(8,128)} fusion(f32[5,160,1280]{2,1,0:T(8,128)} %copy-done, bf16[1280,160]{0,1:T(8,128)(2,1)S(1)} %copy-done.31, bf16[160,1280]{1,0:T(8,128)(2,1)} %collective-permute-done.27, bf16[160,1280]{1,0:T(8,128)(2,1)} %collective-permute-done.23), kind=kLoop, calls=%fused_computation.7 | loop fusion | flops 2867200 | bytes 2867200 | tf_op jit(solution)/shard_map/transpose | solution.py:283
  (147 shorter events, 42.2 us)
Async XLA Ops:
  7.2 71.9 %all-gather.3.cloned.1.call-start = ((), (), s32[]{:S(2)}) async-start(), calls=%async_computation | async-start | bytes 3686400 | tf_op jit(solution)/shard_map/all_gather | solution.py:239
  9.3 13.0 %collective-permute-start.1 = (bf16[320,1024]{1,0:T(8,128)(2,1)}, bf16[320,1024]{1,0:T(8,128)(2,1)S(1)}, u32[]{:S(2)}, u32[]{:S(2)}) collective-permute-start(bf16[320,1024]{1,0:T(8,128)(2,1)} %refs_0_.3), channel_id=1, source_target_pairs={{0,2},{1,9},{2,4},{3,11},{4,6},{5,13},{6,0},{7,15},{8,10},{9,17},{... | collective-permute-start | bytes 1966088 | tf_op jit(solution)/shard_map/ppermute | solution.py:241
  11.5 20.1 %collective-permute-start.2 = (bf16[320,1024]{1,0:T(8,128)(2,1)}, bf16[320,1024]{1,0:T(8,128)(2,1)S(1)}, u32[]{:S(2)}, u32[]{:S(2)}) collective-permute-start(bf16[320,1024]{1,0:T(8,128)(2,1)} %refs_0_.3), channel_id=1, source_target_pairs={{0,6},{1,25},{2,0},{3,27},{4,2},{5,29},{6,4},{7,31},{8,14},{9,1},{... | collective-permute-start | bytes 1966088 | tf_op jit(solution)/shard_map/ppermute | solution.py:241
  13.0 21.5 %collective-permute-start.3 = (bf16[320,1024]{1,0:T(8,128)(2,1)}, bf16[320,1024]{1,0:T(8,128)(2,1)S(1)}, u32[]{:S(2)}, u32[]{:S(2)}) collective-permute-start(bf16[320,1024]{1,0:T(8,128)(2,1)} %refs_0_.3), channel_id=1, source_target_pairs={{0,8},{1,3},{2,10},{3,5},{4,12},{5,7},{6,14},{7,1},{8,16},{9,11},{... | collective-permute-start | bytes 1966088 | tf_op jit(solution)/shard_map/ppermute | solution.py:241
  14.2 20.4 %collective-permute-start.4 = (bf16[320,1024]{1,0:T(8,128)(2,1)}, bf16[320,1024]{1,0:T(8,128)(2,1)S(1)}, u32[]{:S(2)}, u32[]{:S(2)}) collective-permute-start(bf16[320,1024]{1,0:T(8,128)(2,1)} %refs_0_.3), channel_id=1, source_target_pairs={{0,24},{1,7},{2,26},{3,1},{4,28},{5,3},{6,30},{7,5},{8,0},{9,15},{... | collective-permute-start | bytes 1966088 | tf_op jit(solution)/shard_map/ppermute | solution.py:241
  22.3 15.0 %collective-permute-start.6 = (bf16[320,1024]{1,0:T(8,128)(2,1)S(1)}, bf16[320,1024]{1,0:T(8,128)(2,1)S(1)}, u32[]{:S(2)}, u32[]{:S(2)}) collective-permute-start(bf16[320,1024]{1,0:T(8,128)(2,1)S(1)} %collective-permute-done.1.refs_1_), channel_id=1, source_target_pairs={{0,2},{1,9},{2,4},{3,11},{4,6},{5,13},{6,0},{7,15},{8,10},{9,17},{... | collective-permute-start | bytes 1966088 | tf_op jit(solution)/shard_map/ppermute | solution.py:241
  34.6 15.6 %collective-permute-start.7 = (bf16[320,1024]{1,0:T(8,128)(2,1)S(1)}, bf16[320,1024]{1,0:T(8,128)(2,1)S(1)}, u32[]{:S(2)}, u32[]{:S(2)}) collective-permute-start(bf16[320,1024]{1,0:T(8,128)(2,1)S(1)} %collective-permute-done.2.refs_2_), channel_id=1, source_target_pairs={{0,8},{1,3},{2,10},{3,5},{4,12},{5,7},{6,14},{7,1},{8,16},{9,11},{... | collective-permute-start | bytes 1966088 | tf_op jit(solution)/shard_map/ppermute | solution.py:241
  34.6 22.6 %collective-permute-start.5 = (bf16[320,1024]{1,0:T(8,128)(2,1)S(1)}, bf16[320,1024]{1,0:T(8,128)(2,1)S(1)}, u32[]{:S(2)}, u32[]{:S(2)}) collective-permute-start(bf16[320,1024]{1,0:T(8,128)(2,1)S(1)} %collective-permute-done.1.refs_1_), channel_id=1, source_target_pairs={{0,8},{1,3},{2,10},{3,5},{4,12},{5,7},{6,14},{7,1},{8,16},{9,11},{... | collective-permute-start | bytes 1966088 | tf_op jit(solution)/shard_map/ppermute | solution.py:241
  34.7 26.3 %collective-permute-start.8 = (bf16[320,1024]{1,0:T(8,128)(2,1)S(1)}, bf16[320,1024]{1,0:T(8,128)(2,1)S(1)}, u32[]{:S(2)}, u32[]{:S(2)}) collective-permute-start(bf16[320,1024]{1,0:T(8,128)(2,1)S(1)} %collective-permute-done.1.refs_1_), channel_id=1, source_target_pairs={{0,24},{1,7},{2,26},{3,1},{4,28},{5,3},{6,30},{7,5},{8,0},{9,15},{... | collective-permute-start | bytes 1966088 | tf_op jit(solution)/shard_map/ppermute | solution.py:241
  37.4 26.0 %collective-permute-start.12 = (bf16[320,1024]{1,0:T(8,128)(2,1)S(1)}, bf16[320,1024]{1,0:T(8,128)(2,1)S(1)}, u32[]{:S(2)}, u32[]{:S(2)}) collective-permute-start(bf16[320,1024]{1,0:T(8,128)(2,1)S(1)} %collective-permute-done.6.refs_2_), channel_id=1, source_target_pairs={{0,24},{1,7},{2,26},{3,1},{4,28},{5,3},{6,30},{7,5},{8,0},{9,15},{... | collective-permute-start | bytes 1966088 | tf_op jit(solution)/shard_map/ppermute | solution.py:241
  42.7 22.0 %collective-permute-start.10 = (bf16[320,1024]{1,0:T(8,128)(2,1)}, bf16[320,1024]{1,0:T(8,128)(2,1)S(1)}, u32[]{:S(2)}, u32[]{:S(2)}) collective-permute-start(bf16[320,1024]{1,0:T(8,128)(2,1)} %get-tuple-element.31), channel_id=1, source_target_pairs={{0,8},{1,3},{2,10},{3,5},{4,12},{5,7},{6,14},{7,1},{8,16},{9,11},{... | collective-permute-start | bytes 1966088 | tf_op jit(solution)/shard_map/ppermute | solution.py:241
  50.1 21.1 %collective-permute-start.11 = (bf16[320,1024]{1,0:T(8,128)(2,1)S(1)}, bf16[320,1024]{1,0:T(8,128)(2,1)}, u32[]{:S(2)}, u32[]{:S(2)}) collective-permute-start(bf16[320,1024]{1,0:T(8,128)(2,1)S(1)} %collective-permute-done.6.refs_2_), channel_id=1, source_target_pairs={{0,8},{1,3},{2,10},{3,5},{4,12},{5,7},{6,14},{7,1},{8,16},{9,11},{... | collective-permute-start | bytes 1966088 | tf_op jit(solution)/shard_map/ppermute | solution.py:241
  57.2 37.9 %collective-permute-start.14 = (bf16[320,1024]{1,0:T(8,128)(2,1)}, bf16[320,1024]{1,0:T(8,128)(2,1)}, u32[]{:S(2)}, u32[]{:S(2)}) collective-permute-start(bf16[320,1024]{1,0:T(8,128)(2,1)} %collective-permute-done.9.refs_1_), channel_id=1, source_target_pairs={{0,24},{1,7},{2,26},{3,1},{4,28},{5,3},{6,30},{7,5},{8,0},{9,15},{... | collective-permute-start | bytes 1966088 | tf_op jit(solution)/shard_map/ppermute | solution.py:241
  61.9 33.3 %collective-permute-start.13 = (bf16[320,1024]{1,0:T(8,128)(2,1)}, bf16[320,1024]{1,0:T(8,128)(2,1)}, u32[]{:S(2)}, u32[]{:S(2)}) collective-permute-start(bf16[320,1024]{1,0:T(8,128)(2,1)} %get-tuple-element.33), channel_id=1, source_target_pairs={{0,8},{1,3},{2,10},{3,5},{4,12},{5,7},{6,14},{7,1},{8,16},{9,11},{... | collective-permute-start | bytes 1966088 | tf_op jit(solution)/shard_map/ppermute | solution.py:241
  63.3 31.9 %collective-permute-start.15 = (bf16[320,1024]{1,0:T(8,128)(2,1)S(1)}, bf16[320,1024]{1,0:T(8,128)(2,1)}, u32[]{:S(2)}, u32[]{:S(2)}) collective-permute-start(bf16[320,1024]{1,0:T(8,128)(2,1)S(1)} %collective-permute-done.12.refs_0_), channel_id=1, source_target_pairs={{0,24},{1,7},{2,26},{3,1},{4,28},{5,3},{6,30},{7,5},{8,0},{9,15},{... | collective-permute-start | bytes 1966088 | tf_op jit(solution)/shard_map/ppermute | solution.py:241
  65.5 36.6 %collective-permute-start.16 = (f32[2560,128]{1,0:T(8,128)}, f32[2560,128]{1,0:T(8,128)}, u32[]{:S(2)}, u32[]{:S(2)}) collective-permute-start(f32[2560,128]{1,0:T(8,128)} %get-tuple-element.36), channel_id=1, source_target_pairs={{0,1},{1,0},{2,3},{3,2},{4,5},{5,4},{6,7},{7,6},{8,9},{9,8},{10,11... | collective-permute-start | bytes 3932168 | tf_op jit(solution)/shard_map/ppermute | solution.py:240
  71.2 30.9 %collective-permute-start.17 = (f32[2560,128]{1,0:T(8,128)}, f32[2560,128]{1,0:T(8,128)}, u32[]{:S(2)}, u32[]{:S(2)}) collective-permute-start(f32[2560,128]{1,0:T(8,128)} %get-tuple-element.37), channel_id=1, source_target_pairs={{0,1},{1,0},{2,3},{3,2},{4,5},{5,4},{6,7},{7,6},{8,9},{9,8},{10,11... | collective-permute-start | bytes 3932168 | tf_op jit(solution)/shard_map/ppermute | solution.py:240
  101.5 30.3 %collective-permute-start.28 = (bf16[4,160,1280]{2,1,0:T(8,128)(2,1)}, bf16[4,160,1280]{2,1,0:T(8,128)(2,1)}, u32[]{:S(2)}, u32[]{:S(2)}) collective-permute-start(bf16[4,160,1280]{2,1,0:T(8,128)(2,1)} %copy-done.8), channel_id=1, source_target_pairs={{0,1},{1,0},{2,3},{3,2},{4,5},{5,4},{6,7},{7,6},{8,9},{9,8},{10,11... | collective-permute-start | bytes 4915208 | tf_op jit(solution)/shard_map/ppermute | solution.py:240
  114.7 15.3 %collective-permute-start.20 = (bf16[80,1280]{1,0:T(8,128)(2,1)S(1)}, bf16[80,1280]{1,0:T(8,128)(2,1)S(1)}, u32[]{:S(2)}, u32[]{:S(2)}) collective-permute-start(bf16[80,1280]{1,0:T(8,128)(2,1)S(1)} %get-tuple-element.69), channel_id=1, source_target_pairs={{0,32},{32,64},{64,96},{96,128},{128,160},{160,192},{192,224},{224... | collective-permute-start | bytes 614408 | tf_op jit(solution)/shard_map/ppermute | solution.py:268
  116.4 13.6 %collective-permute-start.24 = (bf16[80,1280]{1,0:T(8,128)(2,1)S(1)}, bf16[80,1280]{1,0:T(8,128)(2,1)S(1)}, u32[]{:S(2)}, u32[]{:S(2)}) collective-permute-start(bf16[80,1280]{1,0:T(8,128)(2,1)S(1)} %get-tuple-element.70), channel_id=1, source_target_pairs={{0,224},{32,0},{64,32},{96,64},{128,96},{160,128},{192,160},{224,1... | collective-permute-start | bytes 614408 | tf_op jit(solution)/shard_map/ppermute | solution.py:269
  142.8 14.6 %collective-permute-start.22 = (bf16[160,1280]{1,0:T(8,128)(2,1)S(1)}, bf16[160,1280]{1,0:T(8,128)(2,1)S(1)}, u32[]{:S(2)}, u32[]{:S(2)}) collective-permute-start(bf16[160,1280]{1,0:T(8,128)(2,1)S(1)} %get-tuple-element.57), channel_id=1, source_target_pairs={{0,32},{32,64},{64,96},{96,128},{128,160},{160,192},{192,224},{224... | collective-permute-start | bytes 1228808 | tf_op jit(solution)/shard_map/ppermute | solution.py:268
  142.9 14.5 %collective-permute-start.26 = (bf16[160,1280]{1,0:T(8,128)(2,1)S(1)}, bf16[160,1280]{1,0:T(8,128)(2,1)S(1)}, u32[]{:S(2)}, u32[]{:S(2)}) collective-permute-start(bf16[160,1280]{1,0:T(8,128)(2,1)S(1)} %get-tuple-element.58), channel_id=1, source_target_pairs={{0,224},{32,0},{64,32},{96,64},{128,96},{160,128},{192,160},{224,1... | collective-permute-start | bytes 1228808 | tf_op jit(solution)/shard_map/ppermute | solution.py:269
  157.6 12.5 %collective-permute-start.23 = (bf16[160,1280]{1,0:T(8,128)(2,1)S(1)}, bf16[160,1280]{1,0:T(8,128)(2,1)}, u32[]{:S(2)}, u32[]{:S(2)}) collective-permute-start(bf16[160,1280]{1,0:T(8,128)(2,1)S(1)} %get-tuple-element.55), channel_id=1, source_target_pairs={{0,32},{32,64},{64,96},{96,128},{128,160},{160,192},{192,224},{224... | collective-permute-start | bytes 1228808 | tf_op jit(solution)/shard_map/ppermute | solution.py:268
  157.7 12.4 %collective-permute-start.27 = (bf16[160,1280]{1,0:T(8,128)(2,1)S(1)}, bf16[160,1280]{1,0:T(8,128)(2,1)}, u32[]{:S(2)}, u32[]{:S(2)}) collective-permute-start(bf16[160,1280]{1,0:T(8,128)(2,1)S(1)} %get-tuple-element.56), channel_id=1, source_target_pairs={{0,224},{32,0},{64,32},{96,64},{128,96},{160,128},{192,160},{224,1... | collective-permute-start | bytes 1228808 | tf_op jit(solution)/shard_map/ppermute | solution.py:269
  (44 other events, 381.5 us)
Sparse Core Ops, SparseCore 0:
  9.8 50.0 all-gather.2
where the time goes:
time: 180 us
  Pallas kernels  56.6 us (31%)
  waiting for transfers between devices  44.6 us (25%)
  starting transfers between devices  43.8 us (24%)
  between operations  14.6 us (8%)
  local copies, waits for them, and re-layouts  12.6 us (7%)
  other arithmetic  7.56 us (4%)
    ppermute x15, waiting for transfers between devices, body(): send = lambda value, perm: lax.ppermute(value, 'text', perm)  26.3 us
    pallas_call x2, Pallas kernels, to_slot_order(): pl.pallas_call(functools.partial(slot_kernel, count), out_shape=out, in_s...  19.4 us
    ppermute x15, starting transfers between devices, body(): send = lambda value, perm: lax.ppermute(value, 'text', perm)  17.7 us
    pallas_call x1, Pallas kernels, act_in_arrival_order(): pl.pallas_call(act_kernel, out_shape=[jax.ShapeDtypeStruct((GROUPS, HID,...  14 us
    pallas_call x4, Pallas kernels, products_of(): pl.pallas_call(functools.partial(product_kernel, hand_on), out_shape=out...  14 us
    ppermute x8, starting transfers between devices, body(): swap = lambda value: lax.ppermute(value, 'text', SWAP)  12.9 us
    ppermute x4, starting transfers between devices, body(): lax.ppermute(value.astype(BF16), 'tile', TILE_DOWN).astype(F32)  10.8 us
    unnamed x73, local copies, waits for them, and re-layouts  10.2 us
  transfers between devices with their start and end apart: 32, of which 9 were waited for; matrix products, arithmetic and copies ran while one was open for 3% of the time, Pallas kernels for 31%

commit v1 on v0

--- a/solution.py
+++ b/solution.py
@@ -138,11 +138,9 @@
     )(weight, *pieces, *after)
 
 
-def slot_kernel(count, place_ref, blocks_ref, *refs):
-    if len(refs) == 3:
-        rows_ref, out_ref, picked = refs
-    else:
-        rows_ref, out_ref, picked, sems = refs[8:]
+def slot_kernel(count, gather_rows, keep, place_ref, blocks_ref, *refs):
+    if gather_rows:
+        rows_ref, out_ref, picked, sems = refs[-4:] if keep else (refs[-1], *refs[-4:-1])
         copies = [
             pltpu.make_async_copy(refs[k], rows_ref.at[pl.ds(k * 2 * GROUP_ROWS, 2 * GROUP_ROWS), :], sems.at[k])
             for k in range(8)
@@ -151,6 +149,8 @@
             copy.start()
         for copy in copies:
             copy.wait()
+    else:
+        rows_ref, (out_ref, picked) = refs[0], refs[-2:]
 
     @pl.loop(0, count)
     def _(b):
@@ -170,24 +170,28 @@
         out_ref[b, LANES:HID, :] = right
 
 
-def to_slot_order(place, blocks, rows):
+def to_slot_order(place, blocks, rows, after, keep=False):
     count = blocks.shape[0]
-    vmem = pl.BlockSpec(memory_space=pltpu.VMEM)
+    vmem, anywhere = pl.BlockSpec(memory_space=pltpu.VMEM), pl.BlockSpec(memory_space=pl.ANY)
     out = [pltpu.VMEM((count, HID, BLOCK), F32)]
     whole = len(rows) == 1
-    if not whole:
+    scratch = [pltpu.VMEM((2 * BLOCK, LANES), F32)] + [pltpu.SemaphoreType.DMA((8,))] * (not whole)
+    if keep:
         out.insert(0, pltpu.VMEM((2 * SLOTS, LANES), F32))
+    elif not whole:
+        scratch.append(pltpu.VMEM((2 * SLOTS, LANES), F32))
     return pl.pallas_call(
-        functools.partial(slot_kernel, count),
+        functools.partial(slot_kernel, count, not whole, keep),
         out_shape=out,
         in_specs=[pl.BlockSpec(memory_space=pltpu.SMEM)] * 2
-        + ([vmem] if whole else [pl.BlockSpec(memory_space=pl.ANY)] * len(rows)),
+        + [vmem if whole else anywhere] * len(rows)
+        + [anywhere] * len(after),
         out_specs=[vmem] * len(out),
-        scratch_shapes=[pltpu.VMEM((2 * BLOCK, LANES), F32)] + [pltpu.SemaphoreType.DMA((8,))] * (not whole),
+        scratch_shapes=scratch,
         compiler_params=pltpu.CompilerParams(vmem_limit_bytes=(5 if whole else 46) * 2**20),
         cost_estimate=pl.CostEstimate(flops=0, bytes_accessed=8_000_000 * count, transcendentals=0),
         name="slot_rows",
-    )(place, blocks, *rows)
+    )(place, blocks, *rows, *after)
 
 
 def weight_kernel(first, mine_ref, theirs_ref, *refs):
@@ -208,18 +212,19 @@
         out_theirs[:, columns] = term[HID:] if first else refs[5][:, columns] + term[HID:]
 
 
-def weight_term(mine, theirs, pieces, totals):
+def weight_term(mine, theirs, pieces, totals, after):
     vmem = pl.BlockSpec(memory_space=pltpu.VMEM)
     return pl.pallas_call(
         functools.partial(weight_kernel, not totals),
         out_shape=[jax.ShapeDtypeStruct((HID, WIDTH), F32)] * 2,
-        in_specs=[vmem] * 2 + [pl.BlockSpec(memory_space=pl.ANY)] * 4 + [vmem] * len(totals),
+        in_specs=[vmem] * 2 + [pl.BlockSpec(memory_space=pl.ANY)] * 4 + [vmem] * len(totals)
+        + [pl.BlockSpec(memory_space=pl.ANY)] * len(after),
         out_specs=[vmem] * 2,
         scratch_shapes=[pltpu.VMEM((GROUP_ROWS, WIDTH), BF16), pltpu.SemaphoreType.DMA((4,))],
         compiler_params=pltpu.CompilerParams(vmem_limit_bytes=6 * 2**20),
         cost_estimate=pl.CostEstimate(flops=1_300_000_000, bytes_accessed=8_000_000, transcendentals=0),
         name="weight_term",
-    )(mine, theirs, *pieces, *totals)
+    )(mine, theirs, *pieces, *totals, *after)
 
 
 def gelu_parts(pre):
@@ -263,19 +268,28 @@
         sums.append(part)
     groups = [[got[key] for key in ARRIVAL[4 * g:4 * g + 4]] for g in range(GROUPS)]
     tile = lax.axis_index("tile")
-    rows, early = to_slot_order(place, (tile + jnp.array([4, 3, 5], jnp.int32)) % N_TILE, mine + theirs)
-    (late,) = to_slot_order(place, (tile + jnp.array([2, 6, 1, 7, 0], jnp.int32)) % N_TILE, [rows])
-    up = lambda value: lax.ppermute(value.astype(BF16), "tile", TILE_UP).astype(F32)
-    down = lambda value: lax.ppermute(value.astype(BF16), "tile", TILE_DOWN).astype(F32)
-    rise, fall = up(early[0, :HALF]), down(early[0, HALF:])
-    rise = up(jnp.concatenate([rise + early[1, :HALF], early[1, HALF:]], axis=0))
-    fall = down(jnp.concatenate([early[2, :HALF], fall + early[2, HALF:]], axis=0))
-    rise, fall = up(rise + late[0]), down(fall + late[1])
-    rise, fall = up(rise + late[2]), down(fall + late[3])
-    grad_pre = (late[4] + rise + fall) * slope
+    parts = mine + theirs
+
+    def slots(steps, rows, after, keep=False):
+        return to_slot_order(place, (tile + jnp.array(steps, jnp.int32)) % N_TILE, rows, after, keep)
+
+    rows, across = slots([4], parts, [], keep=True)
+    (third,) = slots([3, 5], [rows], [across])
+    up = lambda value: lax.ppermute(value.astype(BF16), "tile", TILE_UP)
+    down = lambda value: lax.ppermute(value.astype(BF16), "tile", TILE_DOWN)
+    rise, fall = up(across[0, :HALF]), down(across[0, HALF:])
+    (second,) = slots([2, 6], parts, [rise])
+    up3 = jnp.concatenate([rise.astype(F32) + third[0, :HALF], third[0, HALF:]], axis=0)
+    down3 = jnp.concatenate([third[1, :HALF], fall.astype(F32) + third[1, HALF:]], axis=0)
+    rise, fall = up(up3), down(down3)
+    (nearest,) = slots([1, 7, 0], parts, [rise])
+    rise, fall = up(rise.astype(F32) + second[0]), down(fall.astype(F32) + second[1])
+    hop = rise
+    rise, fall = up(rise.astype(F32) + nearest[0]), down(fall.astype(F32) + nearest[1])
+    grad_pre = (nearest[2] + rise.astype(F32) + fall.astype(F32)) * lax.optimization_barrier(slope)
     totals = []
     for g in range(GROUPS):
-        totals = weight_term(act_mine[g], act_theirs[g], groups[g], totals)
+        totals = weight_term(act_mine[g], act_theirs[g], groups[g], totals, [hop] if g == 1 else [])
     grad_w = totals[0] + swap(totals[1])
     sums = jnp.concatenate(sums, axis=0)
     sums = jnp.concatenate([sums, swap(sums)], axis=0)

time: 180 us -> 179 us (level)
  waiting for transfers between devices: 44.6 us -> 30.5 us
  Pallas kernels: 56.6 us -> 64.2 us
  starting transfers between devices: 43.8 us -> 47.4 us
    ppermute x8, waiting for transfers between devices: 15.2 us -> 3.52 us  [the longest x4 3.51 us: body(): up = lambda value: lax.ppermute(value.astype(BF16), 'tile', TILE_UP)]
    pallas_call x2 -> x4, Pallas kernels: 19.4 us -> 27.6 us  [to_slot_order(): pl.pallas_call(functools.partial(slot_kernel, count, not whole, keep), ou...]
    ppermute x8, starting transfers between devices: 12.9 us -> 15.5 us  [body(): swap = lambda value: lax.ppermute(value, 'text', SWAP)]
    ppermute x15, waiting for transfers between devices: 26.3 us -> 24.4 us  [body(): send = lambda value, perm: lax.ppermute(value, 'text', perm)]
    unnamed x73 -> x75, local copies, waits for them, and re-layouts: 10.2 us -> 11.6 us
  transfers between devices with their start and end apart: 32 -> 32, of which waited for: 9 -> 7; matrix products, arithmetic and copies ran while one was open for 3% -> 3% of each run, Pallas kernels for 31% -> 36%
where the time goes in v1:
time: 179 us
  Pallas kernels  64.2 us (36%)
  starting transfers between devices  47.4 us (26%)
  waiting for transfers between devices  30.5 us (17%)
  between operations  14.7 us (8%)
  local copies, waits for them, and re-layouts  12.6 us (7%)
  other arithmetic  9.21 us (5%)
    pallas_call x4, Pallas kernels, to_slot_order(): pl.pallas_call(functools.partial(slot_kernel, count, not whole, keep), ou...  27.6 us
    ppermute x15, waiting for transfers between devices, body(): send = lambda value, perm: lax.ppermute(value, 'text', perm)  24.4 us
    ppermute x15, starting transfers between devices, body(): send = lambda value, perm: lax.ppermute(value, 'text', perm)  17.7 us
    ppermute x8, starting transfers between devices, body(): swap = lambda value: lax.ppermute(value, 'text', SWAP)  15.5 us
    pallas_call x1, Pallas kernels, act_in_arrival_order(): pl.pallas_call(act_kernel, out_shape=[jax.ShapeDtypeStruct((GROUPS, HID,...  14 us
    ppermute x4, starting transfers between devices, body(): down = lambda value: lax.ppermute(value.astype(BF16), 'tile', TILE_DOWN)  14 us
    pallas_call x4, Pallas kernels, products_of(): pl.pallas_call(functools.partial(product_kernel, hand_on), out_shape=out...  12.5 us
    unnamed x75, local copies, waits for them, and re-layouts  11.6 us
  transfers between devices with their start and end apart: 32, of which 7 were waited for; matrix products, arithmetic and copies ran while one was open for 3% of the time, Pallas kernels for 36%

profile of v1, /device:TPU:1, one launch (start us, length us, event | category | flops | bytes accessed | tf_op | source)
XLA Modules:
  0.0 178.6 jit_solution(4726609438524047619)
XLA Ops:
  7.2 2.5 %fusion.19 = (bf16[160,1280]{1,0:T(8,128)(2,1)}, f32[160,1280]{1,0:T(8,128)}) fusion(bf16[1280,160]{0,1:T(8,128)(2,1)} %param.10), kind=kLoop, calls=%fused_computation.28 | loop fusion | flops 2252800 | bytes 1638400 | tf_op jit(solution)/shard_map/convert_element_type | solution.py:244
  16.1 6.4 %collective-permute-done.1.refs_1_ = bf16[320,1024]{1,0:T(8,128)(2,1)S(1)} collective-permute-done((bf16[320,1024]{1,0:T(8,128)(2,1)S(1)}, bf16[320,1024]{1,0:T(8,128)(2,1)S(1)}, u32[]{:S(2)}, u32[]{:S(2)}) %collective-permute-start.1) | collective-permute-done | bytes 655392 | tf_op jit(solution)/shard_map/ppermute | solution.py:246
  24.1 7.8 %collective-permute-start = (bf16[160,1024]{1,0:T(8,128)(2,1)S(1)}, bf16[160,1024]{1,0:T(8,128)(2,1)S(1)}, u32[]{:S(2)}, u32[]{:S(2)}) collective-permute-start(bf16[160,1024]{1,0:T(8,128)(2,1)S(1)} %copy-done.32), channel_id=1, source_target_pairs={{0,1},{1,0},{2,3},{3,2},{4,5},{5,4},{6,7},{7,6},{8,9},{9,8},{10,11... | collective-permute-start | bytes 983048 | tf_op jit(solution)/shard_map/ppermute | solution.py:245
  31.9 2.9 %collective-permute-start.9 = (bf16[320,1024]{1,0:T(8,128)(2,1)S(1)}, bf16[320,1024]{1,0:T(8,128)(2,1)}, u32[]{:S(2)}, u32[]{:S(2)}) collective-permute-start(bf16[320,1024]{1,0:T(8,128)(2,1)S(1)} %collective-permute-done.2.refs_2_), channel_id=1, source_target_pairs={{0,24},{1,7},{2,26},{3,1},{4,28},{5,3},{6,30},{7,5},{8,0},{9,15},{... | collective-permute-start | bytes 1966088 | tf_op jit(solution)/shard_map/ppermute | solution.py:246
  34.9 2.7 %collective-permute-start.8 = (bf16[320,1024]{1,0:T(8,128)(2,1)S(1)}, bf16[320,1024]{1,0:T(8,128)(2,1)S(1)}, u32[]{:S(2)}, u32[]{:S(2)}) collective-permute-start(bf16[320,1024]{1,0:T(8,128)(2,1)S(1)} %collective-permute-done.1.refs_1_), channel_id=1, source_target_pairs={{0,24},{1,7},{2,26},{3,1},{4,28},{5,3},{6,30},{7,5},{8,0},{9,15},{... | collective-permute-start | bytes 1966088 | tf_op jit(solution)/shard_map/ppermute | solution.py:246
  44.1 6.3 %collective-permute-done.7.refs_3_ = bf16[320,1024]{1,0:T(8,128)(2,1)S(1)} collective-permute-done((bf16[320,1024]{1,0:T(8,128)(2,1)S(1)}, bf16[320,1024]{1,0:T(8,128)(2,1)S(1)}, u32[]{:S(2)}, u32[]{:S(2)}) %collective-permute-start.7) | collective-permute-done | bytes 655392 | tf_op jit(solution)/shard_map/ppermute | solution.py:246
  50.4 7.0 %collective-permute-done.5.refs_1_ = bf16[320,1024]{1,0:T(8,128)(2,1)S(1)} collective-permute-done((bf16[320,1024]{1,0:T(8,128)(2,1)S(1)}, bf16[320,1024]{1,0:T(8,128)(2,1)S(1)}, u32[]{:S(2)}, u32[]{:S(2)}) %collective-permute-start.5) | collective-permute-done | bytes 655392 | tf_op jit(solution)/shard_map/ppermute | solution.py:246
  66.7 4.7 %collective-permute-done.11.refs_3_ = bf16[320,1024]{1,0:T(8,128)(2,1)} collective-permute-done((bf16[320,1024]{1,0:T(8,128)(2,1)S(1)}, bf16[320,1024]{1,0:T(8,128)(2,1)}, u32[]{:S(2)}, u32[]{:S(2)}) %collective-permute-start.11) | collective-permute-done | bytes 655392 | tf_op jit(solution)/shard_map/ppermute | solution.py:246
  74.3 4.2 %products.6 = (f32[2560,128]{1,0:T(8,128)S(1)}, f32[2560,128]{1,0:T(8,128)}, f32[4,1024]{1,0:T(4,128)S(1)}) custom-call(bf16[320,1024]{1,0:T(8,128)(2,1)S(1)} %constant_dynamic-update-slice_fusion.weight_ref, bf16[320,1024]{1,0:T(8,128)(2,1)S(1)} %copy-done.24, bf16[320,1024]{1,0:T(8,128)(2,1)} %collective-permute-done.9.refs_1_, ...), custom_call_target="tpu_custom_call" | custom-call | flops 1300000000 | bytes 8000000 | tf_op jit(solution)/shard_map/products/pallas_call | solution.py:129
  81.5 14.0 %act_rows.1 = (bf16[4,160,1280]{2,1,0:T(8,128)(2,1)S(1)}, bf16[4,160,1280]{2,1,0:T(8,128)(2,1)S(1)}) custom-call(s32[10240]{0:T(1024)S(1)} %fusion.25.place_ref, bf16[8,160,1280]{2,1,0:T(8,128)(2,1)S(1)} %bitcast.92), custom_call_target="tpu_custom_call" | custom-call | bytes 70000000 | tf_op jit(solution)/shard_map/act_rows/pallas_call | solution.py:91
  95.7 4.8 %products.7 = (f32[2560,128]{1,0:T(8,128)S(1)}, f32[2560,128]{1,0:T(8,128)}, f32[4,1024]{1,0:T(4,128)S(1)}) custom-call(bf16[320,1024]{1,0:T(8,128)(2,1)S(1)} %constant_dynamic-update-slice_fusion.weight_ref, bf16[320,1024]{1,0:T(8,128)(2,1)} %collective-permute-done.12.refs_0_, bf16[320,1024]{1,0:T(8,128)(2,1)} %collective-permute-done.13.refs_1_, ...), custom_call_target="tpu_custom_call" | custom-call | flops 1300000000 | bytes 8000000 | tf_op jit(solution)/shard_map/products/pallas_call | solution.py:129
  102.5 2.5 %collective-permute-done.19.refs_7_ = f32[2560,128]{1,0:T(8,128)} collective-permute-done((f32[2560,128]{1,0:T(8,128)}, f32[2560,128]{1,0:T(8,128)}, u32[]{:S(2)}, u32[]{:S(2)}) %collective-permute-start.19) | collective-permute-done | bytes 1310752 | tf_op jit(solution)/shard_map/ppermute | solution.py:245
  105.0 7.0 %slot_rows.4 = (f32[20480,128]{1,0:T(8,128)S(1)}, f32[1,160,1280]{2,1,0:T(8,128)S(1)}) custom-call(s32[10240]{0:T(1024)} %copy-done.9, s32[1]{0:T(128)S(6)} %select_n.122.blocks_ref, f32[2560,128]{1,0:T(8,128)} %copy-done, f32[2560,128]{1,0:T(8,128)} %copy-done.2, f32[2560,128]{1,0:T(8,128)} %copy-done.4, f32[2560,128]{1,0:T(8,128)} %copy-done.6, ...), custom_call_target="tpu_custom_call" | custom-call | bytes 8000000 | tf_op jit(solution)/shard_map/slot_rows/pallas_call | solution.py:183
  112.1 5.9 %collective-permute-start.24 = (bf16[80,1280]{1,0:T(8,128)(2,1)S(1)}, bf16[80,1280]{1,0:T(8,128)(2,1)S(1)}, u32[]{:S(2)}, u32[]{:S(2)}) collective-permute-start(bf16[80,1280]{1,0:T(8,128)(2,1)S(1)} %get-tuple-element.71), channel_id=1, source_target_pairs={{0,224},{32,0},{64,32},{96,64},{128,96},{160,128},{192,160},{224,1... | collective-permute-start | bytes 614408 | tf_op jit(solution)/shard_map/ppermute | solution.py:279
  118.0 4.4 %slot_rows.5 = f32[2,160,1280]{2,1,0:T(8,128)S(1)} custom-call(s32[10240]{0:T(1024)S(1)} %copy-done.10, s32[2]{0:T(128)S(1)} %and_select_fusion.1.blocks_ref, f32[20480,128]{1,0:T(8,128)S(1)} %get-tuple-element.41.refs_0_, f32[1,160,1280]{2,1,0:T(8,128)S(1)} %get-tuple-element.40.refs_1_), custom_call_target="tpu_custom_call" | custom-call | bytes 16000000 | tf_op jit(solution)/shard_map/slot_rows/pallas_call | solution.py:183
  122.5 2.9 %collective-permute-done.20.refs_8_ = bf16[80,1280]{1,0:T(8,128)(2,1)S(1)} collective-permute-done((bf16[80,1280]{1,0:T(8,128)(2,1)S(1)}, bf16[80,1280]{1,0:T(8,128)(2,1)S(1)}, u32[]{:S(2)}, u32[]{:S(2)}) %collective-permute-start.20) | collective-permute-done | bytes 204832 | tf_op jit(solution)/shard_map/ppermute | solution.py:278
  125.7 2.7 %collective-permute-start.25 = (bf16[160,1280]{1,0:T(8,128)(2,1)S(1)}, bf16[160,1280]{1,0:T(8,128)(2,1)S(1)}, u32[]{:S(2)}, u32[]{:S(2)}) collective-permute-start(bf16[160,1280]{1,0:T(8,128)(2,1)S(1)} %pad_maximum_fusion.1), channel_id=1, source_target_pairs={{0,224},{32,0},{64,32},{96,64},{128,96},{160,128},{192,160},{224,1... | collective-permute-start | bytes 1228808 | tf_op jit(solution)/shard_map/ppermute | solution.py:279
  128.6 7.3 %slot_rows.7 = f32[2,160,1280]{2,1,0:T(8,128)S(1)} custom-call(s32[10240]{0:T(1024)S(1)} %copy-done.10, s32[2]{0:T(128)S(1)} %and_select_fusion.blocks_ref, f32[2560,128]{1,0:T(8,128)S(1)} %copy-done.1, f32[2560,128]{1,0:T(8,128)S(1)} %copy-done.3, f32[2560,128]{1,0:T(8,128)S(1)} %copy-done.5, f32[2560,128]{1,0:T(8,128)S(1)} %copy-done.7, ...), custom_call_target="tpu_custom_call" | custom-call | bytes 16000000 | tf_op jit(solution)/shard_map/slot_rows/pallas_call | solution.py:183
  136.8 2.7 %collective-permute-start.26 = (bf16[160,1280]{1,0:T(8,128)(2,1)S(1)}, bf16[160,1280]{1,0:T(8,128)(2,1)S(1)}, u32[]{:S(2)}, u32[]{:S(2)}) collective-permute-start(bf16[160,1280]{1,0:T(8,128)(2,1)S(1)} %get-tuple-element.66), channel_id=1, source_target_pairs={{0,224},{32,0},{64,32},{96,64},{128,96},{160,128},{192,160},{224,1... | collective-permute-start | bytes 1228808 | tf_op jit(solution)/shard_map/ppermute | solution.py:279
  141.6 8.9 %slot_rows.6 = f32[3,160,1280]{2,1,0:T(8,128)S(1)} custom-call(s32[10240]{0:T(1024)S(1)} %copy-done.10, s32[3]{0:T(128)S(1)} %and_select_fusion.2.blocks_ref, f32[2560,128]{1,0:T(8,128)S(1)} %copy-done.1, f32[2560,128]{1,0:T(8,128)S(1)} %copy-done.3, f32[2560,128]{1,0:T(8,128)S(1)} %copy-done.5, f32[2560,128]{1,0:T(8,128)S(1)} %copy-done.7, ...), custom_call_target="tpu_custom_call" | custom-call | bytes 24000000 | tf_op jit(solution)/shard_map/slot_rows/pallas_call | solution.py:183
  151.7 2.7 %collective-permute-start.27 = (bf16[160,1280]{1,0:T(8,128)(2,1)}, bf16[160,1280]{1,0:T(8,128)(2,1)}, u32[]{:S(2)}, u32[]{:S(2)}) collective-permute-start(bf16[160,1280]{1,0:T(8,128)(2,1)} %get-tuple-element.56), channel_id=1, source_target_pairs={{0,224},{32,0},{64,32},{96,64},{128,96},{160,128},{192,160},{224,1... | collective-permute-start | bytes 1228808 | tf_op jit(solution)/shard_map/ppermute | solution.py:279
  156.3 2.7 %weight_term.6 = (f32[160,1024]{1,0:T(8,128)S(1)}, f32[160,1024]{1,0:T(8,128)S(1)}) custom-call(bf16[160,1280]{1,0:T(8,128)(2,1)S(1)} %get-tuple-element.63.mine_ref, bf16[160,1280]{1,0:T(8,128)(2,1)S(1)} %get-tuple-element.59.theirs_ref, bf16[320,1024]{1,0:T(8,128)(2,1)S(1)} %copy-done.25, bf16[320,1024]{1,0:T(8,128)(2,1)} %collective-permute-done.9.refs_1_, ...), custom_call_target="tpu_custom_call" | custom-call | flops 1300000000 | bytes 8000000 | tf_op jit(solution)/shard_map/weight_term/pallas_call | solution.py:217
  159.0 3.6 %weight_term.7 = (f32[160,1024]{1,0:T(8,128)S(1)}, f32[160,1024]{1,0:T(8,128)}) custom-call(bf16[160,1280]{1,0:T(8,128)(2,1)S(1)} %get-tuple-element.64.mine_ref, bf16[160,1280]{1,0:T(8,128)(2,1)S(1)} %get-tuple-element.60.theirs_ref, bf16[320,1024]{1,0:T(8,128)(2,1)} %collective-permute-done.12.refs_0_, bf16[320,1024]{1,0:T(8,128)(2,1)} %collective-permute-done.13.refs_1_, ...), custom_call_target="tpu_custom_call" | custom-call | flops 1300000000 | bytes 8000000 | tf_op jit(solution)/shard_map/weight_term/pallas_call | solution.py:217
  162.6 3.4 %collective-permute-start.29 = (f32[160,1024]{1,0:T(8,128)}, f32[160,1024]{1,0:T(8,128)}, u32[]{:S(2)}, u32[]{:S(2)}) collective-permute-start(f32[160,1024]{1,0:T(8,128)} %get-tuple-element.50), channel_id=1, source_target_pairs={{0,1},{1,0},{2,3},{3,2},{4,5},{5,4},{6,7},{7,6},{8,9},{9,8},{10,11... | collective-permute-start | bytes 1966088 | tf_op jit(solution)/shard_map/ppermute | solution.py:245
  (154 shorter events, 43.9 us)
Async XLA Ops:
  7.2 72.4 %all-gather.3.cloned.1.call-start = ((), (), s32[]{:S(2)}) async-start(), calls=%async_computation | async-start | bytes 3686400 | tf_op jit(solution)/shard_map/all_gather | solution.py:244
  9.7 12.8 %collective-permute-start.1 = (bf16[320,1024]{1,0:T(8,128)(2,1)S(1)}, bf16[320,1024]{1,0:T(8,128)(2,1)S(1)}, u32[]{:S(2)}, u32[]{:S(2)}) collective-permute-start(bf16[320,1024]{1,0:T(8,128)(2,1)S(1)} %copy-done.20), channel_id=1, source_target_pairs={{0,2},{1,9},{2,4},{3,11},{4,6},{5,13},{6,0},{7,15},{8,10},{9,17},{... | collective-permute-start | bytes 1966088 | tf_op jit(solution)/shard_map/ppermute | solution.py:246
  11.9 20.0 %collective-permute-start.2 = (bf16[320,1024]{1,0:T(8,128)(2,1)S(1)}, bf16[320,1024]{1,0:T(8,128)(2,1)S(1)}, u32[]{:S(2)}, u32[]{:S(2)}) collective-permute-start(bf16[320,1024]{1,0:T(8,128)(2,1)S(1)} %copy-done.20), channel_id=1, source_target_pairs={{0,6},{1,25},{2,0},{3,27},{4,2},{5,29},{6,4},{7,31},{8,14},{9,1},{... | collective-permute-start | bytes 1966088 | tf_op jit(solution)/shard_map/ppermute | solution.py:246
  13.5 21.3 %collective-permute-start.3 = (bf16[320,1024]{1,0:T(8,128)(2,1)S(1)}, bf16[320,1024]{1,0:T(8,128)(2,1)S(1)}, u32[]{:S(2)}, u32[]{:S(2)}) collective-permute-start(bf16[320,1024]{1,0:T(8,128)(2,1)S(1)} %copy-done.20), channel_id=1, source_target_pairs={{0,8},{1,3},{2,10},{3,5},{4,12},{5,7},{6,14},{7,1},{8,16},{9,11},{... | collective-permute-start | bytes 1966088 | tf_op jit(solution)/shard_map/ppermute | solution.py:246
  14.7 20.2 %collective-permute-start.4 = (bf16[320,1024]{1,0:T(8,128)(2,1)S(1)}, bf16[320,1024]{1,0:T(8,128)(2,1)S(1)}, u32[]{:S(2)}, u32[]{:S(2)}) collective-permute-start(bf16[320,1024]{1,0:T(8,128)(2,1)S(1)} %copy-done.20), channel_id=1, source_target_pairs={{0,24},{1,7},{2,26},{3,1},{4,28},{5,3},{6,30},{7,5},{8,0},{9,15},{... | collective-permute-start | bytes 1966088 | tf_op jit(solution)/shard_map/ppermute | solution.py:246
  22.6 15.0 %collective-permute-start.6 = (bf16[320,1024]{1,0:T(8,128)(2,1)S(1)}, bf16[320,1024]{1,0:T(8,128)(2,1)S(1)}, u32[]{:S(2)}, u32[]{:S(2)}) collective-permute-start(bf16[320,1024]{1,0:T(8,128)(2,1)S(1)} %collective-permute-done.1.refs_1_), channel_id=1, source_target_pairs={{0,2},{1,9},{2,4},{3,11},{4,6},{5,13},{6,0},{7,15},{8,10},{9,17},{... | collective-permute-start | bytes 1966088 | tf_op jit(solution)/shard_map/ppermute | solution.py:246
  31.9 12.1 %collective-permute-start.9 = (bf16[320,1024]{1,0:T(8,128)(2,1)S(1)}, bf16[320,1024]{1,0:T(8,128)(2,1)}, u32[]{:S(2)}, u32[]{:S(2)}) collective-permute-start(bf16[320,1024]{1,0:T(8,128)(2,1)S(1)} %collective-permute-done.2.refs_2_), channel_id=1, source_target_pairs={{0,24},{1,7},{2,26},{3,1},{4,28},{5,3},{6,30},{7,5},{8,0},{9,15},{... | collective-permute-start | bytes 1966088 | tf_op jit(solution)/shard_map/ppermute | solution.py:246
  34.8 15.6 %collective-permute-start.7 = (bf16[320,1024]{1,0:T(8,128)(2,1)S(1)}, bf16[320,1024]{1,0:T(8,128)(2,1)S(1)}, u32[]{:S(2)}, u32[]{:S(2)}) collective-permute-start(bf16[320,1024]{1,0:T(8,128)(2,1)S(1)} %collective-permute-done.2.refs_2_), channel_id=1, source_target_pairs={{0,8},{1,3},{2,10},{3,5},{4,12},{5,7},{6,14},{7,1},{8,16},{9,11},{... | collective-permute-start | bytes 1966088 | tf_op jit(solution)/shard_map/ppermute | solution.py:246
  34.8 22.6 %collective-permute-start.5 = (bf16[320,1024]{1,0:T(8,128)(2,1)S(1)}, bf16[320,1024]{1,0:T(8,128)(2,1)S(1)}, u32[]{:S(2)}, u32[]{:S(2)}) collective-permute-start(bf16[320,1024]{1,0:T(8,128)(2,1)S(1)} %collective-permute-done.1.refs_1_), channel_id=1, source_target_pairs={{0,8},{1,3},{2,10},{3,5},{4,12},{5,7},{6,14},{7,1},{8,16},{9,11},{... | collective-permute-start | bytes 1966088 | tf_op jit(solution)/shard_map/ppermute | solution.py:246
  34.9 26.5 %collective-permute-start.8 = (bf16[320,1024]{1,0:T(8,128)(2,1)S(1)}, bf16[320,1024]{1,0:T(8,128)(2,1)S(1)}, u32[]{:S(2)}, u32[]{:S(2)}) collective-permute-start(bf16[320,1024]{1,0:T(8,128)(2,1)S(1)} %collective-permute-done.1.refs_1_), channel_id=1, source_target_pairs={{0,24},{1,7},{2,26},{3,1},{4,28},{5,3},{6,30},{7,5},{8,0},{9,15},{... | collective-permute-start | bytes 1966088 | tf_op jit(solution)/shard_map/ppermute | solution.py:246
  37.6 26.2 %collective-permute-start.12 = (bf16[320,1024]{1,0:T(8,128)(2,1)S(1)}, bf16[320,1024]{1,0:T(8,128)(2,1)}, u32[]{:S(2)}, u32[]{:S(2)}) collective-permute-start(bf16[320,1024]{1,0:T(8,128)(2,1)S(1)} %collective-permute-done.6.refs_2_), channel_id=1, source_target_pairs={{0,24},{1,7},{2,26},{3,1},{4,28},{5,3},{6,30},{7,5},{8,0},{9,15},{... | collective-permute-start | bytes 1966088 | tf_op jit(solution)/shard_map/ppermute | solution.py:246
  44.0 21.1 %collective-permute-start.10 = (bf16[320,1024]{1,0:T(8,128)(2,1)}, bf16[320,1024]{1,0:T(8,128)(2,1)}, u32[]{:S(2)}, u32[]{:S(2)}) collective-permute-start(bf16[320,1024]{1,0:T(8,128)(2,1)} %get-tuple-element.31), channel_id=1, source_target_pairs={{0,8},{1,3},{2,10},{3,5},{4,12},{5,7},{6,14},{7,1},{8,16},{9,11},{... | collective-permute-start | bytes 1966088 | tf_op jit(solution)/shard_map/ppermute | solution.py:246
  50.4 21.1 %collective-permute-start.11 = (bf16[320,1024]{1,0:T(8,128)(2,1)S(1)}, bf16[320,1024]{1,0:T(8,128)(2,1)}, u32[]{:S(2)}, u32[]{:S(2)}) collective-permute-start(bf16[320,1024]{1,0:T(8,128)(2,1)S(1)} %collective-permute-done.6.refs_2_), channel_id=1, source_target_pairs={{0,8},{1,3},{2,10},{3,5},{4,12},{5,7},{6,14},{7,1},{8,16},{9,11},{... | collective-permute-start | bytes 1966088 | tf_op jit(solution)/shard_map/ppermute | solution.py:246
  57.4 38.2 %collective-permute-start.14 = (bf16[320,1024]{1,0:T(8,128)(2,1)}, bf16[320,1024]{1,0:T(8,128)(2,1)}, u32[]{:S(2)}, u32[]{:S(2)}) collective-permute-start(bf16[320,1024]{1,0:T(8,128)(2,1)} %collective-permute-done.9.refs_1_), channel_id=1, source_target_pairs={{0,24},{1,7},{2,26},{3,1},{4,28},{5,3},{6,30},{7,5},{8,0},{9,15},{... | collective-permute-start | bytes 1966088 | tf_op jit(solution)/shard_map/ppermute | solution.py:246
  62.3 33.4 %collective-permute-start.13 = (bf16[320,1024]{1,0:T(8,128)(2,1)}, bf16[320,1024]{1,0:T(8,128)(2,1)}, u32[]{:S(2)}, u32[]{:S(2)}) collective-permute-start(bf16[320,1024]{1,0:T(8,128)(2,1)} %get-tuple-element.33), channel_id=1, source_target_pairs={{0,8},{1,3},{2,10},{3,5},{4,12},{5,7},{6,14},{7,1},{8,16},{9,11},{... | collective-permute-start | bytes 1966088 | tf_op jit(solution)/shard_map/ppermute | solution.py:246
  63.7 31.9 %collective-permute-start.15 = (bf16[320,1024]{1,0:T(8,128)(2,1)}, bf16[320,1024]{1,0:T(8,128)(2,1)}, u32[]{:S(2)}, u32[]{:S(2)}) collective-permute-start(bf16[320,1024]{1,0:T(8,128)(2,1)} %collective-permute-done.12.refs_0_), channel_id=1, source_target_pairs={{0,24},{1,7},{2,26},{3,1},{4,28},{5,3},{6,30},{7,5},{8,0},{9,15},{... | collective-permute-start | bytes 1966088 | tf_op jit(solution)/shard_map/ppermute | solution.py:246
  65.1 37.3 %collective-permute-start.16 = (f32[2560,128]{1,0:T(8,128)}, f32[2560,128]{1,0:T(8,128)}, u32[]{:S(2)}, u32[]{:S(2)}) collective-permute-start(f32[2560,128]{1,0:T(8,128)} %copy-done.18), channel_id=1, source_target_pairs={{0,1},{1,0},{2,3},{3,2},{4,5},{5,4},{6,7},{7,6},{8,9},{9,8},{10,11... | collective-permute-start | bytes 3932168 | tf_op jit(solution)/shard_map/ppermute | solution.py:245
  71.4 31.0 %collective-permute-start.17 = (f32[2560,128]{1,0:T(8,128)}, f32[2560,128]{1,0:T(8,128)}, u32[]{:S(2)}, u32[]{:S(2)}) collective-permute-start(f32[2560,128]{1,0:T(8,128)} %copy-done.19), channel_id=1, source_target_pairs={{0,1},{1,0},{2,3},{3,2},{4,5},{5,4},{6,7},{7,6},{8,9},{9,8},{10,11... | collective-permute-start | bytes 3932168 | tf_op jit(solution)/shard_map/ppermute | solution.py:245
  101.7 37.8 %collective-permute-start.28 = (bf16[4,160,1280]{2,1,0:T(8,128)(2,1)}, bf16[4,160,1280]{2,1,0:T(8,128)(2,1)S(1)}, u32[]{:S(2)}, u32[]{:S(2)}) collective-permute-start(bf16[4,160,1280]{2,1,0:T(8,128)(2,1)} %copy-done.17), channel_id=1, source_target_pairs={{0,1},{1,0},{2,3},{3,2},{4,5},{5,4},{6,7},{7,6},{8,9},{9,8},{10,11... | collective-permute-start | bytes 4915208 | tf_op jit(solution)/shard_map/ppermute | solution.py:245
  102.4 63.6 %collective-permute-start.30 = (f32[16,1024]{1,0:T(8,128)S(1)}, f32[16,1024]{1,0:T(8,128)S(1)}, u32[]{:S(2)}, u32[]{:S(2)}) collective-permute-start(f32[16,1024]{1,0:T(8,128)S(1)} %pad_maximum_fusion.2), channel_id=1, source_target_pairs={{0,1},{1,0},{2,3},{3,2},{4,5},{5,4},{6,7},{7,6},{8,9},{9,8},{10,11... | collective-permute-start | bytes 196616 | tf_op jit(solution)/shard_map/ppermute | solution.py:245
  136.7 13.8 %collective-permute-start.22 = (bf16[160,1280]{1,0:T(8,128)(2,1)S(1)}, bf16[160,1280]{1,0:T(8,128)(2,1)S(1)}, u32[]{:S(2)}, u32[]{:S(2)}) collective-permute-start(bf16[160,1280]{1,0:T(8,128)(2,1)S(1)} %get-tuple-element.65), channel_id=1, source_target_pairs={{0,32},{32,64},{64,96},{96,128},{128,160},{160,192},{192,224},{224... | collective-permute-start | bytes 1228808 | tf_op jit(solution)/shard_map/ppermute | solution.py:278
  136.8 13.7 %collective-permute-start.26 = (bf16[160,1280]{1,0:T(8,128)(2,1)S(1)}, bf16[160,1280]{1,0:T(8,128)(2,1)S(1)}, u32[]{:S(2)}, u32[]{:S(2)}) collective-permute-start(bf16[160,1280]{1,0:T(8,128)(2,1)S(1)} %get-tuple-element.66), channel_id=1, source_target_pairs={{0,224},{32,0},{64,32},{96,64},{128,96},{160,128},{192,160},{224,1... | collective-permute-start | bytes 1228808 | tf_op jit(solution)/shard_map/ppermute | solution.py:279
  151.7 15.6 %collective-permute-start.23 = (bf16[160,1280]{1,0:T(8,128)(2,1)}, bf16[160,1280]{1,0:T(8,128)(2,1)}, u32[]{:S(2)}, u32[]{:S(2)}) collective-permute-start(bf16[160,1280]{1,0:T(8,128)(2,1)} %get-tuple-element.55), channel_id=1, source_target_pairs={{0,32},{32,64},{64,96},{96,128},{128,160},{160,192},{192,224},{224... | collective-permute-start | bytes 1228808 | tf_op jit(solution)/shard_map/ppermute | solution.py:278
  151.7 15.6 %collective-permute-start.27 = (bf16[160,1280]{1,0:T(8,128)(2,1)}, bf16[160,1280]{1,0:T(8,128)(2,1)}, u32[]{:S(2)}, u32[]{:S(2)}) collective-permute-start(bf16[160,1280]{1,0:T(8,128)(2,1)} %get-tuple-element.56), channel_id=1, source_target_pairs={{0,224},{32,0},{64,32},{96,64},{128,96},{160,128},{192,160},{224,1... | collective-permute-start | bytes 1228808 | tf_op jit(solution)/shard_map/ppermute | solution.py:279
  (45 other events, 266.5 us)
Sparse Core Ops, SparseCore 0:
  9.8 50.0 all-gather.2

commit v2 on v1

--- a/solution.py
+++ b/solution.py
@@ -67,8 +67,14 @@
     return left, right[0:HID - LANES]
 
 
-def act_kernel(place_ref, act_ref, mine_ref, theirs_ref, rows, turned):
+def act_kernel(place_ref, act_ref, piece_ref, mine_ref, theirs_ref, next_ref, rows, turned, sem):
     block = pl.program_id(0)
+    copy = pltpu.make_async_copy(piece_ref, next_ref, sem)
+
+    @pl.when(block == 0)
+    def _():
+        copy.start()
+
     store_rows(turned, 0, act_ref[0].astype(F32).T)
 
     @pl.loop(0, BLOCK, step=UNROLL)
@@ -85,23 +91,33 @@
             out_ref = (mine_ref, theirs_ref)[group // GROUPS]
             out_ref[group % GROUPS, 0:LANES, :] = left.astype(BF16)
             out_ref[group % GROUPS, LANES:HID, :] = right.astype(BF16)
-
-
-def act_in_arrival_order(place, act):
+        copy.wait()
+
+
+def act_in_arrival_order(place, act, piece):
     return pl.pallas_call(
         act_kernel,
-        out_shape=[jax.ShapeDtypeStruct((GROUPS, HID, GROUP_ROWS), BF16)] * 2,
+        out_shape=[jax.ShapeDtypeStruct((GROUPS, HID, GROUP_ROWS), BF16)] * 2
+        + [jax.ShapeDtypeStruct(piece.shape, piece.dtype)],
         grid_spec=pltpu.PrefetchScalarGridSpec(
             num_scalar_prefetch=1,
             grid=(N_TILE,),
-            in_specs=[pl.BlockSpec((1, HID, BLOCK), lambda i, place: (i, 0, 0))],
-            out_specs=[pl.BlockSpec((GROUPS, HID, GROUP_ROWS), lambda i, place: (0, 0, 0), pipeline_mode=pl.Buffered(1))] * 2,
-            scratch_shapes=[pltpu.VMEM((2 * SLOTS, LANES), F32), pltpu.VMEM((2 * BLOCK, LANES), F32)],
+            in_specs=[
+                pl.BlockSpec((1, HID, BLOCK), lambda i, place: (i, 0, 0)),
+                pl.BlockSpec(memory_space=pl.ANY),
+            ],
+            out_specs=[pl.BlockSpec((GROUPS, HID, GROUP_ROWS), lambda i, place: (0, 0, 0), pipeline_mode=pl.Buffered(1))] * 2
+            + [pl.BlockSpec(memory_space=pl.ANY)],
+            scratch_shapes=[
+                pltpu.VMEM((2 * SLOTS, LANES), F32),
+                pltpu.VMEM((2 * BLOCK, LANES), F32),
+                pltpu.SemaphoreType.DMA(()),
+            ],
         ),
         compiler_params=pltpu.CompilerParams(vmem_limit_bytes=17 * 2**20),
         cost_estimate=pl.CostEstimate(flops=0, bytes_accessed=70_000_000, transcendentals=0),
         name="act_rows",
-    )(place, act)
+    )(place, act, piece)
 
 
 def product_kernel(hand_on, weight_ref, *refs):
@@ -188,7 +204,7 @@
         + [anywhere] * len(after),
         out_specs=[vmem] * len(out),
         scratch_shapes=scratch,
-        compiler_params=pltpu.CompilerParams(vmem_limit_bytes=(5 if whole else 46) * 2**20),
+        compiler_params=pltpu.CompilerParams(vmem_limit_bytes=(5 if whole else 50) * 2**20),
         cost_estimate=pl.CostEstimate(flops=0, bytes_accessed=8_000_000 * count, transcendentals=0),
         name="slot_rows",
     )(place, blocks, *rows, *after)
@@ -245,24 +261,23 @@
     swap = lambda value: lax.ppermute(value, "text", SWAP)
     send = lambda value, perm: lax.ppermute(value, "text", perm)
     weight = jnp.concatenate([w_out, swap(w_out)], axis=0)
-    act_mine, act_theirs = act_in_arrival_order(place, act_all)
-    act_theirs = swap(act_theirs)
 
     got = {(0, 0): grad_seq, (1, 0): send(grad_seq, FIRST_UP), (3, 0): send(grad_seq, FIRST_DOWN)}
     got[0, 1], got[0, 3] = send(grad_seq, SECOND_UP), send(grad_seq, SECOND_DOWN)
     got[2, 0] = send(got[1, 0], FIRST_UP)
     for first in (1, 3, 2):
         got[first, 1], got[first, 3] = send(got[first, 0], SECOND_UP), send(got[first, 0], SECOND_DOWN)
+    act_mine, act_theirs, late_piece = act_in_arrival_order(place, act_all, got[3, 3])
+    act_theirs = swap(act_theirs)
     mine, theirs, sums = [], [], []
     for g in range(GROUPS):
         pieces = [got[key] for key in ARRIVAL[4 * g:4 * g + 4]]
-        after = [act_mine] if g == GROUPS - 1 else []
-        kept, sent, part, *handed = products_of(weight, pieces, after, {0: 3, 1: 1}.get(g))
+        kept, sent, part, *handed = products_of(weight, pieces, [], {0: 3, 1: 1}.get(g))
         if g == 0:
             got[0, 2] = send(handed[0], SECOND_UP)
         if g == 1:
             got[1, 2] = send(handed[0], SECOND_UP)
-            got[3, 2], got[2, 2] = send(got[3, 3], SECOND_DOWN), send(got[2, 3], SECOND_DOWN)
+            got[3, 2], got[2, 2] = send(late_piece, SECOND_DOWN), send(got[2, 3], SECOND_DOWN)
         mine.append(kept)
         theirs.append(swap(sent))
         sums.append(part)

time: 179 us -> 180 us (level)
  Pallas kernels: 64.2 us -> 71.6 us
  waiting for transfers between devices: 30.5 us -> 26.2 us
  local copies, waits for them, and re-layouts: 12.6 us -> 10.6 us
    pallas_call x4, Pallas kernels: 12.5 us -> 16.7 us  [products_of(): pl.pallas_call(functools.partial(product_kernel, hand_on), out_shape=out...]
    ppermute x15, waiting for transfers between devices: 24.4 us -> 20.8 us  [body(): send = lambda value, perm: lax.ppermute(value, 'text', perm)]
    unnamed x75 -> x63, local copies, waits for them, and re-layouts: 11.6 us -> 8.28 us
    ppermute x15, starting transfers between devices: 17.7 us -> 20.3 us  [body(): send = lambda value, perm: lax.ppermute(value, 'text', perm)]
    pallas_call x4, Pallas kernels: 27.6 us -> 29.6 us  [to_slot_order(): pl.pallas_call(functools.partial(slot_kernel, count, not whole, keep), ou...]
    ppermute x8, starting transfers between devices: 15.5 us -> 13.5 us  [body(): swap = lambda value: lax.ppermute(value, 'text', SWAP)]
  transfers between devices with their start and end apart: 32 -> 32, of which waited for: 7 -> 6; matrix products, arithmetic and copies ran while one was open for 3% -> 4% of each run, Pallas kernels for 36% -> 40%
where the time goes in v2:
time: 180 us; the launch traced here: 179 us
  Pallas kernels  71.6 us (40%)
  starting transfers between devices  46.8 us (26%)
  waiting for transfers between devices  26.2 us (15%)
  between operations  14.6 us (8%)
  local copies, waits for them, and re-layouts  10.6 us (6%)
  other arithmetic  9.22 us (5%)
    pallas_call x4, Pallas kernels, to_slot_order(): pl.pallas_call(functools.partial(slot_kernel, count, not whole, keep), ou...  29.6 us
    ppermute x15, waiting for transfers between devices, body(): send = lambda value, perm: lax.ppermute(value, 'text', perm)  20.8 us
    ppermute x15, starting transfers between devices, body(): send = lambda value, perm: lax.ppermute(value, 'text', perm)  20.3 us
    pallas_call x4, Pallas kernels, products_of(): pl.pallas_call(functools.partial(product_kernel, hand_on), out_shape=out...  16.7 us
    pallas_call x1, Pallas kernels, act_in_arrival_order(): pl.pallas_call(act_kernel, out_shape=[jax.ShapeDtypeStruct((GROUPS, HID,...  14.3 us
    ppermute x8, starting transfers between devices, body(): swap = lambda value: lax.ppermute(value, 'text', SWAP)  13.5 us
    ppermute x4, starting transfers between devices, body(): down = lambda value: lax.ppermute(value.astype(BF16), 'tile', TILE_DOWN)  12.8 us
    pallas_call x4, Pallas kernels, weight_term(): pl.pallas_call(functools.partial(weight_kernel, not totals), out_shape=[j...  11 us
  transfers between devices with their start and end apart: 32, of which 6 were waited for; matrix products, arithmetic and copies ran while one was open for 4% of the time, Pallas kernels for 40%

profile of v2, /device:TPU:1, one launch (start us, length us, event | category | flops | bytes accessed | tf_op | source)
XLA Modules:
  0.0 179.0 jit_solution(4211697336417054175)
XLA Ops:
  16.1 6.5 %collective-permute-done.1.refs_1_ = bf16[320,1024]{1,0:T(8,128)(2,1)} collective-permute-done((bf16[320,1024]{1,0:T(8,128)(2,1)S(1)}, bf16[320,1024]{1,0:T(8,128)(2,1)}, u32[]{:S(2)}, u32[]{:S(2)}) %collective-permute-start.1) | collective-permute-done | bytes 655392 | tf_op jit(solution)/shard_map/ppermute | solution.py:262
  24.2 7.7 %collective-permute-start = (bf16[160,1024]{1,0:T(8,128)(2,1)S(1)}, bf16[160,1024]{1,0:T(8,128)(2,1)S(1)}, u32[]{:S(2)}, u32[]{:S(2)}) collective-permute-start(bf16[160,1024]{1,0:T(8,128)(2,1)S(1)} %copy-done.26), channel_id=1, source_target_pairs={{0,1},{1,0},{2,3},{3,2},{4,5},{5,4},{6,7},{7,6},{8,9},{9,8},{10,11... | collective-permute-start | bytes 983048 | tf_op jit(solution)/shard_map/ppermute | solution.py:261
  32.0 3.0 %collective-permute-start.9 = (bf16[320,1024]{1,0:T(8,128)(2,1)S(1)}, bf16[320,1024]{1,0:T(8,128)(2,1)S(1)}, u32[]{:S(2)}, u32[]{:S(2)}) collective-permute-start(bf16[320,1024]{1,0:T(8,128)(2,1)S(1)} %collective-permute-done.2.refs_2_), channel_id=1, source_target_pairs={{0,24},{1,7},{2,26},{3,1},{4,28},{5,3},{6,30},{7,5},{8,0},{9,15},{... | collective-permute-start | bytes 1966088 | tf_op jit(solution)/shard_map/ppermute | solution.py:262
  35.0 2.7 %collective-permute-start.8 = (bf16[320,1024]{1,0:T(8,128)(2,1)}, bf16[320,1024]{1,0:T(8,128)(2,1)}, u32[]{:S(2)}, u32[]{:S(2)}) collective-permute-start(bf16[320,1024]{1,0:T(8,128)(2,1)} %collective-permute-done.1.refs_1_), channel_id=1, source_target_pairs={{0,24},{1,7},{2,26},{3,1},{4,28},{5,3},{6,30},{7,5},{8,0},{9,15},{... | collective-permute-start | bytes 1966088 | tf_op jit(solution)/shard_map/ppermute | solution.py:262
  37.7 2.7 %collective-permute-start.12 = (bf16[320,1024]{1,0:T(8,128)(2,1)}, bf16[320,1024]{1,0:T(8,128)(2,1)}, u32[]{:S(2)}, u32[]{:S(2)}) collective-permute-start(bf16[320,1024]{1,0:T(8,128)(2,1)} %collective-permute-done.6.refs_2_), channel_id=1, source_target_pairs={{0,24},{1,7},{2,26},{3,1},{4,28},{5,3},{6,30},{7,5},{8,0},{9,15},{... | collective-permute-start | bytes 1966088 | tf_op jit(solution)/shard_map/ppermute | solution.py:262
  40.5 4.0 %products.4 = (f32[2560,128]{1,0:T(8,128)S(1)}, f32[2560,128]{1,0:T(8,128)}, f32[4,1024]{1,0:T(4,128)S(1)}, bf16[320,1024]{1,0:T(8,128)(2,1)}) custom-call(bf16[320,1024]{1,0:T(8,128)(2,1)S(1)} %constant_dynamic-update-slice_fusion.weight_ref, bf16[320,1024]{1,0:T(8,128)(2,1)S(1)} %copy-done.18, bf16[320,1024]{1,0:T(8,128)(2,1)} %collective-permute-done.1.refs_1_, ...), custom_call_target="tpu_custom_call" | custom-call | flops 1300000000 | bytes 8000000 | tf_op jit(solution)/shard_map/products/pallas_call | solution.py:145
  45.7 5.0 %collective-permute-done.7.refs_3_ = bf16[320,1024]{1,0:T(8,128)(2,1)S(1)} collective-permute-done((bf16[320,1024]{1,0:T(8,128)(2,1)S(1)}, bf16[320,1024]{1,0:T(8,128)(2,1)S(1)}, u32[]{:S(2)}, u32[]{:S(2)}) %collective-permute-start.7) | collective-permute-done | bytes 655392 | tf_op jit(solution)/shard_map/ppermute | solution.py:262
  50.7 7.0 %collective-permute-done.5.refs_1_ = bf16[320,1024]{1,0:T(8,128)(2,1)S(1)} collective-permute-done((bf16[320,1024]{1,0:T(8,128)(2,1)}, bf16[320,1024]{1,0:T(8,128)(2,1)S(1)}, u32[]{:S(2)}, u32[]{:S(2)}) %collective-permute-start.5) | collective-permute-done | bytes 655392 | tf_op jit(solution)/shard_map/ppermute | solution.py:262
  57.7 4.1 %products.5 = (f32[2560,128]{1,0:T(8,128)S(1)}, f32[2560,128]{1,0:T(8,128)}, f32[4,1024]{1,0:T(4,128)S(1)}, bf16[320,1024]{1,0:T(8,128)(2,1)}) custom-call(bf16[320,1024]{1,0:T(8,128)(2,1)S(1)} %constant_dynamic-update-slice_fusion.weight_ref, bf16[320,1024]{1,0:T(8,128)(2,1)S(1)} %collective-permute-done.4.refs_0_, ...), custom_call_target="tpu_custom_call" | custom-call | flops 1300000000 | bytes 8000000 | tf_op jit(solution)/shard_map/products/pallas_call | solution.py:145
  63.7 2.7 %collective-permute-start.15 = (bf16[320,1024]{1,0:T(8,128)(2,1)}, bf16[320,1024]{1,0:T(8,128)(2,1)}, u32[]{:S(2)}, u32[]{:S(2)}) collective-permute-start(bf16[320,1024]{1,0:T(8,128)(2,1)} %collective-permute-done.12.refs_0_), channel_id=1, source_target_pairs={{0,24},{1,7},{2,26},{3,1},{4,28},{5,3},{6,30},{7,5},{8,0},{9,15},{... | collective-permute-start | bytes 1966088 | tf_op jit(solution)/shard_map/ppermute | solution.py:262
  69.4 14.3 %act_rows.1 = (bf16[4,160,1280]{2,1,0:T(8,128)(2,1)S(1)}, bf16[4,160,1280]{2,1,0:T(8,128)(2,1)S(1)}, bf16[320,1024]{1,0:T(8,128)(2,1)S(1)}) custom-call(s32[10240]{0:T(1024)S(1)} %fusion.25.place_ref, bf16[8,160,1280]{2,1,0:T(8,128)(2,1)S(1)} %bitcast.92, bf16[320,1024]{1,0:T(8,128)(2,1)S(1)} %copy-done.13), custom_call_target="tpu_custom_call" | custom-call | bytes 70000000 | tf_op jit(solution)/shard_map/act_rows/pallas_call | solution.py:98
  85.6 4.2 %products.6 = (f32[2560,128]{1,0:T(8,128)S(1)}, f32[2560,128]{1,0:T(8,128)}, f32[4,1024]{1,0:T(4,128)S(1)}) custom-call(bf16[320,1024]{1,0:T(8,128)(2,1)S(1)} %copy-done.16, bf16[320,1024]{1,0:T(8,128)(2,1)} %collective-permute-done.8.refs_0_, bf16[320,1024]{1,0:T(8,128)(2,1)S(1)} %copy-done.13, bf16[320,1024]{1,0:T(8,128)(2,1)} %collective-permute-done.10.refs_2_, ...), custom_call_target="tpu_custom_call" | custom-call | flops 1300000000 | bytes 8000000 | tf_op jit(solution)/shard_map/products/pallas_call | solution.py:145
  93.3 4.4 %products.7 = (f32[2560,128]{1,0:T(8,128)S(1)}, f32[2560,128]{1,0:T(8,128)}, f32[4,1024]{1,0:T(4,128)S(1)}) custom-call(bf16[320,1024]{1,0:T(8,128)(2,1)S(1)} %copy-done.16, bf16[320,1024]{1,0:T(8,128)(2,1)} %collective-permute-done.12.refs_0_, bf16[320,1024]{1,0:T(8,128)(2,1)} %collective-permute-done.13.refs_1_, ...), custom_call_target="tpu_custom_call" | custom-call | flops 1300000000 | bytes 8000000 | tf_op jit(solution)/shard_map/products/pallas_call | solution.py:145
  99.4 2.7 %collective-permute-done.19.refs_7_ = f32[2560,128]{1,0:T(8,128)} collective-permute-done((f32[2560,128]{1,0:T(8,128)}, f32[2560,128]{1,0:T(8,128)}, u32[]{:S(2)}, u32[]{:S(2)}) %collective-permute-start.19) | collective-permute-done | bytes 1310752 | tf_op jit(solution)/shard_map/ppermute | solution.py:261
  102.1 7.0 %slot_rows.4 = (f32[20480,128]{1,0:T(8,128)S(1)}, f32[1,160,1280]{2,1,0:T(8,128)S(1)}) custom-call(s32[10240]{0:T(1024)} %copy-done.6, s32[1]{0:T(128)S(6)} %select_n.122.blocks_ref, f32[2560,128]{1,0:T(8,128)} %copy-done, f32[2560,128]{1,0:T(8,128)} %copy-done.2, f32[2560,128]{1,0:T(8,128)} %copy-done.3, f32[2560,128]{1,0:T(8,128)} %copy-done.4, ...), custom_call_target="tpu_custom_call" | custom-call | bytes 8000000 | tf_op jit(solution)/shard_map/slot_rows/pallas_call | solution.py:199
  109.2 4.7 %collective-permute-start.24 = (bf16[80,1280]{1,0:T(8,128)(2,1)S(1)}, bf16[80,1280]{1,0:T(8,128)(2,1)S(1)}, u32[]{:S(2)}, u32[]{:S(2)}) collective-permute-start(bf16[80,1280]{1,0:T(8,128)(2,1)S(1)} %get-tuple-element.73), channel_id=1, source_target_pairs={{0,224},{32,0},{64,32},{96,64},{128,96},{160,128},{192,160},{224,1... | collective-permute-start | bytes 614408 | tf_op jit(solution)/shard_map/ppermute | solution.py:294
  114.0 4.4 %slot_rows.5 = f32[2,160,1280]{2,1,0:T(8,128)S(1)} custom-call(s32[10240]{0:T(1024)S(1)} %copy-done.7, s32[2]{0:T(128)S(1)} %and_select_fusion.1.blocks_ref, f32[20480,128]{1,0:T(8,128)S(1)} %get-tuple-element.42.refs_0_, f32[1,160,1280]{2,1,0:T(8,128)S(1)} %get-tuple-element.41.refs_1_), custom_call_target="tpu_custom_call" | custom-call | bytes 16000000 | tf_op jit(solution)/shard_map/slot_rows/pallas_call | solution.py:199
  121.4 2.7 %collective-permute-start.25 = (bf16[160,1280]{1,0:T(8,128)(2,1)S(1)}, bf16[160,1280]{1,0:T(8,128)(2,1)S(1)}, u32[]{:S(2)}, u32[]{:S(2)}) collective-permute-start(bf16[160,1280]{1,0:T(8,128)(2,1)S(1)} %pad_maximum_fusion.1), channel_id=1, source_target_pairs={{0,224},{32,0},{64,32},{96,64},{128,96},{160,128},{192,160},{224,1... | collective-permute-start | bytes 1228808 | tf_op jit(solution)/shard_map/ppermute | solution.py:294
  126.4 8.2 %slot_rows.7 = f32[2,160,1280]{2,1,0:T(8,128)S(1)} custom-call(s32[10240]{0:T(1024)S(1)} %copy-done.7, s32[2]{0:T(128)S(1)} %and_select_fusion.blocks_ref, f32[2560,128]{1,0:T(8,128)S(1)} %copy-done.1, f32[2560,128]{1,0:T(8,128)} %copy-done.2, f32[2560,128]{1,0:T(8,128)} %copy-done.3, f32[2560,128]{1,0:T(8,128)} %copy-done.4, ...), custom_call_target="tpu_custom_call" | custom-call | bytes 16000000 | tf_op jit(solution)/shard_map/slot_rows/pallas_call | solution.py:199
  135.0 2.6 %collective-permute-start.26 = (bf16[160,1280]{1,0:T(8,128)(2,1)S(1)}, bf16[160,1280]{1,0:T(8,128)(2,1)S(1)}, u32[]{:S(2)}, u32[]{:S(2)}) collective-permute-start(bf16[160,1280]{1,0:T(8,128)(2,1)S(1)} %get-tuple-element.68), channel_id=1, source_target_pairs={{0,224},{32,0},{64,32},{96,64},{128,96},{160,128},{192,160},{224,1... | collective-permute-start | bytes 1228808 | tf_op jit(solution)/shard_map/ppermute | solution.py:294
  141.5 10.1 %slot_rows.6 = f32[3,160,1280]{2,1,0:T(8,128)S(1)} custom-call(s32[10240]{0:T(1024)S(1)} %copy-done.7, s32[3]{0:T(128)S(1)} %and_select_fusion.2.blocks_ref, f32[2560,128]{1,0:T(8,128)} %copy-done, f32[2560,128]{1,0:T(8,128)} %copy-done.2, f32[2560,128]{1,0:T(8,128)} %copy-done.3, f32[2560,128]{1,0:T(8,128)} %copy-done.4, ...), custom_call_target="tpu_custom_call" | custom-call | bytes 24000000 | tf_op jit(solution)/shard_map/slot_rows/pallas_call | solution.py:199
  152.7 2.7 %collective-permute-start.27 = (bf16[160,1280]{1,0:T(8,128)(2,1)}, bf16[160,1280]{1,0:T(8,128)(2,1)}, u32[]{:S(2)}, u32[]{:S(2)}) collective-permute-start(bf16[160,1280]{1,0:T(8,128)(2,1)} %get-tuple-element.58), channel_id=1, source_target_pairs={{0,224},{32,0},{64,32},{96,64},{128,96},{160,128},{192,160},{224,1... | collective-permute-start | bytes 1228808 | tf_op jit(solution)/shard_map/ppermute | solution.py:294
  158.0 2.6 %weight_term.6 = (f32[160,1024]{1,0:T(8,128)S(1)}, f32[160,1024]{1,0:T(8,128)S(1)}) custom-call(bf16[160,1280]{1,0:T(8,128)(2,1)S(1)} %get-tuple-element.65.mine_ref, bf16[160,1280]{1,0:T(8,128)(2,1)S(1)} %get-tuple-element.61.theirs_ref, bf16[320,1024]{1,0:T(8,128)(2,1)} %collective-permute-done.8.refs_0_, bf16[320,1024]{1,0:T(8,128)(2,1)S(1)} %copy-done.14, ...), custom_call_target="tpu_custom_call" | custom-call | flops 1300000000 | bytes 8000000 | tf_op jit(solution)/shard_map/weight_term/pallas_call | solution.py:233
  160.7 3.4 %weight_term.7 = (f32[160,1024]{1,0:T(8,128)S(1)}, f32[160,1024]{1,0:T(8,128)}) custom-call(bf16[160,1280]{1,0:T(8,128)(2,1)S(1)} %get-tuple-element.66.mine_ref, bf16[160,1280]{1,0:T(8,128)(2,1)S(1)} %get-tuple-element.62.theirs_ref, bf16[320,1024]{1,0:T(8,128)(2,1)} %collective-permute-done.12.refs_0_, bf16[320,1024]{1,0:T(8,128)(2,1)} %collective-permute-done.13.refs_1_, ...), custom_call_target="tpu_custom_call" | custom-call | flops 1300000000 | bytes 8000000 | tf_op jit(solution)/shard_map/weight_term/pallas_call | solution.py:233
  (142 shorter events, 45.0 us)
Async XLA Ops:
  7.2 59.2 %all-gather.3.cloned.1.call-start = ((), (), s32[]{:S(2)}) async-start(), calls=%async_computation | async-start | bytes 3686400 | tf_op jit(solution)/shard_map/all_gather | solution.py:260
  11.9 20.0 %collective-permute-start.2 = (bf16[320,1024]{1,0:T(8,128)(2,1)S(1)}, bf16[320,1024]{1,0:T(8,128)(2,1)S(1)}, u32[]{:S(2)}, u32[]{:S(2)}) collective-permute-start(bf16[320,1024]{1,0:T(8,128)(2,1)S(1)} %copy-done.18), channel_id=1, source_target_pairs={{0,6},{1,25},{2,0},{3,27},{4,2},{5,29},{6,4},{7,31},{8,14},{9,1},{... | collective-permute-start | bytes 1966088 | tf_op jit(solution)/shard_map/ppermute | solution.py:262
  13.5 21.6 %collective-permute-start.3 = (bf16[320,1024]{1,0:T(8,128)(2,1)S(1)}, bf16[320,1024]{1,0:T(8,128)(2,1)S(1)}, u32[]{:S(2)}, u32[]{:S(2)}) collective-permute-start(bf16[320,1024]{1,0:T(8,128)(2,1)S(1)} %copy-done.18), channel_id=1, source_target_pairs={{0,8},{1,3},{2,10},{3,5},{4,12},{5,7},{6,14},{7,1},{8,16},{9,11},{... | collective-permute-start | bytes 1966088 | tf_op jit(solution)/shard_map/ppermute | solution.py:262
  14.7 23.0 %collective-permute-start.4 = (bf16[320,1024]{1,0:T(8,128)(2,1)S(1)}, bf16[320,1024]{1,0:T(8,128)(2,1)S(1)}, u32[]{:S(2)}, u32[]{:S(2)}) collective-permute-start(bf16[320,1024]{1,0:T(8,128)(2,1)S(1)} %copy-done.18), channel_id=1, source_target_pairs={{0,24},{1,7},{2,26},{3,1},{4,28},{5,3},{6,30},{7,5},{8,0},{9,15},{... | collective-permute-start | bytes 1966088 | tf_op jit(solution)/shard_map/ppermute | solution.py:262
  22.7 15.0 %collective-permute-start.6 = (bf16[320,1024]{1,0:T(8,128)(2,1)}, bf16[320,1024]{1,0:T(8,128)(2,1)}, u32[]{:S(2)}, u32[]{:S(2)}) collective-permute-start(bf16[320,1024]{1,0:T(8,128)(2,1)} %collective-permute-done.1.refs_1_), channel_id=1, source_target_pairs={{0,2},{1,9},{2,4},{3,11},{4,6},{5,13},{6,0},{7,15},{8,10},{9,17},{... | collective-permute-start | bytes 1966088 | tf_op jit(solution)/shard_map/ppermute | solution.py:262
  32.0 30.9 %collective-permute-start.9 = (bf16[320,1024]{1,0:T(8,128)(2,1)S(1)}, bf16[320,1024]{1,0:T(8,128)(2,1)S(1)}, u32[]{:S(2)}, u32[]{:S(2)}) collective-permute-start(bf16[320,1024]{1,0:T(8,128)(2,1)S(1)} %collective-permute-done.2.refs_2_), channel_id=1, source_target_pairs={{0,24},{1,7},{2,26},{3,1},{4,28},{5,3},{6,30},{7,5},{8,0},{9,15},{... | collective-permute-start | bytes 1966088 | tf_op jit(solution)/shard_map/ppermute | solution.py:262
  35.0 15.7 %collective-permute-start.7 = (bf16[320,1024]{1,0:T(8,128)(2,1)S(1)}, bf16[320,1024]{1,0:T(8,128)(2,1)S(1)}, u32[]{:S(2)}, u32[]{:S(2)}) collective-permute-start(bf16[320,1024]{1,0:T(8,128)(2,1)S(1)} %collective-permute-done.2.refs_2_), channel_id=1, source_target_pairs={{0,8},{1,3},{2,10},{3,5},{4,12},{5,7},{6,14},{7,1},{8,16},{9,11},{... | collective-permute-start | bytes 1966088 | tf_op jit(solution)/shard_map/ppermute | solution.py:262
  35.0 48.7 %collective-permute-start.8 = (bf16[320,1024]{1,0:T(8,128)(2,1)}, bf16[320,1024]{1,0:T(8,128)(2,1)}, u32[]{:S(2)}, u32[]{:S(2)}) collective-permute-start(bf16[320,1024]{1,0:T(8,128)(2,1)} %collective-permute-done.1.refs_1_), channel_id=1, source_target_pairs={{0,24},{1,7},{2,26},{3,1},{4,28},{5,3},{6,30},{7,5},{8,0},{9,15},{... | collective-permute-start | bytes 1966088 | tf_op jit(solution)/shard_map/ppermute | solution.py:262
  37.7 20.0 %collective-permute-start.5 = (bf16[320,1024]{1,0:T(8,128)(2,1)}, bf16[320,1024]{1,0:T(8,128)(2,1)S(1)}, u32[]{:S(2)}, u32[]{:S(2)}) collective-permute-start(bf16[320,1024]{1,0:T(8,128)(2,1)} %collective-permute-done.1.refs_1_), channel_id=1, source_target_pairs={{0,8},{1,3},{2,10},{3,5},{4,12},{5,7},{6,14},{7,1},{8,16},{9,11},{... | collective-permute-start | bytes 1966088 | tf_op jit(solution)/shard_map/ppermute | solution.py:262
  37.7 26.0 %collective-permute-start.12 = (bf16[320,1024]{1,0:T(8,128)(2,1)}, bf16[320,1024]{1,0:T(8,128)(2,1)}, u32[]{:S(2)}, u32[]{:S(2)}) collective-permute-start(bf16[320,1024]{1,0:T(8,128)(2,1)} %collective-permute-done.6.refs_2_), channel_id=1, source_target_pairs={{0,24},{1,7},{2,26},{3,1},{4,28},{5,3},{6,30},{7,5},{8,0},{9,15},{... | collective-permute-start | bytes 1966088 | tf_op jit(solution)/shard_map/ppermute | solution.py:262
  50.7 34.4 %collective-permute-start.10 = (bf16[320,1024]{1,0:T(8,128)(2,1)}, bf16[320,1024]{1,0:T(8,128)(2,1)}, u32[]{:S(2)}, u32[]{:S(2)}) collective-permute-start(bf16[320,1024]{1,0:T(8,128)(2,1)} %get-tuple-element.32), channel_id=1, source_target_pairs={{0,8},{1,3},{2,10},{3,5},{4,12},{5,7},{6,14},{7,1},{8,16},{9,11},{... | collective-permute-start | bytes 1966088 | tf_op jit(solution)/shard_map/ppermute | solution.py:262
  57.7 27.4 %collective-permute-start.11 = (bf16[320,1024]{1,0:T(8,128)(2,1)}, bf16[320,1024]{1,0:T(8,128)(2,1)}, u32[]{:S(2)}, u32[]{:S(2)}) collective-permute-start(bf16[320,1024]{1,0:T(8,128)(2,1)} %collective-permute-done.6.refs_2_), channel_id=1, source_target_pairs={{0,8},{1,3},{2,10},{3,5},{4,12},{5,7},{6,14},{7,1},{8,16},{9,11},{... | collective-permute-start | bytes 1966088 | tf_op jit(solution)/shard_map/ppermute | solution.py:262
  63.7 27.1 %collective-permute-start.13 = (bf16[320,1024]{1,0:T(8,128)(2,1)}, bf16[320,1024]{1,0:T(8,128)(2,1)}, u32[]{:S(2)}, u32[]{:S(2)}) collective-permute-start(bf16[320,1024]{1,0:T(8,128)(2,1)} %get-tuple-element.34), channel_id=1, source_target_pairs={{0,8},{1,3},{2,10},{3,5},{4,12},{5,7},{6,14},{7,1},{8,16},{9,11},{... | collective-permute-start | bytes 1966088 | tf_op jit(solution)/shard_map/ppermute | solution.py:262
  63.7 27.3 %collective-permute-start.15 = (bf16[320,1024]{1,0:T(8,128)(2,1)}, bf16[320,1024]{1,0:T(8,128)(2,1)}, u32[]{:S(2)}, u32[]{:S(2)}) collective-permute-start(bf16[320,1024]{1,0:T(8,128)(2,1)} %collective-permute-done.12.refs_0_), channel_id=1, source_target_pairs={{0,24},{1,7},{2,26},{3,1},{4,28},{5,3},{6,30},{7,5},{8,0},{9,15},{... | collective-permute-start | bytes 1966088 | tf_op jit(solution)/shard_map/ppermute | solution.py:262
  85.1 14.4 %collective-permute-start.16 = (f32[2560,128]{1,0:T(8,128)}, f32[2560,128]{1,0:T(8,128)}, u32[]{:S(2)}, u32[]{:S(2)}) collective-permute-start(f32[2560,128]{1,0:T(8,128)} %get-tuple-element.37), channel_id=1, source_target_pairs={{0,1},{1,0},{2,3},{3,2},{4,5},{5,4},{6,7},{7,6},{8,9},{9,8},{10,11... | collective-permute-start | bytes 3932168 | tf_op jit(solution)/shard_map/ppermute | solution.py:261
  85.1 14.4 %collective-permute-start.17 = (f32[2560,128]{1,0:T(8,128)}, f32[2560,128]{1,0:T(8,128)}, u32[]{:S(2)}, u32[]{:S(2)}) collective-permute-start(f32[2560,128]{1,0:T(8,128)} %get-tuple-element.38), channel_id=1, source_target_pairs={{0,1},{1,0},{2,3},{3,2},{4,5},{5,4},{6,7},{7,6},{8,9},{9,8},{10,11... | collective-permute-start | bytes 3932168 | tf_op jit(solution)/shard_map/ppermute | solution.py:261
  98.8 38.8 %collective-permute-start.28 = (bf16[4,160,1280]{2,1,0:T(8,128)(2,1)}, bf16[4,160,1280]{2,1,0:T(8,128)(2,1)}, u32[]{:S(2)}, u32[]{:S(2)}) collective-permute-start(bf16[4,160,1280]{2,1,0:T(8,128)(2,1)} %copy-done.17), channel_id=1, source_target_pairs={{0,1},{1,0},{2,3},{3,2},{4,5},{5,4},{6,7},{7,6},{8,9},{9,8},{10,11... | collective-permute-start | bytes 4915208 | tf_op jit(solution)/shard_map/ppermute | solution.py:261
  121.3 13.4 %collective-permute-start.21 = (bf16[160,1280]{1,0:T(8,128)(2,1)S(1)}, bf16[160,1280]{1,0:T(8,128)(2,1)S(1)}, u32[]{:S(2)}, u32[]{:S(2)}) collective-permute-start(bf16[160,1280]{1,0:T(8,128)(2,1)S(1)} %pad_maximum_fusion), channel_id=1, source_target_pairs={{0,32},{32,64},{64,96},{96,128},{128,160},{160,192},{192,224},{224... | collective-permute-start | bytes 1228808 | tf_op jit(solution)/shard_map/ppermute | solution.py:293
  121.4 13.3 %collective-permute-start.25 = (bf16[160,1280]{1,0:T(8,128)(2,1)S(1)}, bf16[160,1280]{1,0:T(8,128)(2,1)S(1)}, u32[]{:S(2)}, u32[]{:S(2)}) collective-permute-start(bf16[160,1280]{1,0:T(8,128)(2,1)S(1)} %pad_maximum_fusion.1), channel_id=1, source_target_pairs={{0,224},{32,0},{64,32},{96,64},{128,96},{160,128},{192,160},{224,1... | collective-permute-start | bytes 1228808 | tf_op jit(solution)/shard_map/ppermute | solution.py:294
  124.3 42.2 %collective-permute-start.30 = (f32[16,1024]{1,0:T(8,128)S(1)}, f32[16,1024]{1,0:T(8,128)S(1)}, u32[]{:S(2)}, u32[]{:S(2)}) collective-permute-start(f32[16,1024]{1,0:T(8,128)S(1)} %pad_maximum_fusion.2), channel_id=1, source_target_pairs={{0,1},{1,0},{2,3},{3,2},{4,5},{5,4},{6,7},{7,6},{8,9},{9,8},{10,11... | collective-permute-start | bytes 196616 | tf_op jit(solution)/shard_map/ppermute | solution.py:261
  134.9 16.7 %collective-permute-start.22 = (bf16[160,1280]{1,0:T(8,128)(2,1)S(1)}, bf16[160,1280]{1,0:T(8,128)(2,1)S(1)}, u32[]{:S(2)}, u32[]{:S(2)}) collective-permute-start(bf16[160,1280]{1,0:T(8,128)(2,1)S(1)} %get-tuple-element.67), channel_id=1, source_target_pairs={{0,32},{32,64},{64,96},{96,128},{128,160},{160,192},{192,224},{224... | collective-permute-start | bytes 1228808 | tf_op jit(solution)/shard_map/ppermute | solution.py:293
  135.0 16.6 %collective-permute-start.26 = (bf16[160,1280]{1,0:T(8,128)(2,1)S(1)}, bf16[160,1280]{1,0:T(8,128)(2,1)S(1)}, u32[]{:S(2)}, u32[]{:S(2)}) collective-permute-start(bf16[160,1280]{1,0:T(8,128)(2,1)S(1)} %get-tuple-element.68), channel_id=1, source_target_pairs={{0,224},{32,0},{64,32},{96,64},{128,96},{160,128},{192,160},{224,1... | collective-permute-start | bytes 1228808 | tf_op jit(solution)/shard_map/ppermute | solution.py:294
  152.7 15.0 %collective-permute-start.23 = (bf16[160,1280]{1,0:T(8,128)(2,1)}, bf16[160,1280]{1,0:T(8,128)(2,1)}, u32[]{:S(2)}, u32[]{:S(2)}) collective-permute-start(bf16[160,1280]{1,0:T(8,128)(2,1)} %get-tuple-element.57), channel_id=1, source_target_pairs={{0,32},{32,64},{64,96},{96,128},{128,160},{160,192},{192,224},{224... | collective-permute-start | bytes 1228808 | tf_op jit(solution)/shard_map/ppermute | solution.py:293
  152.7 15.0 %collective-permute-start.27 = (bf16[160,1280]{1,0:T(8,128)(2,1)}, bf16[160,1280]{1,0:T(8,128)(2,1)}, u32[]{:S(2)}, u32[]{:S(2)}) collective-permute-start(bf16[160,1280]{1,0:T(8,128)(2,1)} %get-tuple-element.58), channel_id=1, source_target_pairs={{0,224},{32,0},{64,32},{96,64},{128,96},{160,128},{192,160},{224,1... | collective-permute-start | bytes 1228808 | tf_op jit(solution)/shard_map/ppermute | solution.py:294
  (39 other events, 300.0 us)
Sparse Core Ops, SparseCore 0:
  9.8 50.0 all-gather.2

commit v3 on v2

--- a/solution.py
+++ b/solution.py
@@ -210,6 +210,29 @@
     )(place, blocks, *rows, *after)
 
 
+def hop_kernel(which, fresh, terms_ref, come_ref, out_ref):
+    term, come = terms_ref[which], come_ref[...].astype(F32)
+    if fresh is None:
+        out_ref[...] = (term + come).astype(BF16)
+        return
+    added = slice(HALF, HID) if fresh == 0 else slice(0, HALF)
+    out_ref[added, :] = (term[added] + come).astype(BF16)
+    out_ref[fresh:fresh + HALF, :] = term[fresh:fresh + HALF].astype(BF16)
+
+
+def hop(which, fresh, terms, come):
+    vmem = pl.BlockSpec(memory_space=pltpu.VMEM)
+    return pl.pallas_call(
+        functools.partial(hop_kernel, which, fresh),
+        out_shape=jax.ShapeDtypeStruct((HID, BLOCK), BF16),
+        in_specs=[vmem] * 2,
+        out_specs=vmem,
+        compiler_params=pltpu.CompilerParams(vmem_limit_bytes=4 * 2**20),
+        cost_estimate=pl.CostEstimate(flops=0, bytes_accessed=1_500_000, transcendentals=0),
+        name="hop_sum",
+    )(terms, come)
+
+
 def weight_kernel(first, mine_ref, theirs_ref, *refs):
     pieces = refs[:4]
     out_mine, out_theirs, held, sems = refs[-4:]
@@ -265,16 +288,17 @@
     got = {(0, 0): grad_seq, (1, 0): send(grad_seq, FIRST_UP), (3, 0): send(grad_seq, FIRST_DOWN)}
     got[0, 1], got[0, 3] = send(grad_seq, SECOND_UP), send(grad_seq, SECOND_DOWN)
     got[2, 0] = send(got[1, 0], FIRST_UP)
-    for first in (1, 3, 2):
+    for first in (1, 2):
         got[first, 1], got[first, 3] = send(got[first, 0], SECOND_UP), send(got[first, 0], SECOND_DOWN)
+    got[0, 2] = send(got[0, 1], SECOND_UP)
+    first_products = products_of(weight, [got[key] for key in ARRIVAL[:4]], [], 2)
+    got[3, 1], got[3, 3] = send(first_products[3], SECOND_UP), send(got[3, 0], SECOND_DOWN)
     act_mine, act_theirs, late_piece = act_in_arrival_order(place, act_all, got[3, 3])
     act_theirs = swap(act_theirs)
     mine, theirs, sums = [], [], []
     for g in range(GROUPS):
         pieces = [got[key] for key in ARRIVAL[4 * g:4 * g + 4]]
-        kept, sent, part, *handed = products_of(weight, pieces, [], {0: 3, 1: 1}.get(g))
-        if g == 0:
-            got[0, 2] = send(handed[0], SECOND_UP)
+        kept, sent, part, *handed = first_products if g == 0 else products_of(weight, pieces, [], 1 if g == 1 else None)
         if g == 1:
             got[1, 2] = send(handed[0], SECOND_UP)
             got[3, 2], got[2, 2] = send(late_piece, SECOND_DOWN), send(got[2, 3], SECOND_DOWN)
@@ -294,17 +318,15 @@
     down = lambda value: lax.ppermute(value.astype(BF16), "tile", TILE_DOWN)
     rise, fall = up(across[0, :HALF]), down(across[0, HALF:])
     (second,) = slots([2, 6], parts, [rise])
-    up3 = jnp.concatenate([rise.astype(F32) + third[0, :HALF], third[0, HALF:]], axis=0)
-    down3 = jnp.concatenate([third[1, :HALF], fall.astype(F32) + third[1, HALF:]], axis=0)
-    rise, fall = up(up3), down(down3)
+    rise, fall = up(hop(0, HALF, third, rise)), down(hop(1, 0, third, fall))
     (nearest,) = slots([1, 7, 0], parts, [rise])
-    rise, fall = up(rise.astype(F32) + second[0]), down(fall.astype(F32) + second[1])
-    hop = rise
-    rise, fall = up(rise.astype(F32) + nearest[0]), down(fall.astype(F32) + nearest[1])
+    rise, fall = up(hop(0, None, second, rise)), down(hop(1, None, second, fall))
+    arrived = rise
+    rise, fall = up(hop(0, None, nearest, rise)), down(hop(1, None, nearest, fall))
     grad_pre = (nearest[2] + rise.astype(F32) + fall.astype(F32)) * lax.optimization_barrier(slope)
     totals = []
     for g in range(GROUPS):
-        totals = weight_term(act_mine[g], act_theirs[g], groups[g], totals, [hop] if g == 1 else [])
+        totals = weight_term(act_mine[g], act_theirs[g], groups[g], totals, [arrived] if g == 1 else [])
     grad_w = totals[0] + swap(totals[1])
     sums = jnp.concatenate(sums, axis=0)
     sums = jnp.concatenate([sums, swap(sums)], axis=0)

time: 180 us -> 176 us (0.978)
  starting transfers between devices: 46.8 us -> 38.7 us
  waiting for transfers between devices: 26.2 us -> 32 us
    ppermute x15, waiting for transfers between devices: 20.8 us -> 26.4 us  [body(): send = lambda value, perm: lax.ppermute(value, 'text', perm)]
    ppermute x8, starting transfers between devices: 13.5 us -> 9.98 us  [body(): swap = lambda value: lax.ppermute(value, 'text', SWAP)]
    ppermute x15, starting transfers between devices: 20.3 us -> 17 us  [body(): send = lambda value, perm: lax.ppermute(value, 'text', perm)]
    ppermute x4, starting transfers between devices: 12.8 us -> 9.81 us  [body(): down = lambda value: lax.ppermute(value.astype(BF16), 'tile', TILE_DOWN)]
    pallas_call x0 -> x6, Pallas kernels: none -> 2 us  [hop(): pl.pallas_call(functools.partial(hop_kernel, which, fresh), out_shape=jax...]
    unnamed x63 -> x51, local copies, waits for them, and re-layouts: 8.28 us -> 7.62 us
  transfers between devices with their start and end apart: 32 -> 32, of which waited for: 6 -> 6; matrix products, arithmetic and copies ran while one was open for 4% -> 3% of each run, Pallas kernels for 40% -> 41%
where the time goes in v3:
time: 176 us; the launch traced here: 175 us
  Pallas kernels  72.5 us (41%)
  starting transfers between devices  38.7 us (22%)
  waiting for transfers between devices  32 us (18%)
  between operations  14.5 us (8%)
  local copies, waits for them, and re-layouts  9.93 us (6%)
  other arithmetic  7.64 us (4%)
    pallas_call x4, Pallas kernels, to_slot_order(): pl.pallas_call(functools.partial(slot_kernel, count, not whole, keep), ou...  29.6 us
    ppermute x15, waiting for transfers between devices, body(): send = lambda value, perm: lax.ppermute(value, 'text', perm)  26.4 us
    ppermute x15, starting transfers between devices, body(): send = lambda value, perm: lax.ppermute(value, 'text', perm)  17 us
    pallas_call x4, Pallas kernels, products_of(): pl.pallas_call(functools.partial(product_kernel, hand_on), out_shape=out...  15.9 us
    pallas_call x1, Pallas kernels, act_in_arrival_order(): pl.pallas_call(act_kernel, out_shape=[jax.ShapeDtypeStruct((GROUPS, HID,...  14.1 us
    pallas_call x4, Pallas kernels, weight_term(): pl.pallas_call(functools.partial(weight_kernel, not totals), out_shape=[j...  10.9 us
    ppermute x8, starting transfers between devices, body(): swap = lambda value: lax.ppermute(value, 'text', SWAP)  9.98 us
    ppermute x4, starting transfers between devices, body(): down = lambda value: lax.ppermute(value.astype(BF16), 'tile', TILE_DOWN)  9.81 us
  transfers between devices with their start and end apart: 32, of which 6 were waited for; matrix products, arithmetic and copies ran while one was open for 3% of the time, Pallas kernels for 41%

profile of v3, /device:TPU:1, one launch (start us, length us, event | category | flops | bytes accessed | tf_op | source)
XLA Modules:
  0.0 175.3 jit_solution(7244796469714068994)
XLA Ops:
  7.2 2.4 %fusion.11 = (bf16[160,1280]{1,0:T(8,128)(2,1)}, f32[160,1280]{1,0:T(8,128)}) fusion(bf16[1280,160]{0,1:T(8,128)(2,1)} %param.10), kind=kLoop, calls=%fused_computation.16 | loop fusion | flops 2252800 | bytes 1638400 | tf_op jit(solution)/shard_map/convert_element_type | solution.py:283
  16.2 9.7 %collective-permute-done.1.refs_1_ = bf16[320,1024]{1,0:T(8,128)(2,1)} collective-permute-done((bf16[320,1024]{1,0:T(8,128)(2,1)}, bf16[320,1024]{1,0:T(8,128)(2,1)}, u32[]{:S(2)}, u32[]{:S(2)}) %collective-permute-start.1) | collective-permute-done | bytes 655392 | tf_op jit(solution)/shard_map/ppermute | solution.py:285
  26.3 3.3 %collective-permute-start.4 = (bf16[320,1024]{1,0:T(8,128)(2,1)}, bf16[320,1024]{1,0:T(8,128)(2,1)S(1)}, u32[]{:S(2)}, u32[]{:S(2)}) collective-permute-start(bf16[320,1024]{1,0:T(8,128)(2,1)} %refs_0_.3), channel_id=1, source_target_pairs={{0,24},{1,7},{2,26},{3,1},{4,28},{5,3},{6,30},{7,5},{8,0},{9,15},{... | collective-permute-start | bytes 1966088 | tf_op jit(solution)/shard_map/ppermute | solution.py:285
  29.7 4.5 %products.4 = (f32[2560,128]{1,0:T(8,128)S(1)}, f32[2560,128]{1,0:T(8,128)}, f32[4,1024]{1,0:T(4,128)S(1)}, bf16[320,1024]{1,0:T(8,128)(2,1)}) custom-call(bf16[320,1024]{1,0:T(8,128)(2,1)S(1)} %constant_dynamic-update-slice_fusion.weight_ref, bf16[320,1024]{1,0:T(8,128)(2,1)} %refs_0_.3, bf16[320,1024]{1,0:T(8,128)(2,1)} %collective-permute-done.1.refs_1_, ...), custom_call_target="tpu_custom_call" | custom-call | flops 1300000000 | bytes 8000000 | tf_op jit(solution)/shard_map/products/pallas_call | solution.py:145
  35.5 2.5 %collective-permute-start.9 = (bf16[320,1024]{1,0:T(8,128)(2,1)}, bf16[320,1024]{1,0:T(8,128)(2,1)}, u32[]{:S(2)}, u32[]{:S(2)}) collective-permute-start(bf16[320,1024]{1,0:T(8,128)(2,1)} %collective-permute-done.2.refs_2_), channel_id=1, source_target_pairs={{0,24},{1,7},{2,26},{3,1},{4,28},{5,3},{6,30},{7,5},{8,0},{9,15},{... | collective-permute-start | bytes 1966088 | tf_op jit(solution)/shard_map/ppermute | solution.py:285
  39.9 6.8 %collective-permute-done.5.refs_1_ = bf16[320,1024]{1,0:T(8,128)(2,1)S(1)} collective-permute-done((bf16[320,1024]{1,0:T(8,128)(2,1)}, bf16[320,1024]{1,0:T(8,128)(2,1)S(1)}, u32[]{:S(2)}, u32[]{:S(2)}) %collective-permute-start.5) | collective-permute-done | bytes 655392 | tf_op jit(solution)/shard_map/ppermute | solution.py:285
  46.7 8.4 %collective-permute-done.7.refs_3_ = bf16[320,1024]{1,0:T(8,128)(2,1)S(1)} collective-permute-done((bf16[320,1024]{1,0:T(8,128)(2,1)}, bf16[320,1024]{1,0:T(8,128)(2,1)S(1)}, u32[]{:S(2)}, u32[]{:S(2)}) %collective-permute-start.7) | collective-permute-done | bytes 655392 | tf_op jit(solution)/shard_map/ppermute | solution.py:285
  56.4 2.6 %products.5 = (f32[2560,128]{1,0:T(8,128)S(1)}, f32[2560,128]{1,0:T(8,128)}, f32[4,1024]{1,0:T(4,128)S(1)}, bf16[320,1024]{1,0:T(8,128)(2,1)}) custom-call(bf16[320,1024]{1,0:T(8,128)(2,1)S(1)} %copy-done.15, bf16[320,1024]{1,0:T(8,128)(2,1)S(1)} %collective-permute-done.4.refs_0_, bf16[320,1024]{1,0:T(8,128)(2,1)S(1)} %collective-permute-done.5.refs_1_, ...), custom_call_target="tpu_custom_call" | custom-call | flops 1300000000 | bytes 8000000 | tf_op jit(solution)/shard_map/products/pallas_call | solution.py:145
  60.1 2.7 %collective-permute-start.15 = (bf16[320,1024]{1,0:T(8,128)(2,1)}, bf16[320,1024]{1,0:T(8,128)(2,1)}, u32[]{:S(2)}, u32[]{:S(2)}) collective-permute-start(bf16[320,1024]{1,0:T(8,128)(2,1)} %collective-permute-done.12.refs_0_), channel_id=1, source_target_pairs={{0,24},{1,7},{2,26},{3,1},{4,28},{5,3},{6,30},{7,5},{8,0},{9,15},{... | collective-permute-start | bytes 1966088 | tf_op jit(solution)/shard_map/ppermute | solution.py:285
  64.7 14.1 %act_rows.1 = (bf16[4,160,1280]{2,1,0:T(8,128)(2,1)S(1)}, bf16[4,160,1280]{2,1,0:T(8,128)(2,1)S(1)}, bf16[320,1024]{1,0:T(8,128)(2,1)S(1)}) custom-call(s32[10240]{0:T(1024)S(1)} %fusion.13.place_ref, bf16[8,160,1280]{2,1,0:T(8,128)(2,1)S(1)} %bitcast.52, bf16[320,1024]{1,0:T(8,128)(2,1)} %collective-permute-done.9.refs_1_.piece_ref), custom_call_target="tpu_custom_call" | custom-call | bytes 70000000 | tf_op jit(solution)/shard_map/act_rows/pallas_call | solution.py:98
  81.2 4.4 %products.6 = (f32[2560,128]{1,0:T(8,128)S(1)}, f32[2560,128]{1,0:T(8,128)}, f32[4,1024]{1,0:T(4,128)S(1)}) custom-call(bf16[320,1024]{1,0:T(8,128)(2,1)S(1)} %copy-done.16, bf16[320,1024]{1,0:T(8,128)(2,1)} %collective-permute-done.8.refs_0_, bf16[320,1024]{1,0:T(8,128)(2,1)} %collective-permute-done.9.refs_1_.piece_ref, ...), custom_call_target="tpu_custom_call" | custom-call | flops 1300000000 | bytes 8000000 | tf_op jit(solution)/shard_map/products/pallas_call | solution.py:145
  88.6 4.4 %products.7 = (f32[2560,128]{1,0:T(8,128)S(1)}, f32[2560,128]{1,0:T(8,128)}, f32[4,1024]{1,0:T(4,128)S(1)}) custom-call(bf16[320,1024]{1,0:T(8,128)(2,1)S(1)} %copy-done.16, bf16[320,1024]{1,0:T(8,128)(2,1)} %collective-permute-done.12.refs_0_, bf16[320,1024]{1,0:T(8,128)(2,1)} %collective-permute-done.13.refs_1_, ...), custom_call_target="tpu_custom_call" | custom-call | flops 1300000000 | bytes 8000000 | tf_op jit(solution)/shard_map/products/pallas_call | solution.py:145
  95.7 2.8 %collective-permute-done.19.refs_7_ = f32[2560,128]{1,0:T(8,128)} collective-permute-done((f32[2560,128]{1,0:T(8,128)}, f32[2560,128]{1,0:T(8,128)}, u32[]{:S(2)}, u32[]{:S(2)}) %collective-permute-start.19) | collective-permute-done | bytes 1310752 | tf_op jit(solution)/shard_map/ppermute | solution.py:284
  98.5 7.0 %slot_rows.4 = (f32[20480,128]{1,0:T(8,128)S(1)}, f32[1,160,1280]{2,1,0:T(8,128)S(1)}) custom-call(s32[10240]{0:T(1024)} %copy-done.6, s32[1]{0:T(128)S(6)} %select_n.123.blocks_ref, f32[2560,128]{1,0:T(8,128)} %copy-done, f32[2560,128]{1,0:T(8,128)} %copy-done.2, f32[2560,128]{1,0:T(8,128)} %copy-done.3, f32[2560,128]{1,0:T(8,128)} %copy-done.4, ...), custom_call_target="tpu_custom_call" | custom-call | bytes 8000000 | tf_op jit(solution)/shard_map/slot_rows/pallas_call | solution.py:199
  105.6 5.8 %collective-permute-start.24 = (bf16[80,1280]{1,0:T(8,128)(2,1)S(1)}, bf16[80,1280]{1,0:T(8,128)(2,1)S(1)}, u32[]{:S(2)}, u32[]{:S(2)}) collective-permute-start(bf16[80,1280]{1,0:T(8,128)(2,1)S(1)} %get-tuple-element.65), channel_id=1, source_target_pairs={{0,224},{32,0},{64,32},{96,64},{128,96},{160,128},{192,160},{224,1... | collective-permute-start | bytes 614408 | tf_op jit(solution)/shard_map/ppermute | solution.py:318
  111.3 4.4 %slot_rows.5.terms_ref = f32[2,160,1280]{2,1,0:T(8,128)S(1)} custom-call(s32[10240]{0:T(1024)S(1)} %copy-done.7, s32[2]{0:T(128)S(1)} %and_select_fusion.1.blocks_ref, f32[20480,128]{1,0:T(8,128)S(1)} %get-tuple-element.41.refs_0_, f32[1,160,1280]{2,1,0:T(8,128)S(1)} %get-tuple-element.42.refs_1_), custom_call_target="tpu_custom_call" | custom-call | bytes 16000000 | tf_op jit(solution)/shard_map/slot_rows/pallas_call | solution.py:199
  115.7 2.8 %collective-permute-done.20.come_ref.refs_8_ = bf16[80,1280]{1,0:T(8,128)(2,1)S(1)} collective-permute-done((bf16[80,1280]{1,0:T(8,128)(2,1)S(1)}, bf16[80,1280]{1,0:T(8,128)(2,1)S(1)}, u32[]{:S(2)}, u32[]{:S(2)}) %collective-permute-start.20) | collective-permute-done | bytes 204832 | tf_op jit(solution)/shard_map/ppermute | solution.py:317
  118.7 2.7 %collective-permute-start.25 = (bf16[160,1280]{1,0:T(8,128)(2,1)S(1)}, bf16[160,1280]{1,0:T(8,128)(2,1)S(1)}, u32[]{:S(2)}, u32[]{:S(2)}) collective-permute-start(bf16[160,1280]{1,0:T(8,128)(2,1)S(1)} %hop_sum.9), channel_id=1, source_target_pairs={{0,224},{32,0},{64,32},{96,64},{128,96},{160,128},{192,160},{224,1... | collective-permute-start | bytes 1228808 | tf_op jit(solution)/shard_map/ppermute | solution.py:318
  123.8 8.2 %slot_rows.7.terms_ref = f32[2,160,1280]{2,1,0:T(8,128)S(1)} custom-call(s32[10240]{0:T(1024)S(1)} %copy-done.7, s32[2]{0:T(128)S(1)} %and_select_fusion.blocks_ref, f32[2560,128]{1,0:T(8,128)S(1)} %copy-done.1, f32[2560,128]{1,0:T(8,128)} %copy-done.2, f32[2560,128]{1,0:T(8,128)} %copy-done.3, f32[2560,128]{1,0:T(8,128)} %copy-done.4, ...), custom_call_target="tpu_custom_call" | custom-call | bytes 16000000 | tf_op jit(solution)/shard_map/slot_rows/pallas_call | solution.py:199
  135.3 2.7 %weight_term.4 = (f32[160,1024]{1,0:T(8,128)S(1)}, f32[160,1024]{1,0:T(8,128)S(1)}) custom-call(bf16[160,1280]{1,0:T(8,128)(2,1)S(1)} %get-tuple-element.61.mine_ref, bf16[160,1280]{1,0:T(8,128)(2,1)S(1)} %get-tuple-element.57.theirs_ref, bf16[320,1024]{1,0:T(8,128)(2,1)} %refs_0_.3, bf16[320,1024]{1,0:T(8,128)(2,1)} %collective-permute-done.1.refs_1_, ...), custom_call_target="tpu_custom_call" | custom-call | flops 1300000000 | bytes 8000000 | tf_op jit(solution)/shard_map/weight_term/pallas_call | solution.py:256
  138.0 10.1 %slot_rows.6.terms_ref = f32[3,160,1280]{2,1,0:T(8,128)S(1)} custom-call(s32[10240]{0:T(1024)S(1)} %copy-done.7, s32[3]{0:T(128)S(1)} %and_select_fusion.2.blocks_ref, f32[2560,128]{1,0:T(8,128)} %copy-done, f32[2560,128]{1,0:T(8,128)} %copy-done.2, f32[2560,128]{1,0:T(8,128)} %copy-done.3, f32[2560,128]{1,0:T(8,128)} %copy-done.4, ...), custom_call_target="tpu_custom_call" | custom-call | bytes 24000000 | tf_op jit(solution)/shard_map/slot_rows/pallas_call | solution.py:199
  153.2 2.8 %weight_term.6 = (f32[160,1024]{1,0:T(8,128)S(1)}, f32[160,1024]{1,0:T(8,128)S(1)}) custom-call(bf16[160,1280]{1,0:T(8,128)(2,1)S(1)} %get-tuple-element.63.mine_ref, bf16[160,1280]{1,0:T(8,128)(2,1)S(1)} %get-tuple-element.59.theirs_ref, bf16[320,1024]{1,0:T(8,128)(2,1)} %collective-permute-done.8.refs_0_, ...), custom_call_target="tpu_custom_call" | custom-call | flops 1300000000 | bytes 8000000 | tf_op jit(solution)/shard_map/weight_term/pallas_call | solution.py:256
  156.0 3.4 %weight_term.7 = (f32[160,1024]{1,0:T(8,128)S(1)}, f32[160,1024]{1,0:T(8,128)}) custom-call(bf16[160,1280]{1,0:T(8,128)(2,1)S(1)} %get-tuple-element.64.mine_ref, bf16[160,1280]{1,0:T(8,128)(2,1)S(1)} %get-tuple-element.60.theirs_ref, bf16[320,1024]{1,0:T(8,128)(2,1)} %collective-permute-done.12.refs_0_, bf16[320,1024]{1,0:T(8,128)(2,1)} %collective-permute-done.13.refs_1_, ...), custom_call_target="tpu_custom_call" | custom-call | flops 1300000000 | bytes 8000000 | tf_op jit(solution)/shard_map/weight_term/pallas_call | solution.py:256
  159.5 3.3 %collective-permute-start.29 = (f32[160,1024]{1,0:T(8,128)}, f32[160,1024]{1,0:T(8,128)}, u32[]{:S(2)}, u32[]{:S(2)}) collective-permute-start(f32[160,1024]{1,0:T(8,128)} %get-tuple-element.52), channel_id=1, source_target_pairs={{0,1},{1,0},{2,3},{3,2},{4,5},{5,4},{6,7},{7,6},{8,9},{9,8},{10,11... | collective-permute-start | bytes 1966088 | tf_op jit(solution)/shard_map/ppermute | solution.py:284
  (129 shorter events, 39.1 us)
Async XLA Ops:
  7.2 55.6 %all-gather.3.cloned.1.call-start = ((), (), s32[]{:S(2)}) async-start(), calls=%async_computation | async-start | bytes 3686400 | tf_op jit(solution)/shard_map/all_gather | solution.py:283
  9.7 16.3 %collective-permute-start.1 = (bf16[320,1024]{1,0:T(8,128)(2,1)}, bf16[320,1024]{1,0:T(8,128)(2,1)}, u32[]{:S(2)}, u32[]{:S(2)}) collective-permute-start(bf16[320,1024]{1,0:T(8,128)(2,1)} %refs_0_.3), channel_id=1, source_target_pairs={{0,2},{1,9},{2,4},{3,11},{4,6},{5,13},{6,0},{7,15},{8,10},{9,17},{... | collective-permute-start | bytes 1966088 | tf_op jit(solution)/shard_map/ppermute | solution.py:285
  11.9 17.9 %collective-permute-start.3 = (bf16[320,1024]{1,0:T(8,128)(2,1)}, bf16[320,1024]{1,0:T(8,128)(2,1)}, u32[]{:S(2)}, u32[]{:S(2)}) collective-permute-start(bf16[320,1024]{1,0:T(8,128)(2,1)} %refs_0_.3), channel_id=1, source_target_pairs={{0,8},{1,3},{2,10},{3,5},{4,12},{5,7},{6,14},{7,1},{8,16},{9,11},{... | collective-permute-start | bytes 1966088 | tf_op jit(solution)/shard_map/ppermute | solution.py:285
  13.1 16.7 %collective-permute-start.2 = (bf16[320,1024]{1,0:T(8,128)(2,1)}, bf16[320,1024]{1,0:T(8,128)(2,1)}, u32[]{:S(2)}, u32[]{:S(2)}) collective-permute-start(bf16[320,1024]{1,0:T(8,128)(2,1)} %refs_0_.3), channel_id=1, source_target_pairs={{0,6},{1,25},{2,0},{3,27},{4,2},{5,29},{6,4},{7,31},{8,14},{9,1},{... | collective-permute-start | bytes 1966088 | tf_op jit(solution)/shard_map/ppermute | solution.py:285
  14.6 15.0 %collective-permute-start = (bf16[160,1024]{1,0:T(8,128)(2,1)S(1)}, bf16[160,1024]{1,0:T(8,128)(2,1)S(1)}, u32[]{:S(2)}, u32[]{:S(2)}) collective-permute-start(bf16[160,1024]{1,0:T(8,128)(2,1)S(1)} %copy-done.20), channel_id=1, source_target_pairs={{0,1},{1,0},{2,3},{3,2},{4,5},{5,4},{6,7},{7,6},{8,9},{9,8},{10,11... | collective-permute-start | bytes 983048 | tf_op jit(solution)/shard_map/ppermute | solution.py:284
  26.3 13.5 %collective-permute-start.4 = (bf16[320,1024]{1,0:T(8,128)(2,1)}, bf16[320,1024]{1,0:T(8,128)(2,1)S(1)}, u32[]{:S(2)}, u32[]{:S(2)}) collective-permute-start(bf16[320,1024]{1,0:T(8,128)(2,1)} %refs_0_.3), channel_id=1, source_target_pairs={{0,24},{1,7},{2,26},{3,1},{4,28},{5,3},{6,30},{7,5},{8,0},{9,15},{... | collective-permute-start | bytes 1966088 | tf_op jit(solution)/shard_map/ppermute | solution.py:285
  29.6 17.0 %collective-permute-start.5 = (bf16[320,1024]{1,0:T(8,128)(2,1)}, bf16[320,1024]{1,0:T(8,128)(2,1)S(1)}, u32[]{:S(2)}, u32[]{:S(2)}) collective-permute-start(bf16[320,1024]{1,0:T(8,128)(2,1)} %collective-permute-done.1.refs_1_), channel_id=1, source_target_pairs={{0,8},{1,3},{2,10},{3,5},{4,12},{5,7},{6,14},{7,1},{8,16},{9,11},{... | collective-permute-start | bytes 1966088 | tf_op jit(solution)/shard_map/ppermute | solution.py:285
  35.4 19.7 %collective-permute-start.7 = (bf16[320,1024]{1,0:T(8,128)(2,1)}, bf16[320,1024]{1,0:T(8,128)(2,1)S(1)}, u32[]{:S(2)}, u32[]{:S(2)}) collective-permute-start(bf16[320,1024]{1,0:T(8,128)(2,1)} %get-tuple-element.31), channel_id=1, source_target_pairs={{0,8},{1,3},{2,10},{3,5},{4,12},{5,7},{6,14},{7,1},{8,16},{9,11},{... | collective-permute-start | bytes 1966088 | tf_op jit(solution)/shard_map/ppermute | solution.py:285
  35.5 24.6 %collective-permute-start.9 = (bf16[320,1024]{1,0:T(8,128)(2,1)}, bf16[320,1024]{1,0:T(8,128)(2,1)}, u32[]{:S(2)}, u32[]{:S(2)}) collective-permute-start(bf16[320,1024]{1,0:T(8,128)(2,1)} %collective-permute-done.2.refs_2_), channel_id=1, source_target_pairs={{0,24},{1,7},{2,26},{3,1},{4,28},{5,3},{6,30},{7,5},{8,0},{9,15},{... | collective-permute-start | bytes 1966088 | tf_op jit(solution)/shard_map/ppermute | solution.py:285
  38.0 22.1 %collective-permute-start.12 = (bf16[320,1024]{1,0:T(8,128)(2,1)S(1)}, bf16[320,1024]{1,0:T(8,128)(2,1)}, u32[]{:S(2)}, u32[]{:S(2)}) collective-permute-start(bf16[320,1024]{1,0:T(8,128)(2,1)S(1)} %collective-permute-done.6.refs_2_), channel_id=1, source_target_pairs={{0,24},{1,7},{2,26},{3,1},{4,28},{5,3},{6,30},{7,5},{8,0},{9,15},{... | collective-permute-start | bytes 1966088 | tf_op jit(solution)/shard_map/ppermute | solution.py:285
  39.8 39.0 %collective-permute-start.10 = (bf16[320,1024]{1,0:T(8,128)(2,1)}, bf16[320,1024]{1,0:T(8,128)(2,1)}, u32[]{:S(2)}, u32[]{:S(2)}) collective-permute-start(bf16[320,1024]{1,0:T(8,128)(2,1)} %collective-permute-done.3.refs_3_), channel_id=1, source_target_pairs={{0,8},{1,3},{2,10},{3,5},{4,12},{5,7},{6,14},{7,1},{8,16},{9,11},{... | collective-permute-start | bytes 1966088 | tf_op jit(solution)/shard_map/ppermute | solution.py:285
  46.7 33.5 %collective-permute-start.8 = (bf16[320,1024]{1,0:T(8,128)(2,1)}, bf16[320,1024]{1,0:T(8,128)(2,1)}, u32[]{:S(2)}, u32[]{:S(2)}) collective-permute-start(bf16[320,1024]{1,0:T(8,128)(2,1)} %collective-permute-done.1.refs_1_), channel_id=1, source_target_pairs={{0,24},{1,7},{2,26},{3,1},{4,28},{5,3},{6,30},{7,5},{8,0},{9,15},{... | collective-permute-start | bytes 1966088 | tf_op jit(solution)/shard_map/ppermute | solution.py:285
  55.0 26.1 %collective-permute-start.11 = (bf16[320,1024]{1,0:T(8,128)(2,1)S(1)}, bf16[320,1024]{1,0:T(8,128)(2,1)}, u32[]{:S(2)}, u32[]{:S(2)}) collective-permute-start(bf16[320,1024]{1,0:T(8,128)(2,1)S(1)} %collective-permute-done.6.refs_2_), channel_id=1, source_target_pairs={{0,8},{1,3},{2,10},{3,5},{4,12},{5,7},{6,14},{7,1},{8,16},{9,11},{... | collective-permute-start | bytes 1966088 | tf_op jit(solution)/shard_map/ppermute | solution.py:285
  60.1 26.5 %collective-permute-start.13 = (bf16[320,1024]{1,0:T(8,128)(2,1)}, bf16[320,1024]{1,0:T(8,128)(2,1)}, u32[]{:S(2)}, u32[]{:S(2)}) collective-permute-start(bf16[320,1024]{1,0:T(8,128)(2,1)} %get-tuple-element.34), channel_id=1, source_target_pairs={{0,8},{1,3},{2,10},{3,5},{4,12},{5,7},{6,14},{7,1},{8,16},{9,11},{... | collective-permute-start | bytes 1966088 | tf_op jit(solution)/shard_map/ppermute | solution.py:285
  60.1 27.0 %collective-permute-start.15 = (bf16[320,1024]{1,0:T(8,128)(2,1)}, bf16[320,1024]{1,0:T(8,128)(2,1)}, u32[]{:S(2)}, u32[]{:S(2)}) collective-permute-start(bf16[320,1024]{1,0:T(8,128)(2,1)} %collective-permute-done.12.refs_0_), channel_id=1, source_target_pairs={{0,24},{1,7},{2,26},{3,1},{4,28},{5,3},{6,30},{7,5},{8,0},{9,15},{... | collective-permute-start | bytes 1966088 | tf_op jit(solution)/shard_map/ppermute | solution.py:285
  80.1 15.5 %collective-permute-start.16 = (f32[2560,128]{1,0:T(8,128)}, f32[2560,128]{1,0:T(8,128)}, u32[]{:S(2)}, u32[]{:S(2)}) collective-permute-start(f32[2560,128]{1,0:T(8,128)} %get-tuple-element.37), channel_id=1, source_target_pairs={{0,1},{1,0},{2,3},{3,2},{4,5},{5,4},{6,7},{7,6},{8,9},{9,8},{10,11... | collective-permute-start | bytes 3932168 | tf_op jit(solution)/shard_map/ppermute | solution.py:284
  81.1 14.5 %collective-permute-start.17 = (f32[2560,128]{1,0:T(8,128)}, f32[2560,128]{1,0:T(8,128)}, u32[]{:S(2)}, u32[]{:S(2)}) collective-permute-start(f32[2560,128]{1,0:T(8,128)} %get-tuple-element.38), channel_id=1, source_target_pairs={{0,1},{1,0},{2,3},{3,2},{4,5},{5,4},{6,7},{7,6},{8,9},{9,8},{10,11... | collective-permute-start | bytes 3932168 | tf_op jit(solution)/shard_map/ppermute | solution.py:284
  95.5 38.3 %collective-permute-start.28 = (bf16[4,160,1280]{2,1,0:T(8,128)(2,1)}, bf16[4,160,1280]{2,1,0:T(8,128)(2,1)}, u32[]{:S(2)}, u32[]{:S(2)}) collective-permute-start(bf16[4,160,1280]{2,1,0:T(8,128)(2,1)} %copy-done.17), channel_id=1, source_target_pairs={{0,1},{1,0},{2,3},{3,2},{4,5},{5,4},{6,7},{7,6},{8,9},{9,8},{10,11... | collective-permute-start | bytes 4915208 | tf_op jit(solution)/shard_map/ppermute | solution.py:284
  118.6 13.6 %collective-permute-start.21 = (bf16[160,1280]{1,0:T(8,128)(2,1)S(1)}, bf16[160,1280]{1,0:T(8,128)(2,1)S(1)}, u32[]{:S(2)}, u32[]{:S(2)}) collective-permute-start(bf16[160,1280]{1,0:T(8,128)(2,1)S(1)} %hop_sum.6), channel_id=1, source_target_pairs={{0,32},{32,64},{64,96},{96,128},{128,160},{160,192},{192,224},{224... | collective-permute-start | bytes 1228808 | tf_op jit(solution)/shard_map/ppermute | solution.py:317
  118.7 13.2 %collective-permute-start.25 = (bf16[160,1280]{1,0:T(8,128)(2,1)S(1)}, bf16[160,1280]{1,0:T(8,128)(2,1)S(1)}, u32[]{:S(2)}, u32[]{:S(2)}) collective-permute-start(bf16[160,1280]{1,0:T(8,128)(2,1)S(1)} %hop_sum.9), channel_id=1, source_target_pairs={{0,224},{32,0},{64,32},{96,64},{128,96},{160,128},{192,160},{224,1... | collective-permute-start | bytes 1228808 | tf_op jit(solution)/shard_map/ppermute | solution.py:318
  121.6 41.2 %collective-permute-start.30 = (f32[16,1024]{1,0:T(8,128)S(1)}, f32[16,1024]{1,0:T(8,128)S(1)}, u32[]{:S(2)}, u32[]{:S(2)}) collective-permute-start(f32[16,1024]{1,0:T(8,128)S(1)} %pad_maximum_fusion), channel_id=1, source_target_pairs={{0,1},{1,0},{2,3},{3,2},{4,5},{5,4},{6,7},{7,6},{8,9},{9,8},{10,11... | collective-permute-start | bytes 196616 | tf_op jit(solution)/shard_map/ppermute | solution.py:284
  132.1 16.0 %collective-permute-start.26 = (bf16[160,1280]{1,0:T(8,128)(2,1)S(1)}, bf16[160,1280]{1,0:T(8,128)(2,1)S(1)}, u32[]{:S(2)}, u32[]{:S(2)}) collective-permute-start(bf16[160,1280]{1,0:T(8,128)(2,1)S(1)} %hop_sum.10), channel_id=1, source_target_pairs={{0,224},{32,0},{64,32},{96,64},{128,96},{160,128},{192,160},{224,1... | collective-permute-start | bytes 1228808 | tf_op jit(solution)/shard_map/ppermute | solution.py:318
  132.3 18.0 %collective-permute-start.22 = (bf16[160,1280]{1,0:T(8,128)(2,1)S(1)}, bf16[160,1280]{1,0:T(8,128)(2,1)S(1)}, u32[]{:S(2)}, u32[]{:S(2)}) collective-permute-start(bf16[160,1280]{1,0:T(8,128)(2,1)S(1)} %hop_sum.7), channel_id=1, source_target_pairs={{0,32},{32,64},{64,96},{96,128},{128,160},{160,192},{192,224},{224... | collective-permute-start | bytes 1228808 | tf_op jit(solution)/shard_map/ppermute | solution.py:317
  149.0 15.1 %collective-permute-start.27 = (bf16[160,1280]{1,0:T(8,128)(2,1)}, bf16[160,1280]{1,0:T(8,128)(2,1)}, u32[]{:S(2)}, u32[]{:S(2)}) collective-permute-start(bf16[160,1280]{1,0:T(8,128)(2,1)} %hop_sum.11), channel_id=1, source_target_pairs={{0,224},{32,0},{64,32},{96,64},{128,96},{160,128},{192,160},{224,1... | collective-permute-start | bytes 1228808 | tf_op jit(solution)/shard_map/ppermute | solution.py:318
  (33 other events, 240.5 us)
Sparse Core Ops, SparseCore 0:
  9.8 50.0 all-gather.2

commit v4 on v3

--- a/solution.py
+++ b/solution.py
@@ -210,7 +210,8 @@
     )(place, blocks, *rows, *after)
 
 
-def hop_kernel(which, fresh, terms_ref, come_ref, out_ref):
+def hop_kernel(which, fresh, terms_ref, come_ref, *refs):
+    out_ref = refs[-1]
     term, come = terms_ref[which], come_ref[...].astype(F32)
     if fresh is None:
         out_ref[...] = (term + come).astype(BF16)
@@ -220,17 +221,17 @@
     out_ref[fresh:fresh + HALF, :] = term[fresh:fresh + HALF].astype(BF16)
 
 
-def hop(which, fresh, terms, come):
+def hop(which, fresh, terms, come, after=()):
     vmem = pl.BlockSpec(memory_space=pltpu.VMEM)
     return pl.pallas_call(
         functools.partial(hop_kernel, which, fresh),
         out_shape=jax.ShapeDtypeStruct((HID, BLOCK), BF16),
-        in_specs=[vmem] * 2,
+        in_specs=[vmem] * 2 + [pl.BlockSpec(memory_space=pl.ANY)] * len(after),
         out_specs=vmem,
         compiler_params=pltpu.CompilerParams(vmem_limit_bytes=4 * 2**20),
         cost_estimate=pl.CostEstimate(flops=0, bytes_accessed=1_500_000, transcendentals=0),
         name="hop_sum",
-    )(terms, come)
+    )(terms, come, *after)
 
 
 def weight_kernel(first, mine_ref, theirs_ref, *refs):
@@ -313,20 +314,20 @@
         return to_slot_order(place, (tile + jnp.array(steps, jnp.int32)) % N_TILE, rows, after, keep)
 
     rows, across = slots([4], parts, [], keep=True)
-    (third,) = slots([3, 5], [rows], [across])
+    (middle,) = slots([3, 5, 2, 6], [rows], [across])
     up = lambda value: lax.ppermute(value.astype(BF16), "tile", TILE_UP)
     down = lambda value: lax.ppermute(value.astype(BF16), "tile", TILE_DOWN)
     rise, fall = up(across[0, :HALF]), down(across[0, HALF:])
-    (second,) = slots([2, 6], parts, [rise])
-    rise, fall = up(hop(0, HALF, third, rise)), down(hop(1, 0, third, fall))
     (nearest,) = slots([1, 7, 0], parts, [rise])
-    rise, fall = up(hop(0, None, second, rise)), down(hop(1, None, second, fall))
-    arrived = rise
+    rise, fall = up(hop(0, HALF, middle, rise)), down(hop(1, 0, middle, fall))
+    arrived = [rise]
+    totals = weight_term(act_mine[0], act_theirs[0], groups[0], [], [])
+    rise, fall = up(hop(2, None, middle, rise, totals[:1])), down(hop(3, None, middle, fall))
+    arrived.append(rise)
     rise, fall = up(hop(0, None, nearest, rise)), down(hop(1, None, nearest, fall))
     grad_pre = (nearest[2] + rise.astype(F32) + fall.astype(F32)) * lax.optimization_barrier(slope)
-    totals = []
-    for g in range(GROUPS):
-        totals = weight_term(act_mine[g], act_theirs[g], groups[g], totals, [arrived] if g == 1 else [])
+    for g in range(1, GROUPS):
+        totals = weight_term(act_mine[g], act_theirs[g], groups[g], totals, arrived[1:] if g == 1 else [])
     grad_w = totals[0] + swap(totals[1])
     sums = jnp.concatenate(sums, axis=0)
     sums = jnp.concatenate([sums, swap(sums)], axis=0)

time: 176 us -> 177 us (level)
  Pallas kernels: 72.5 us -> 70.2 us
  local copies, waits for them, and re-layouts: 9.93 us -> 12 us
    pallas_call x4 -> x3, Pallas kernels: 29.6 us -> 24.3 us  [to_slot_order(): pl.pallas_call(functools.partial(slot_kernel, count, not whole, keep), ou...]
    ppermute x4, starting transfers between devices: 9.81 us -> 13.9 us  [body(): down = lambda value: lax.ppermute(value.astype(BF16), 'tile', TILE_DOWN)]
    ppermute x8, starting transfers between devices: 9.98 us -> 7.16 us  [body(): swap = lambda value: lax.ppermute(value, 'text', SWAP)]
    unnamed x51 -> x57, local copies, waits for them, and re-layouts: 7.62 us -> 7.38 us
  transfers between devices with their start and end apart: 32 -> 32, of which waited for: 6 -> 6; matrix products, arithmetic and copies ran while one was open for 3% -> 4% of each run, Pallas kernels for 41% -> 40%
where the time goes in v4:
time: 177 us
  Pallas kernels  70.2 us (40%)
  starting transfers between devices  38.7 us (22%)
  waiting for transfers between devices  33.6 us (19%)
  between operations  14.5 us (8%)
  local copies, waits for them, and re-layouts  12 us (7%)
  other arithmetic  7.66 us (4%)
    ppermute x15, waiting for transfers between devices, body(): send = lambda value, perm: lax.ppermute(value, 'text', perm)  26.1 us
    pallas_call x3, Pallas kernels, to_slot_order(): pl.pallas_call(functools.partial(slot_kernel, count, not whole, keep), ou...  24.3 us
    ppermute x15, starting transfers between devices, body(): send = lambda value, perm: lax.ppermute(value, 'text', perm)  17.4 us
    pallas_call x4, Pallas kernels, products_of(): pl.pallas_call(functools.partial(product_kernel, hand_on), out_shape=out...  16.8 us
    pallas_call x1, Pallas kernels, act_in_arrival_order(): pl.pallas_call(act_kernel, out_shape=[jax.ShapeDtypeStruct((GROUPS, HID,...  15.3 us
    ppermute x4, starting transfers between devices, body(): down = lambda value: lax.ppermute(value.astype(BF16), 'tile', TILE_DOWN)  13.9 us
    pallas_call x4, Pallas kernels, weight_term(): pl.pallas_call(functools.partial(weight_kernel, not totals), out_shape=[j...  11.7 us
    unnamed x57, local copies, waits for them, and re-layouts  7.38 us
  transfers between devices with their start and end apart: 32, of which 6 were waited for; matrix products, arithmetic and copies ran while one was open for 4% of the time, Pallas kernels for 40%

profile of v4, /device:TPU:1, one launch (start us, length us, event | category | flops | bytes accessed | tf_op | source)
XLA Modules:
  0.0 176.7 jit_solution(17100695850960558071)
XLA Ops:
  16.3 9.5 %collective-permute-done.1.refs_1_ = bf16[320,1024]{1,0:T(8,128)(2,1)} collective-permute-done((bf16[320,1024]{1,0:T(8,128)(2,1)S(1)}, bf16[320,1024]{1,0:T(8,128)(2,1)}, u32[]{:S(2)}, u32[]{:S(2)}) %collective-permute-start.1) | collective-permute-done | bytes 655392 | tf_op jit(solution)/shard_map/ppermute | solution.py:286
  26.1 3.3 %collective-permute-start.4 = (bf16[320,1024]{1,0:T(8,128)(2,1)S(1)}, bf16[320,1024]{1,0:T(8,128)(2,1)S(1)}, u32[]{:S(2)}, u32[]{:S(2)}) collective-permute-start(bf16[320,1024]{1,0:T(8,128)(2,1)S(1)} %copy-done.20), channel_id=1, source_target_pairs={{0,24},{1,7},{2,26},{3,1},{4,28},{5,3},{6,30},{7,5},{8,0},{9,15},{... | collective-permute-start | bytes 1966088 | tf_op jit(solution)/shard_map/ppermute | solution.py:286
  29.6 4.3 %products.4 = (f32[2560,128]{1,0:T(8,128)S(1)}, f32[2560,128]{1,0:T(8,128)}, f32[4,1024]{1,0:T(4,128)S(1)}, bf16[320,1024]{1,0:T(8,128)(2,1)}) custom-call(bf16[320,1024]{1,0:T(8,128)(2,1)S(1)} %constant_dynamic-update-slice_fusion.weight_ref, bf16[320,1024]{1,0:T(8,128)(2,1)S(1)} %copy-done.20, bf16[320,1024]{1,0:T(8,128)(2,1)} %collective-permute-done.1.refs_1_, ...), custom_call_target="tpu_custom_call" | custom-call | flops 1300000000 | bytes 8000000 | tf_op jit(solution)/shard_map/products/pallas_call | solution.py:145
  35.2 2.5 %collective-permute-start.9 = (bf16[320,1024]{1,0:T(8,128)(2,1)}, bf16[320,1024]{1,0:T(8,128)(2,1)}, u32[]{:S(2)}, u32[]{:S(2)}) collective-permute-start(bf16[320,1024]{1,0:T(8,128)(2,1)} %collective-permute-done.2.refs_2_), channel_id=1, source_target_pairs={{0,24},{1,7},{2,26},{3,1},{4,28},{5,3},{6,30},{7,5},{8,0},{9,15},{... | collective-permute-start | bytes 1966088 | tf_op jit(solution)/shard_map/ppermute | solution.py:286
  39.7 6.8 %collective-permute-done.5.refs_1_ = bf16[320,1024]{1,0:T(8,128)(2,1)S(1)} collective-permute-done((bf16[320,1024]{1,0:T(8,128)(2,1)}, bf16[320,1024]{1,0:T(8,128)(2,1)S(1)}, u32[]{:S(2)}, u32[]{:S(2)}) %collective-permute-start.5) | collective-permute-done | bytes 655392 | tf_op jit(solution)/shard_map/ppermute | solution.py:286
  46.6 8.3 %collective-permute-done.7.refs_3_ = bf16[320,1024]{1,0:T(8,128)(2,1)} collective-permute-done((bf16[320,1024]{1,0:T(8,128)(2,1)}, bf16[320,1024]{1,0:T(8,128)(2,1)}, u32[]{:S(2)}, u32[]{:S(2)}) %collective-permute-start.7) | collective-permute-done | bytes 655392 | tf_op jit(solution)/shard_map/ppermute | solution.py:286
  56.0 3.7 %products.5 = (f32[2560,128]{1,0:T(8,128)S(1)}, f32[2560,128]{1,0:T(8,128)}, f32[4,1024]{1,0:T(4,128)S(1)}, bf16[320,1024]{1,0:T(8,128)(2,1)}) custom-call(bf16[320,1024]{1,0:T(8,128)(2,1)S(1)} %copy-done.16, bf16[320,1024]{1,0:T(8,128)(2,1)S(1)} %collective-permute-done.4.refs_0_, bf16[320,1024]{1,0:T(8,128)(2,1)S(1)} %collective-permute-done.5.refs_1_, ...), custom_call_target="tpu_custom_call" | custom-call | flops 1300000000 | bytes 8000000 | tf_op jit(solution)/shard_map/products/pallas_call | solution.py:145
  60.8 2.8 %collective-permute-start.15 = (bf16[320,1024]{1,0:T(8,128)(2,1)}, bf16[320,1024]{1,0:T(8,128)(2,1)}, u32[]{:S(2)}, u32[]{:S(2)}) collective-permute-start(bf16[320,1024]{1,0:T(8,128)(2,1)} %collective-permute-done.12.refs_0_), channel_id=1, source_target_pairs={{0,24},{1,7},{2,26},{3,1},{4,28},{5,3},{6,30},{7,5},{8,0},{9,15},{... | collective-permute-start | bytes 1966088 | tf_op jit(solution)/shard_map/ppermute | solution.py:286
  65.5 15.3 %act_rows.1 = (bf16[4,160,1280]{2,1,0:T(8,128)(2,1)S(1)}, bf16[4,160,1280]{2,1,0:T(8,128)(2,1)}, bf16[320,1024]{1,0:T(8,128)(2,1)S(1)}) custom-call(s32[10240]{0:T(1024)S(1)} %fusion.13.place_ref, bf16[8,160,1280]{2,1,0:T(8,128)(2,1)S(1)} %bitcast.52, bf16[320,1024]{1,0:T(8,128)(2,1)} %collective-permute-done.9.refs_1_.piece_ref), custom_call_target="tpu_custom_call" | custom-call | bytes 70000000 | tf_op jit(solution)/shard_map/act_rows/pallas_call | solution.py:98
  83.3 4.4 %products.6 = (f32[2560,128]{1,0:T(8,128)S(1)}, f32[2560,128]{1,0:T(8,128)}, f32[4,1024]{1,0:T(4,128)S(1)}) custom-call(bf16[320,1024]{1,0:T(8,128)(2,1)S(1)} %copy-done.17, bf16[320,1024]{1,0:T(8,128)(2,1)} %collective-permute-done.8.refs_0_, bf16[320,1024]{1,0:T(8,128)(2,1)} %collective-permute-done.9.refs_1_.piece_ref, ...), custom_call_target="tpu_custom_call" | custom-call | flops 1300000000 | bytes 8000000 | tf_op jit(solution)/shard_map/products/pallas_call | solution.py:145
  90.6 4.4 %products.7 = (f32[2560,128]{1,0:T(8,128)S(1)}, f32[2560,128]{1,0:T(8,128)}, f32[4,1024]{1,0:T(4,128)S(1)}) custom-call(bf16[320,1024]{1,0:T(8,128)(2,1)S(1)} %copy-done.17, bf16[320,1024]{1,0:T(8,128)(2,1)} %collective-permute-done.12.refs_0_, bf16[320,1024]{1,0:T(8,128)(2,1)} %collective-permute-done.13.refs_1_, ...), custom_call_target="tpu_custom_call" | custom-call | flops 1300000000 | bytes 8000000 | tf_op jit(solution)/shard_map/products/pallas_call | solution.py:145
  97.4 3.0 %collective-permute-done.19.refs_7_ = f32[2560,128]{1,0:T(8,128)} collective-permute-done((f32[2560,128]{1,0:T(8,128)}, f32[2560,128]{1,0:T(8,128)}, u32[]{:S(2)}, u32[]{:S(2)}) %collective-permute-start.19) | collective-permute-done | bytes 1310752 | tf_op jit(solution)/shard_map/ppermute | solution.py:285
  100.3 7.0 %slot_rows.3 = (f32[20480,128]{1,0:T(8,128)S(1)}, f32[1,160,1280]{2,1,0:T(8,128)S(1)}) custom-call(s32[10240]{0:T(1024)} %copy-done.6, s32[1]{0:T(128)S(6)} %select_n.118.blocks_ref, f32[2560,128]{1,0:T(8,128)} %copy-done, f32[2560,128]{1,0:T(8,128)} %copy-done.2, f32[2560,128]{1,0:T(8,128)} %copy-done.3, f32[2560,128]{1,0:T(8,128)} %copy-done.4, ...), custom_call_target="tpu_custom_call" | custom-call | bytes 8000000 | tf_op jit(solution)/shard_map/slot_rows/pallas_call | solution.py:199
  107.4 5.7 %collective-permute-start.25 = (bf16[80,1280]{1,0:T(8,128)(2,1)S(1)}, bf16[80,1280]{1,0:T(8,128)(2,1)S(1)}, u32[]{:S(2)}, u32[]{:S(2)}) collective-permute-start(bf16[80,1280]{1,0:T(8,128)(2,1)S(1)} %get-tuple-element.65), channel_id=1, source_target_pairs={{0,224},{32,0},{64,32},{96,64},{128,96},{160,128},{192,160},{224,1... | collective-permute-start | bytes 614408 | tf_op jit(solution)/shard_map/ppermute | solution.py:319
  114.0 7.6 %slot_rows.5.terms_ref = f32[4,160,1280]{2,1,0:T(8,128)S(1)} custom-call(s32[10240]{0:T(1024)S(1)} %copy-done.7, s32[4]{0:T(128)S(1)} %and_select_fusion.blocks_ref, f32[20480,128]{1,0:T(8,128)S(1)} %get-tuple-element.42.refs_0_, f32[1,160,1280]{2,1,0:T(8,128)S(1)} %get-tuple-element.41.refs_1_), custom_call_target="tpu_custom_call" | custom-call | bytes 32000000 | tf_op jit(solution)/shard_map/slot_rows/pallas_call | solution.py:199
  121.8 2.7 %collective-permute-start.26 = (bf16[160,1280]{1,0:T(8,128)(2,1)S(1)}, bf16[160,1280]{1,0:T(8,128)(2,1)S(1)}, u32[]{:S(2)}, u32[]{:S(2)}) collective-permute-start(bf16[160,1280]{1,0:T(8,128)(2,1)S(1)} %hop_sum.9), channel_id=1, source_target_pairs={{0,224},{32,0},{64,32},{96,64},{128,96},{160,128},{192,160},{224,1... | collective-permute-start | bytes 1228808 | tf_op jit(solution)/shard_map/ppermute | solution.py:319
  126.1 2.7 %weight_term.4 = (f32[160,1024]{1,0:T(8,128)S(1)}, f32[160,1024]{1,0:T(8,128)S(1)}) custom-call(bf16[160,1280]{1,0:T(8,128)(2,1)S(1)} %get-tuple-element.64.mine_ref, bf16[160,1280]{1,0:T(8,128)(2,1)S(1)} %get-tuple-element.60.theirs_ref, bf16[320,1024]{1,0:T(8,128)(2,1)S(1)} %copy-done.21, bf16[320,1024]{1,0:T(8,128)(2,1)} %collective-permute-done.1.refs_1_, ...), custom_call_target="tpu_custom_call" | custom-call | flops 1300000000 | bytes 8000000 | tf_op jit(solution)/shard_map/weight_term/pallas_call | solution.py:257
  128.8 4.5 %collective-permute-done.21.come_ref = bf16[160,1280]{1,0:T(8,128)(2,1)S(1)} collective-permute-done((bf16[160,1280]{1,0:T(8,128)(2,1)S(1)}, bf16[160,1280]{1,0:T(8,128)(2,1)S(1)}, u32[]{:S(2)}, u32[]{:S(2)}) %collective-permute-start.21) | collective-permute-done | bytes 409632 | tf_op jit(solution)/shard_map/ppermute | solution.py:318
  133.6 2.7 %collective-permute-start.27 = (bf16[160,1280]{1,0:T(8,128)(2,1)S(1)}, bf16[160,1280]{1,0:T(8,128)(2,1)S(1)}, u32[]{:S(2)}, u32[]{:S(2)}) collective-permute-start(bf16[160,1280]{1,0:T(8,128)(2,1)S(1)} %hop_sum.10), channel_id=1, source_target_pairs={{0,224},{32,0},{64,32},{96,64},{128,96},{160,128},{192,160},{224,1... | collective-permute-start | bytes 1228808 | tf_op jit(solution)/shard_map/ppermute | solution.py:319
  138.6 9.8 %slot_rows.4.terms_ref = f32[3,160,1280]{2,1,0:T(8,128)S(1)} custom-call(s32[10240]{0:T(1024)S(1)} %copy-done.7, s32[3]{0:T(128)S(1)} %and_select_fusion.1.blocks_ref, f32[2560,128]{1,0:T(8,128)S(1)} %copy-done.1, f32[2560,128]{1,0:T(8,128)} %copy-done.2, f32[2560,128]{1,0:T(8,128)} %copy-done.3, f32[2560,128]{1,0:T(8,128)} %copy-done.4, ...), custom_call_target="tpu_custom_call" | custom-call | bytes 24000000 | tf_op jit(solution)/shard_map/slot_rows/pallas_call | solution.py:199
  150.2 2.7 %collective-permute-start.28 = (bf16[160,1280]{1,0:T(8,128)(2,1)}, bf16[160,1280]{1,0:T(8,128)(2,1)}, u32[]{:S(2)}, u32[]{:S(2)}) collective-permute-start(bf16[160,1280]{1,0:T(8,128)(2,1)} %hop_sum.11), channel_id=1, source_target_pairs={{0,224},{32,0},{64,32},{96,64},{128,96},{160,128},{192,160},{224,1... | collective-permute-start | bytes 1228808 | tf_op jit(solution)/shard_map/ppermute | solution.py:319
  152.8 2.8 %weight_term.5 = (f32[160,1024]{1,0:T(8,128)S(1)}, f32[160,1024]{1,0:T(8,128)S(1)}) custom-call(bf16[160,1280]{1,0:T(8,128)(2,1)S(1)} %get-tuple-element.61.mine_ref, bf16[160,1280]{1,0:T(8,128)(2,1)S(1)} %get-tuple-element.57.theirs_ref, bf16[320,1024]{1,0:T(8,128)(2,1)S(1)} %copy-done.11, bf16[320,1024]{1,0:T(8,128)(2,1)S(1)} %copy-done.13, ...), custom_call_target="tpu_custom_call" | custom-call | flops 1300000000 | bytes 8000000 | tf_op jit(solution)/shard_map/weight_term/pallas_call | solution.py:257
  155.6 2.8 %weight_term.6 = (f32[160,1024]{1,0:T(8,128)S(1)}, f32[160,1024]{1,0:T(8,128)S(1)}) custom-call(bf16[160,1280]{1,0:T(8,128)(2,1)S(1)} %copy-done.14, bf16[160,1280]{1,0:T(8,128)(2,1)S(1)} %get-tuple-element.58.theirs_ref, bf16[320,1024]{1,0:T(8,128)(2,1)} %collective-permute-done.8.refs_0_, bf16[320,1024]{1,0:T(8,128)(2,1)} %collective-permute-done.9.refs_1_.piece_ref, ...), custom_call_target="tpu_custom_call" | custom-call | flops 1300000000 | bytes 8000000 | tf_op jit(solution)/shard_map/weight_term/pallas_call | solution.py:257
  158.5 3.4 %weight_term.7 = (f32[160,1024]{1,0:T(8,128)S(1)}, f32[160,1024]{1,0:T(8,128)}) custom-call(bf16[160,1280]{1,0:T(8,128)(2,1)S(1)} %get-tuple-element.63.mine_ref, bf16[160,1280]{1,0:T(8,128)(2,1)S(1)} %get-tuple-element.59.theirs_ref, bf16[320,1024]{1,0:T(8,128)(2,1)} %collective-permute-done.12.refs_0_, bf16[320,1024]{1,0:T(8,128)(2,1)} %collective-permute-done.13.refs_1_, ...), custom_call_target="tpu_custom_call" | custom-call | flops 1300000000 | bytes 8000000 | tf_op jit(solution)/shard_map/weight_term/pallas_call | solution.py:257
  (133 shorter events, 39.4 us)
Async XLA Ops:
  7.2 56.4 %all-gather.3.cloned.1.call-start = ((), (), s32[]{:S(2)}) async-start(), calls=%async_computation | async-start | bytes 3686400 | tf_op jit(solution)/shard_map/all_gather | solution.py:284
  9.7 16.1 %collective-permute-start.1 = (bf16[320,1024]{1,0:T(8,128)(2,1)S(1)}, bf16[320,1024]{1,0:T(8,128)(2,1)}, u32[]{:S(2)}, u32[]{:S(2)}) collective-permute-start(bf16[320,1024]{1,0:T(8,128)(2,1)S(1)} %copy-done.20), channel_id=1, source_target_pairs={{0,2},{1,9},{2,4},{3,11},{4,6},{5,13},{6,0},{7,15},{8,10},{9,17},{... | collective-permute-start | bytes 1966088 | tf_op jit(solution)/shard_map/ppermute | solution.py:286
  11.9 17.7 %collective-permute-start.3 = (bf16[320,1024]{1,0:T(8,128)(2,1)S(1)}, bf16[320,1024]{1,0:T(8,128)(2,1)}, u32[]{:S(2)}, u32[]{:S(2)}) collective-permute-start(bf16[320,1024]{1,0:T(8,128)(2,1)S(1)} %copy-done.20), channel_id=1, source_target_pairs={{0,8},{1,3},{2,10},{3,5},{4,12},{5,7},{6,14},{7,1},{8,16},{9,11},{... | collective-permute-start | bytes 1966088 | tf_op jit(solution)/shard_map/ppermute | solution.py:286
  13.1 16.5 %collective-permute-start.2 = (bf16[320,1024]{1,0:T(8,128)(2,1)S(1)}, bf16[320,1024]{1,0:T(8,128)(2,1)}, u32[]{:S(2)}, u32[]{:S(2)}) collective-permute-start(bf16[320,1024]{1,0:T(8,128)(2,1)S(1)} %copy-done.20), channel_id=1, source_target_pairs={{0,6},{1,25},{2,0},{3,27},{4,2},{5,29},{6,4},{7,31},{8,14},{9,1},{... | collective-permute-start | bytes 1966088 | tf_op jit(solution)/shard_map/ppermute | solution.py:286
  14.7 14.8 %collective-permute-start = (bf16[160,1024]{1,0:T(8,128)(2,1)S(1)}, bf16[160,1024]{1,0:T(8,128)(2,1)S(1)}, u32[]{:S(2)}, u32[]{:S(2)}) collective-permute-start(bf16[160,1024]{1,0:T(8,128)(2,1)S(1)} %copy-done.24), channel_id=1, source_target_pairs={{0,1},{1,0},{2,3},{3,2},{4,5},{5,4},{6,7},{7,6},{8,9},{9,8},{10,11... | collective-permute-start | bytes 983048 | tf_op jit(solution)/shard_map/ppermute | solution.py:285
  26.1 13.5 %collective-permute-start.4 = (bf16[320,1024]{1,0:T(8,128)(2,1)S(1)}, bf16[320,1024]{1,0:T(8,128)(2,1)S(1)}, u32[]{:S(2)}, u32[]{:S(2)}) collective-permute-start(bf16[320,1024]{1,0:T(8,128)(2,1)S(1)} %copy-done.20), channel_id=1, source_target_pairs={{0,24},{1,7},{2,26},{3,1},{4,28},{5,3},{6,30},{7,5},{8,0},{9,15},{... | collective-permute-start | bytes 1966088 | tf_op jit(solution)/shard_map/ppermute | solution.py:286
  29.5 17.1 %collective-permute-start.5 = (bf16[320,1024]{1,0:T(8,128)(2,1)}, bf16[320,1024]{1,0:T(8,128)(2,1)S(1)}, u32[]{:S(2)}, u32[]{:S(2)}) collective-permute-start(bf16[320,1024]{1,0:T(8,128)(2,1)} %collective-permute-done.1.refs_1_), channel_id=1, source_target_pairs={{0,8},{1,3},{2,10},{3,5},{4,12},{5,7},{6,14},{7,1},{8,16},{9,11},{... | collective-permute-start | bytes 1966088 | tf_op jit(solution)/shard_map/ppermute | solution.py:286
  35.0 19.9 %collective-permute-start.7 = (bf16[320,1024]{1,0:T(8,128)(2,1)}, bf16[320,1024]{1,0:T(8,128)(2,1)}, u32[]{:S(2)}, u32[]{:S(2)}) collective-permute-start(bf16[320,1024]{1,0:T(8,128)(2,1)} %get-tuple-element.31), channel_id=1, source_target_pairs={{0,8},{1,3},{2,10},{3,5},{4,12},{5,7},{6,14},{7,1},{8,16},{9,11},{... | collective-permute-start | bytes 1966088 | tf_op jit(solution)/shard_map/ppermute | solution.py:286
  35.2 25.7 %collective-permute-start.9 = (bf16[320,1024]{1,0:T(8,128)(2,1)}, bf16[320,1024]{1,0:T(8,128)(2,1)}, u32[]{:S(2)}, u32[]{:S(2)}) collective-permute-start(bf16[320,1024]{1,0:T(8,128)(2,1)} %collective-permute-done.2.refs_2_), channel_id=1, source_target_pairs={{0,24},{1,7},{2,26},{3,1},{4,28},{5,3},{6,30},{7,5},{8,0},{9,15},{... | collective-permute-start | bytes 1966088 | tf_op jit(solution)/shard_map/ppermute | solution.py:286
  37.7 23.1 %collective-permute-start.12 = (bf16[320,1024]{1,0:T(8,128)(2,1)S(1)}, bf16[320,1024]{1,0:T(8,128)(2,1)}, u32[]{:S(2)}, u32[]{:S(2)}) collective-permute-start(bf16[320,1024]{1,0:T(8,128)(2,1)S(1)} %collective-permute-done.6.refs_2_), channel_id=1, source_target_pairs={{0,24},{1,7},{2,26},{3,1},{4,28},{5,3},{6,30},{7,5},{8,0},{9,15},{... | collective-permute-start | bytes 1966088 | tf_op jit(solution)/shard_map/ppermute | solution.py:286
  39.6 41.2 %collective-permute-start.10 = (bf16[320,1024]{1,0:T(8,128)(2,1)}, bf16[320,1024]{1,0:T(8,128)(2,1)}, u32[]{:S(2)}, u32[]{:S(2)}) collective-permute-start(bf16[320,1024]{1,0:T(8,128)(2,1)} %collective-permute-done.3.refs_3_), channel_id=1, source_target_pairs={{0,8},{1,3},{2,10},{3,5},{4,12},{5,7},{6,14},{7,1},{8,16},{9,11},{... | collective-permute-start | bytes 1966088 | tf_op jit(solution)/shard_map/ppermute | solution.py:286
  46.6 35.7 %collective-permute-start.8 = (bf16[320,1024]{1,0:T(8,128)(2,1)}, bf16[320,1024]{1,0:T(8,128)(2,1)}, u32[]{:S(2)}, u32[]{:S(2)}) collective-permute-start(bf16[320,1024]{1,0:T(8,128)(2,1)} %collective-permute-done.1.refs_1_), channel_id=1, source_target_pairs={{0,24},{1,7},{2,26},{3,1},{4,28},{5,3},{6,30},{7,5},{8,0},{9,15},{... | collective-permute-start | bytes 1966088 | tf_op jit(solution)/shard_map/ppermute | solution.py:286
  54.9 28.3 %collective-permute-start.11 = (bf16[320,1024]{1,0:T(8,128)(2,1)S(1)}, bf16[320,1024]{1,0:T(8,128)(2,1)}, u32[]{:S(2)}, u32[]{:S(2)}) collective-permute-start(bf16[320,1024]{1,0:T(8,128)(2,1)S(1)} %collective-permute-done.6.refs_2_), channel_id=1, source_target_pairs={{0,8},{1,3},{2,10},{3,5},{4,12},{5,7},{6,14},{7,1},{8,16},{9,11},{... | collective-permute-start | bytes 1966088 | tf_op jit(solution)/shard_map/ppermute | solution.py:286
  60.8 27.9 %collective-permute-start.13 = (bf16[320,1024]{1,0:T(8,128)(2,1)}, bf16[320,1024]{1,0:T(8,128)(2,1)}, u32[]{:S(2)}, u32[]{:S(2)}) collective-permute-start(bf16[320,1024]{1,0:T(8,128)(2,1)} %get-tuple-element.34), channel_id=1, source_target_pairs={{0,8},{1,3},{2,10},{3,5},{4,12},{5,7},{6,14},{7,1},{8,16},{9,11},{... | collective-permute-start | bytes 1966088 | tf_op jit(solution)/shard_map/ppermute | solution.py:286
  60.8 28.4 %collective-permute-start.15 = (bf16[320,1024]{1,0:T(8,128)(2,1)}, bf16[320,1024]{1,0:T(8,128)(2,1)}, u32[]{:S(2)}, u32[]{:S(2)}) collective-permute-start(bf16[320,1024]{1,0:T(8,128)(2,1)} %collective-permute-done.12.refs_0_), channel_id=1, source_target_pairs={{0,24},{1,7},{2,26},{3,1},{4,28},{5,3},{6,30},{7,5},{8,0},{9,15},{... | collective-permute-start | bytes 1966088 | tf_op jit(solution)/shard_map/ppermute | solution.py:286
  82.3 15.0 %collective-permute-start.16 = (f32[2560,128]{1,0:T(8,128)}, f32[2560,128]{1,0:T(8,128)}, u32[]{:S(2)}, u32[]{:S(2)}) collective-permute-start(f32[2560,128]{1,0:T(8,128)} %get-tuple-element.37), channel_id=1, source_target_pairs={{0,1},{1,0},{2,3},{3,2},{4,5},{5,4},{6,7},{7,6},{8,9},{9,8},{10,11... | collective-permute-start | bytes 3932168 | tf_op jit(solution)/shard_map/ppermute | solution.py:285
  83.2 14.1 %collective-permute-start.17 = (f32[2560,128]{1,0:T(8,128)}, f32[2560,128]{1,0:T(8,128)}, u32[]{:S(2)}, u32[]{:S(2)}) collective-permute-start(f32[2560,128]{1,0:T(8,128)} %get-tuple-element.38), channel_id=1, source_target_pairs={{0,1},{1,0},{2,3},{3,2},{4,5},{5,4},{6,7},{7,6},{8,9},{9,8},{10,11... | collective-permute-start | bytes 3932168 | tf_op jit(solution)/shard_map/ppermute | solution.py:285
  97.3 27.3 %collective-permute-start.22 = (bf16[4,160,1280]{2,1,0:T(8,128)(2,1)}, bf16[4,160,1280]{2,1,0:T(8,128)(2,1)}, u32[]{:S(2)}, u32[]{:S(2)}) collective-permute-start(bf16[4,160,1280]{2,1,0:T(8,128)(2,1)} %get-tuple-element.44), channel_id=1, source_target_pairs={{0,1},{1,0},{2,3},{3,2},{4,5},{5,4},{6,7},{7,6},{8,9},{9,8},{10,11... | collective-permute-start | bytes 4915208 | tf_op jit(solution)/shard_map/ppermute | solution.py:285
  107.4 14.3 %collective-permute-start.25 = (bf16[80,1280]{1,0:T(8,128)(2,1)S(1)}, bf16[80,1280]{1,0:T(8,128)(2,1)S(1)}, u32[]{:S(2)}, u32[]{:S(2)}) collective-permute-start(bf16[80,1280]{1,0:T(8,128)(2,1)S(1)} %get-tuple-element.65), channel_id=1, source_target_pairs={{0,224},{32,0},{64,32},{96,64},{128,96},{160,128},{192,160},{224,1... | collective-permute-start | bytes 614408 | tf_op jit(solution)/shard_map/ppermute | solution.py:319
  133.4 15.0 %collective-permute-start.23 = (bf16[160,1280]{1,0:T(8,128)(2,1)S(1)}, bf16[160,1280]{1,0:T(8,128)(2,1)S(1)}, u32[]{:S(2)}, u32[]{:S(2)}) collective-permute-start(bf16[160,1280]{1,0:T(8,128)(2,1)S(1)} %hop_sum.7), channel_id=1, source_target_pairs={{0,32},{32,64},{64,96},{96,128},{128,160},{160,192},{192,224},{224... | collective-permute-start | bytes 1228808 | tf_op jit(solution)/shard_map/ppermute | solution.py:318
  133.6 15.7 %collective-permute-start.27 = (bf16[160,1280]{1,0:T(8,128)(2,1)S(1)}, bf16[160,1280]{1,0:T(8,128)(2,1)S(1)}, u32[]{:S(2)}, u32[]{:S(2)}) collective-permute-start(bf16[160,1280]{1,0:T(8,128)(2,1)S(1)} %hop_sum.10), channel_id=1, source_target_pairs={{0,224},{32,0},{64,32},{96,64},{128,96},{160,128},{192,160},{224,1... | collective-permute-start | bytes 1228808 | tf_op jit(solution)/shard_map/ppermute | solution.py:319
  136.4 26.1 %collective-permute-start.30 = (f32[16,1024]{1,0:T(8,128)S(1)}, f32[16,1024]{1,0:T(8,128)}, u32[]{:S(2)}, u32[]{:S(2)}) collective-permute-start(f32[16,1024]{1,0:T(8,128)S(1)} %pad_maximum_fusion), channel_id=1, source_target_pairs={{0,1},{1,0},{2,3},{3,2},{4,5},{5,4},{6,7},{7,6},{8,9},{9,8},{10,11... | collective-permute-start | bytes 196616 | tf_op jit(solution)/shard_map/ppermute | solution.py:285
  149.3 16.2 %collective-permute-start.24 = (bf16[160,1280]{1,0:T(8,128)(2,1)}, bf16[160,1280]{1,0:T(8,128)(2,1)}, u32[]{:S(2)}, u32[]{:S(2)}) collective-permute-start(bf16[160,1280]{1,0:T(8,128)(2,1)} %hop_sum.8), channel_id=1, source_target_pairs={{0,32},{32,64},{64,96},{96,128},{128,160},{160,192},{192,224},{224... | collective-permute-start | bytes 1228808 | tf_op jit(solution)/shard_map/ppermute | solution.py:318
  150.2 15.3 %collective-permute-start.28 = (bf16[160,1280]{1,0:T(8,128)(2,1)}, bf16[160,1280]{1,0:T(8,128)(2,1)}, u32[]{:S(2)}, u32[]{:S(2)}) collective-permute-start(bf16[160,1280]{1,0:T(8,128)(2,1)} %hop_sum.11), channel_id=1, source_target_pairs={{0,224},{32,0},{64,32},{96,64},{128,96},{160,128},{192,160},{224,1... | collective-permute-start | bytes 1228808 | tf_op jit(solution)/shard_map/ppermute | solution.py:319
  (36 other events, 331.6 us)
Sparse Core Ops, SparseCore 0:
  9.8 50.0 all-gather.2

commit v5 on v4

--- a/solution.py
+++ b/solution.py
@@ -234,33 +234,37 @@
     )(terms, come, *after)
 
 
-def weight_kernel(first, mine_ref, theirs_ref, *refs):
+def weight_kernel(group, first, mine_ref, theirs_ref, *refs):
     pieces = refs[:4]
-    out_mine, out_theirs, held, sems = refs[-4:]
+    out_mine, out_theirs, act, held, sems = refs[-5:]
     copies = [
         pltpu.make_async_copy(piece, held.at[pl.ds(k * ROWS, ROWS), :], sems.at[k]) for k, piece in enumerate(pieces)
     ]
+    copies.append(pltpu.make_async_copy(mine_ref.at[group], act.at[pl.ds(0, HID), :], sems.at[4]))
+    copies.append(pltpu.make_async_copy(theirs_ref.at[group], act.at[pl.ds(HID, HID), :], sems.at[5]))
     for copy in copies:
         copy.start()
     for copy in copies:
         copy.wait()
-    act = jnp.concatenate([mine_ref[...], theirs_ref[...]], axis=0)
     for n in range(0, WIDTH, 256):
         columns = slice(n, n + 256)
-        term = jnp.dot(act, held[:, columns], preferred_element_type=F32)
+        term = jnp.dot(act[...], held[:, columns], preferred_element_type=F32)
         out_mine[:, columns] = term[:HID] if first else refs[4][:, columns] + term[:HID]
         out_theirs[:, columns] = term[HID:] if first else refs[5][:, columns] + term[HID:]
 
 
-def weight_term(mine, theirs, pieces, totals, after):
-    vmem = pl.BlockSpec(memory_space=pltpu.VMEM)
-    return pl.pallas_call(
-        functools.partial(weight_kernel, not totals),
+def weight_term(group, mine, theirs, pieces, totals, after):
+    vmem, anywhere = pl.BlockSpec(memory_space=pltpu.VMEM), pl.BlockSpec(memory_space=pl.ANY)
+    return pl.pallas_call(
+        functools.partial(weight_kernel, group, not totals),
         out_shape=[jax.ShapeDtypeStruct((HID, WIDTH), F32)] * 2,
-        in_specs=[vmem] * 2 + [pl.BlockSpec(memory_space=pl.ANY)] * 4 + [vmem] * len(totals)
-        + [pl.BlockSpec(memory_space=pl.ANY)] * len(after),
+        in_specs=[anywhere] * 6 + [vmem] * len(totals) + [anywhere] * len(after),
         out_specs=[vmem] * 2,
-        scratch_shapes=[pltpu.VMEM((GROUP_ROWS, WIDTH), BF16), pltpu.SemaphoreType.DMA((4,))],
+        scratch_shapes=[
+            pltpu.VMEM((2 * HID, GROUP_ROWS), BF16),
+            pltpu.VMEM((GROUP_ROWS, WIDTH), BF16),
+            pltpu.SemaphoreType.DMA((6,)),
+        ],
         compiler_params=pltpu.CompilerParams(vmem_limit_bytes=6 * 2**20),
         cost_estimate=pl.CostEstimate(flops=1_300_000_000, bytes_accessed=8_000_000, transcendentals=0),
         name="weight_term",
@@ -321,17 +325,18 @@
     (nearest,) = slots([1, 7, 0], parts, [rise])
     rise, fall = up(hop(0, HALF, middle, rise)), down(hop(1, 0, middle, fall))
     arrived = [rise]
-    totals = weight_term(act_mine[0], act_theirs[0], groups[0], [], [])
-    rise, fall = up(hop(2, None, middle, rise, totals[:1])), down(hop(3, None, middle, fall))
+    totals = weight_term(0, act_mine, act_theirs, groups[0], [], [])
+    totals = weight_term(1, act_mine, act_theirs, groups[1], totals, [])
+    sums = jnp.concatenate(sums, axis=0)
+    sums = jnp.concatenate([sums, swap(sums)], axis=0)
+    grad_bias = jnp.sum(sums[piece_of], axis=0)
+    rise, fall = up(hop(2, None, middle, rise, [totals[0], grad_bias])), down(hop(3, None, middle, fall))
     arrived.append(rise)
     rise, fall = up(hop(0, None, nearest, rise)), down(hop(1, None, nearest, fall))
     grad_pre = (nearest[2] + rise.astype(F32) + fall.astype(F32)) * lax.optimization_barrier(slope)
-    for g in range(1, GROUPS):
-        totals = weight_term(act_mine[g], act_theirs[g], groups[g], totals, arrived[1:] if g == 1 else [])
+    for g in range(2, GROUPS):
+        totals = weight_term(g, act_mine, act_theirs, groups[g], totals, arrived[1:] if g == 2 else [])
     grad_w = totals[0] + swap(totals[1])
-    sums = jnp.concatenate(sums, axis=0)
-    sums = jnp.concatenate([sums, swap(sums)], axis=0)
-    grad_bias = jnp.sum(sums[piece_of], axis=0)
     return grad_pre.T, grad_w, grad_bias
 
 

time: 177 us -> 181 us (1.023)
  local copies, waits for them, and re-layouts: 12 us -> 17 us
    unnamed x57 -> x87, local copies, waits for them, and re-layouts: 7.38 us -> 11.2 us
    ppermute x4, waiting for transfers between devices: 4.49 us -> 0.82 us  [body(): up = lambda value: lax.ppermute(value.astype(BF16), 'tile', TILE_UP)]
    squeeze x2 -> x0, local copies, waits for them, and re-layouts: 2.34 us -> none  [the longest x1 1.48 us: body(): act_theirs[g]]
    ppermute x8, waiting for transfers between devices: 2.97 us -> 5.12 us  [body(): swap = lambda value: lax.ppermute(value, 'text', SWAP)]
    pallas_call x6, Pallas kernels: 2.04 us -> 4.01 us  [hop(): pl.pallas_call(functools.partial(hop_kernel, which, fresh), out_shape=jax...]
    concatenate x1, local copies, waits for them, and re-layouts: 1.63 us -> 3.46 us  [body(): sums = jnp.concatenate([sums, swap(sums)], axis=0)]
  transfers between devices with their start and end apart: 32 -> 32, of which waited for: 6 -> 7; matrix products, arithmetic and copies ran while one was open for 4% -> 5% of each run, Pallas kernels for 40% -> 39%
where the time goes in v5:
time: 181 us; the launch traced here: 180 us
  Pallas kernels  70.8 us (39%)
  starting transfers between devices  38.4 us (21%)
  waiting for transfers between devices  32.4 us (18%)
  local copies, waits for them, and re-layouts  17 us (9%)
  between operations  14.7 us (8%)
  other arithmetic  6.11 us (3%)
    ppermute x15, waiting for transfers between devices, body(): send = lambda value, perm: lax.ppermute(value, 'text', perm)  26.5 us
    pallas_call x3, Pallas kernels, to_slot_order(): pl.pallas_call(functools.partial(slot_kernel, count, not whole, keep), ou...  24.3 us
    ppermute x15, starting transfers between devices, body(): send = lambda value, perm: lax.ppermute(value, 'text', perm)  17.2 us
    pallas_call x1, Pallas kernels, act_in_arrival_order(): pl.pallas_call(act_kernel, out_shape=[jax.ShapeDtypeStruct((GROUPS, HID,...  15.5 us
    pallas_call x4, Pallas kernels, products_of(): pl.pallas_call(functools.partial(product_kernel, hand_on), out_shape=out...  15.1 us
    ppermute x4, starting transfers between devices, body(): down = lambda value: lax.ppermute(value.astype(BF16), 'tile', TILE_DOWN)  13.8 us
    pallas_call x4, Pallas kernels, weight_term(): pl.pallas_call(functools.partial(weight_kernel, group, not totals), out_s...  11.9 us
    unnamed x87, local copies, waits for them, and re-layouts  11.2 us
  transfers between devices with their start and end apart: 32, of which 7 were waited for; matrix products, arithmetic and copies ran while one was open for 5% of the time, Pallas kernels for 39%

profile of v5, /device:TPU:1, one launch (start us, length us, event | category | flops | bytes accessed | tf_op | source)
XLA Modules:
  0.0 179.5 jit_solution(1045723323841549720)
XLA Ops:
  16.2 9.7 %collective-permute-done.1.refs_1_ = bf16[320,1024]{1,0:T(8,128)(2,1)} collective-permute-done((bf16[320,1024]{1,0:T(8,128)(2,1)}, bf16[320,1024]{1,0:T(8,128)(2,1)}, u32[]{:S(2)}, u32[]{:S(2)}) %collective-permute-start.1) | collective-permute-done | bytes 655392 | tf_op jit(solution)/shard_map/ppermute | solution.py:290
  26.3 3.3 %collective-permute-start.4 = (bf16[320,1024]{1,0:T(8,128)(2,1)}, bf16[320,1024]{1,0:T(8,128)(2,1)S(1)}, u32[]{:S(2)}, u32[]{:S(2)}) collective-permute-start(bf16[320,1024]{1,0:T(8,128)(2,1)} %refs_0_.3), channel_id=1, source_target_pairs={{0,24},{1,7},{2,26},{3,1},{4,28},{5,3},{6,30},{7,5},{8,0},{9,15},{... | collective-permute-start | bytes 1966088 | tf_op jit(solution)/shard_map/ppermute | solution.py:290
  29.7 4.5 %products.4 = (f32[2560,128]{1,0:T(8,128)S(1)}, f32[2560,128]{1,0:T(8,128)}, f32[4,1024]{1,0:T(4,128)S(1)}, bf16[320,1024]{1,0:T(8,128)(2,1)}) custom-call(bf16[320,1024]{1,0:T(8,128)(2,1)S(1)} %constant_dynamic-update-slice_fusion.weight_ref, bf16[320,1024]{1,0:T(8,128)(2,1)} %refs_0_.3, bf16[320,1024]{1,0:T(8,128)(2,1)} %collective-permute-done.1.refs_1_, ...), custom_call_target="tpu_custom_call" | custom-call | flops 1300000000 | bytes 8000000 | tf_op jit(solution)/shard_map/products/pallas_call | solution.py:145
  35.5 2.5 %collective-permute-start.9 = (bf16[320,1024]{1,0:T(8,128)(2,1)}, bf16[320,1024]{1,0:T(8,128)(2,1)S(1)}, u32[]{:S(2)}, u32[]{:S(2)}) collective-permute-start(bf16[320,1024]{1,0:T(8,128)(2,1)} %collective-permute-done.2.refs_2_), channel_id=1, source_target_pairs={{0,24},{1,7},{2,26},{3,1},{4,28},{5,3},{6,30},{7,5},{8,0},{9,15},{... | collective-permute-start | bytes 1966088 | tf_op jit(solution)/shard_map/ppermute | solution.py:290
  39.9 6.8 %collective-permute-done.5.refs_1_ = bf16[320,1024]{1,0:T(8,128)(2,1)S(1)} collective-permute-done((bf16[320,1024]{1,0:T(8,128)(2,1)}, bf16[320,1024]{1,0:T(8,128)(2,1)S(1)}, u32[]{:S(2)}, u32[]{:S(2)}) %collective-permute-start.5) | collective-permute-done | bytes 655392 | tf_op jit(solution)/shard_map/ppermute | solution.py:290
  46.7 8.4 %collective-permute-done.7.refs_3_ = bf16[320,1024]{1,0:T(8,128)(2,1)} collective-permute-done((bf16[320,1024]{1,0:T(8,128)(2,1)}, bf16[320,1024]{1,0:T(8,128)(2,1)}, u32[]{:S(2)}, u32[]{:S(2)}) %collective-permute-start.7) | collective-permute-done | bytes 655392 | tf_op jit(solution)/shard_map/ppermute | solution.py:290
  56.1 3.8 %products.5 = (f32[2560,128]{1,0:T(8,128)S(1)}, f32[2560,128]{1,0:T(8,128)}, f32[4,1024]{1,0:T(4,128)S(1)}, bf16[320,1024]{1,0:T(8,128)(2,1)}) custom-call(bf16[320,1024]{1,0:T(8,128)(2,1)S(1)} %copy-done.30, bf16[320,1024]{1,0:T(8,128)(2,1)S(1)} %collective-permute-done.4.refs_0_, bf16[320,1024]{1,0:T(8,128)(2,1)S(1)} %collective-permute-done.5.refs_1_, ...), custom_call_target="tpu_custom_call" | custom-call | flops 1300000000 | bytes 8000000 | tf_op jit(solution)/shard_map/products/pallas_call | solution.py:145
  61.1 2.8 %collective-permute-start.15 = (bf16[320,1024]{1,0:T(8,128)(2,1)S(1)}, bf16[320,1024]{1,0:T(8,128)(2,1)S(1)}, u32[]{:S(2)}, u32[]{:S(2)}) collective-permute-start(bf16[320,1024]{1,0:T(8,128)(2,1)S(1)} %collective-permute-done.12.refs_0_), channel_id=1, source_target_pairs={{0,24},{1,7},{2,26},{3,1},{4,28},{5,3},{6,30},{7,5},{8,0},{9,15},{... | collective-permute-start | bytes 1966088 | tf_op jit(solution)/shard_map/ppermute | solution.py:290
  65.8 15.5 %act_rows.1 = (bf16[4,160,1280]{2,1,0:T(8,128)(2,1)S(1)}, bf16[4,160,1280]{2,1,0:T(8,128)(2,1)}, bf16[320,1024]{1,0:T(8,128)(2,1)S(1)}) custom-call(s32[10240]{0:T(1024)S(1)} %fusion.13.place_ref, bf16[8,160,1280]{2,1,0:T(8,128)(2,1)S(1)} %bitcast.36, bf16[320,1024]{1,0:T(8,128)(2,1)S(1)} %collective-permute-done.9.refs_1_.piece_ref), custom_call_target="tpu_custom_call" | custom-call | bytes 70000000 | tf_op jit(solution)/shard_map/act_rows/pallas_call | solution.py:98
  83.8 4.2 %products.6 = (f32[2560,128]{1,0:T(8,128)S(1)}, f32[2560,128]{1,0:T(8,128)}, f32[4,1024]{1,0:T(4,128)S(1)}) custom-call(bf16[320,1024]{1,0:T(8,128)(2,1)S(1)} %copy-done.31, bf16[320,1024]{1,0:T(8,128)(2,1)} %collective-permute-done.8.refs_0_, bf16[320,1024]{1,0:T(8,128)(2,1)S(1)} %collective-permute-done.9.refs_1_.piece_ref, ...), custom_call_target="tpu_custom_call" | custom-call | flops 1300000000 | bytes 8000000 | tf_op jit(solution)/shard_map/products/pallas_call | solution.py:145
  91.1 2.7 %products.7 = (f32[2560,128]{1,0:T(8,128)S(1)}, f32[2560,128]{1,0:T(8,128)}, f32[4,1024]{1,0:T(4,128)S(1)}) custom-call(bf16[320,1024]{1,0:T(8,128)(2,1)S(1)} %copy-done.31, bf16[320,1024]{1,0:T(8,128)(2,1)S(1)} %collective-permute-done.12.refs_0_, bf16[320,1024]{1,0:T(8,128)(2,1)S(1)} %collective-permute-done.13.refs_1_, ...), custom_call_target="tpu_custom_call" | custom-call | flops 1300000000 | bytes 8000000 | tf_op jit(solution)/shard_map/products/pallas_call | solution.py:145
  96.2 4.7 %collective-permute-done.19.refs_7_ = f32[2560,128]{1,0:T(8,128)S(1)} collective-permute-done((f32[2560,128]{1,0:T(8,128)}, f32[2560,128]{1,0:T(8,128)S(1)}, u32[]{:S(2)}, u32[]{:S(2)}) %collective-permute-start.19) | collective-permute-done | bytes 1310752 | tf_op jit(solution)/shard_map/ppermute | solution.py:289
  101.9 7.0 %slot_rows.3 = (f32[20480,128]{1,0:T(8,128)S(1)}, f32[1,160,1280]{2,1,0:T(8,128)S(1)}) custom-call(s32[10240]{0:T(1024)} %copy-done.13, s32[1]{0:T(128)S(6)} %select_n.118.blocks_ref, f32[2560,128]{1,0:T(8,128)} %copy-done.3, f32[2560,128]{1,0:T(8,128)} %copy-done.5, f32[2560,128]{1,0:T(8,128)} %copy-done.6, f32[2560,128]{1,0:T(8,128)} %copy-done.7, ...), custom_call_target="tpu_custom_call" | custom-call | bytes 8000000 | tf_op jit(solution)/shard_map/slot_rows/pallas_call | solution.py:199
  109.0 5.7 %collective-permute-start.26 = (bf16[80,1280]{1,0:T(8,128)(2,1)S(1)}, bf16[80,1280]{1,0:T(8,128)(2,1)S(1)}, u32[]{:S(2)}, u32[]{:S(2)}) collective-permute-start(bf16[80,1280]{1,0:T(8,128)(2,1)S(1)} %get-tuple-element.57), channel_id=1, source_target_pairs={{0,224},{32,0},{64,32},{96,64},{128,96},{160,128},{192,160},{224,1... | collective-permute-start | bytes 614408 | tf_op jit(solution)/shard_map/ppermute | solution.py:323
  115.9 7.6 %slot_rows.5.terms_ref = f32[4,160,1280]{2,1,0:T(8,128)S(1)} custom-call(s32[10240]{0:T(1024)S(1)} %copy-done.14, s32[4]{0:T(128)S(1)} %and_select_fusion.blocks_ref, f32[20480,128]{1,0:T(8,128)S(1)} %get-tuple-element.42.refs_0_, f32[1,160,1280]{2,1,0:T(8,128)S(1)} %copy-done.10), custom_call_target="tpu_custom_call" | custom-call | bytes 32000000 | tf_op jit(solution)/shard_map/slot_rows/pallas_call | solution.py:199
  125.2 2.7 %collective-permute-start.27 = (bf16[160,1280]{1,0:T(8,128)(2,1)}, bf16[160,1280]{1,0:T(8,128)(2,1)}, u32[]{:S(2)}, u32[]{:S(2)}) collective-permute-start(bf16[160,1280]{1,0:T(8,128)(2,1)} %hop_sum.9), channel_id=1, source_target_pairs={{0,224},{32,0},{64,32},{96,64},{128,96},{160,128},{192,160},{224,1... | collective-permute-start | bytes 1228808 | tf_op jit(solution)/shard_map/ppermute | solution.py:323
  130.2 3.5 %concatenate.12 = f32[32,1024]{1,0:T(8,128)} concatenate(f32[4,1024]{1,0:T(4,128)S(1)} %get-tuple-element.48, f32[4,1024]{1,0:T(4,128)S(1)} %get-tuple-element.49, f32[4,1024]{1,0:T(4,128)} %copy-done.32, f32[4,1024]{1,0:T(4,128)} %copy-done.34, f32[16,1024]{1,0:T(8,128)} %collective-permute-done.23), dimensions={0} | concatenate | bytes 262144 | tf_op jit(solution)/shard_map/concatenate | solution.py:331
  138.4 3.0 %weight_term.4 = (f32[160,1024]{1,0:T(8,128)S(1)}, f32[160,1024]{1,0:T(8,128)S(1)}) custom-call(bf16[4,160,1280]{2,1,0:T(8,128)(2,1)S(1)} %copy-done.1, bf16[4,160,1280]{2,1,0:T(8,128)(2,1)} %collective-permute-done.22.theirs_ref, bf16[320,1024]{1,0:T(8,128)(2,1)} %refs_0_.3, bf16[320,1024]{1,0:T(8,128)(2,1)} %collective-permute-done.1.refs_1_, ...), custom_call_target="tpu_custom_call" | custom-call | flops 1300000000 | bytes 8000000 | tf_op jit(solution)/shard_map/weight_term/pallas_call | solution.py:258
  141.4 2.9 %weight_term.5 = (f32[160,1024]{1,0:T(8,128)S(1)}, f32[160,1024]{1,0:T(8,128)S(1)}) custom-call(bf16[4,160,1280]{2,1,0:T(8,128)(2,1)S(1)} %copy-done.1, bf16[4,160,1280]{2,1,0:T(8,128)(2,1)} %collective-permute-done.22.theirs_ref, bf16[320,1024]{1,0:T(8,128)(2,1)S(1)} %copy-done.20, bf16[320,1024]{1,0:T(8,128)(2,1)S(1)} %copy-done.24, ...), custom_call_target="tpu_custom_call" | custom-call | flops 1300000000 | bytes 8000000 | tf_op jit(solution)/shard_map/weight_term/pallas_call | solution.py:258
  146.8 2.6 %collective-permute-start.28 = (bf16[160,1280]{1,0:T(8,128)(2,1)S(1)}, bf16[160,1280]{1,0:T(8,128)(2,1)S(1)}, u32[]{:S(2)}, u32[]{:S(2)}) collective-permute-start(bf16[160,1280]{1,0:T(8,128)(2,1)S(1)} %hop_sum.10), channel_id=1, source_target_pairs={{0,224},{32,0},{64,32},{96,64},{128,96},{160,128},{192,160},{224,1... | collective-permute-start | bytes 1228808 | tf_op jit(solution)/shard_map/ppermute | solution.py:323
  149.4 9.8 %slot_rows.4.terms_ref = f32[3,160,1280]{2,1,0:T(8,128)S(1)} custom-call(s32[10240]{0:T(1024)S(1)} %copy-done.14, s32[3]{0:T(128)S(1)} %and_select_fusion.1.blocks_ref, f32[2560,128]{1,0:T(8,128)S(1)} %copy-done.4, f32[2560,128]{1,0:T(8,128)} %copy-done.5, f32[2560,128]{1,0:T(8,128)} %copy-done.6, f32[2560,128]{1,0:T(8,128)} %copy-done.7, ...), custom_call_target="tpu_custom_call" | custom-call | bytes 24000000 | tf_op jit(solution)/shard_map/slot_rows/pallas_call | solution.py:199
  159.5 2.7 %collective-permute-start.29 = (bf16[160,1280]{1,0:T(8,128)(2,1)S(1)}, bf16[160,1280]{1,0:T(8,128)(2,1)S(1)}, u32[]{:S(2)}, u32[]{:S(2)}) collective-permute-start(bf16[160,1280]{1,0:T(8,128)(2,1)S(1)} %hop_sum.11), channel_id=1, source_target_pairs={{0,224},{32,0},{64,32},{96,64},{128,96},{160,128},{192,160},{224,1... | collective-permute-start | bytes 1228808 | tf_op jit(solution)/shard_map/ppermute | solution.py:323
  162.3 2.9 %weight_term.6 = (f32[160,1024]{1,0:T(8,128)S(1)}, f32[160,1024]{1,0:T(8,128)S(1)}) custom-call(bf16[4,160,1280]{2,1,0:T(8,128)(2,1)S(1)} %copy-done.2, bf16[4,160,1280]{2,1,0:T(8,128)(2,1)} %collective-permute-done.22.theirs_ref, bf16[320,1024]{1,0:T(8,128)(2,1)} %collective-permute-done.8.refs_0_, bf16[320,1024]{1,0:T(8,128)(2,1)S(1)} %copy-done.12, ...), custom_call_target="tpu_custom_call" | custom-call | flops 1300000000 | bytes 8000000 | tf_op jit(solution)/shard_map/weight_term/pallas_call | solution.py:258
  165.2 3.1 %weight_term.7 = (f32[160,1024]{1,0:T(8,128)S(1)}, f32[160,1024]{1,0:T(8,128)S(1)}) custom-call(bf16[4,160,1280]{2,1,0:T(8,128)(2,1)S(1)} %copy-done.2, bf16[4,160,1280]{2,1,0:T(8,128)(2,1)} %collective-permute-done.22.theirs_ref, bf16[320,1024]{1,0:T(8,128)(2,1)S(1)} %copy-done.16, bf16[320,1024]{1,0:T(8,128)(2,1)S(1)} %copy-done.22, ...), custom_call_target="tpu_custom_call" | custom-call | flops 1300000000 | bytes 8000000 | tf_op jit(solution)/shard_map/weight_term/pallas_call | solution.py:258
  (161 shorter events, 42.7 us)
Async XLA Ops:
  7.2 56.7 %all-gather.3.cloned.1.call-start = ((), (), s32[]{:S(2)}) async-start(), calls=%async_computation | async-start | bytes 3686400 | tf_op jit(solution)/shard_map/all_gather | solution.py:288
  9.7 16.3 %collective-permute-start.1 = (bf16[320,1024]{1,0:T(8,128)(2,1)}, bf16[320,1024]{1,0:T(8,128)(2,1)}, u32[]{:S(2)}, u32[]{:S(2)}) collective-permute-start(bf16[320,1024]{1,0:T(8,128)(2,1)} %refs_0_.3), channel_id=1, source_target_pairs={{0,2},{1,9},{2,4},{3,11},{4,6},{5,13},{6,0},{7,15},{8,10},{9,17},{... | collective-permute-start | bytes 1966088 | tf_op jit(solution)/shard_map/ppermute | solution.py:290
  11.9 17.9 %collective-permute-start.3 = (bf16[320,1024]{1,0:T(8,128)(2,1)}, bf16[320,1024]{1,0:T(8,128)(2,1)}, u32[]{:S(2)}, u32[]{:S(2)}) collective-permute-start(bf16[320,1024]{1,0:T(8,128)(2,1)} %refs_0_.3), channel_id=1, source_target_pairs={{0,8},{1,3},{2,10},{3,5},{4,12},{5,7},{6,14},{7,1},{8,16},{9,11},{... | collective-permute-start | bytes 1966088 | tf_op jit(solution)/shard_map/ppermute | solution.py:290
  13.1 16.7 %collective-permute-start.2 = (bf16[320,1024]{1,0:T(8,128)(2,1)}, bf16[320,1024]{1,0:T(8,128)(2,1)}, u32[]{:S(2)}, u32[]{:S(2)}) collective-permute-start(bf16[320,1024]{1,0:T(8,128)(2,1)} %refs_0_.3), channel_id=1, source_target_pairs={{0,6},{1,25},{2,0},{3,27},{4,2},{5,29},{6,4},{7,31},{8,14},{9,1},{... | collective-permute-start | bytes 1966088 | tf_op jit(solution)/shard_map/ppermute | solution.py:290
  14.6 15.0 %collective-permute-start = (bf16[160,1024]{1,0:T(8,128)(2,1)S(1)}, bf16[160,1024]{1,0:T(8,128)(2,1)S(1)}, u32[]{:S(2)}, u32[]{:S(2)}) collective-permute-start(bf16[160,1024]{1,0:T(8,128)(2,1)S(1)} %copy-done.39), channel_id=1, source_target_pairs={{0,1},{1,0},{2,3},{3,2},{4,5},{5,4},{6,7},{7,6},{8,9},{9,8},{10,11... | collective-permute-start | bytes 983048 | tf_op jit(solution)/shard_map/ppermute | solution.py:289
  26.0 12.1 %collective-permute-start.6 = (bf16[320,1024]{1,0:T(8,128)(2,1)}, bf16[320,1024]{1,0:T(8,128)(2,1)S(1)}, u32[]{:S(2)}, u32[]{:S(2)}) collective-permute-start(bf16[320,1024]{1,0:T(8,128)(2,1)} %collective-permute-done.1.refs_1_), channel_id=1, source_target_pairs={{0,2},{1,9},{2,4},{3,11},{4,6},{5,13},{6,0},{7,15},{8,10},{9,17},{... | collective-permute-start | bytes 1966088 | tf_op jit(solution)/shard_map/ppermute | solution.py:290
  26.3 13.5 %collective-permute-start.4 = (bf16[320,1024]{1,0:T(8,128)(2,1)}, bf16[320,1024]{1,0:T(8,128)(2,1)S(1)}, u32[]{:S(2)}, u32[]{:S(2)}) collective-permute-start(bf16[320,1024]{1,0:T(8,128)(2,1)} %refs_0_.3), channel_id=1, source_target_pairs={{0,24},{1,7},{2,26},{3,1},{4,28},{5,3},{6,30},{7,5},{8,0},{9,15},{... | collective-permute-start | bytes 1966088 | tf_op jit(solution)/shard_map/ppermute | solution.py:290
  29.6 17.0 %collective-permute-start.5 = (bf16[320,1024]{1,0:T(8,128)(2,1)}, bf16[320,1024]{1,0:T(8,128)(2,1)S(1)}, u32[]{:S(2)}, u32[]{:S(2)}) collective-permute-start(bf16[320,1024]{1,0:T(8,128)(2,1)} %collective-permute-done.1.refs_1_), channel_id=1, source_target_pairs={{0,8},{1,3},{2,10},{3,5},{4,12},{5,7},{6,14},{7,1},{8,16},{9,11},{... | collective-permute-start | bytes 1966088 | tf_op jit(solution)/shard_map/ppermute | solution.py:290
  35.4 19.6 %collective-permute-start.7 = (bf16[320,1024]{1,0:T(8,128)(2,1)}, bf16[320,1024]{1,0:T(8,128)(2,1)}, u32[]{:S(2)}, u32[]{:S(2)}) collective-permute-start(bf16[320,1024]{1,0:T(8,128)(2,1)} %get-tuple-element.31), channel_id=1, source_target_pairs={{0,8},{1,3},{2,10},{3,5},{4,12},{5,7},{6,14},{7,1},{8,16},{9,11},{... | collective-permute-start | bytes 1966088 | tf_op jit(solution)/shard_map/ppermute | solution.py:290
  35.5 25.5 %collective-permute-start.9 = (bf16[320,1024]{1,0:T(8,128)(2,1)}, bf16[320,1024]{1,0:T(8,128)(2,1)S(1)}, u32[]{:S(2)}, u32[]{:S(2)}) collective-permute-start(bf16[320,1024]{1,0:T(8,128)(2,1)} %collective-permute-done.2.refs_2_), channel_id=1, source_target_pairs={{0,24},{1,7},{2,26},{3,1},{4,28},{5,3},{6,30},{7,5},{8,0},{9,15},{... | collective-permute-start | bytes 1966088 | tf_op jit(solution)/shard_map/ppermute | solution.py:290
  38.1 23.0 %collective-permute-start.12 = (bf16[320,1024]{1,0:T(8,128)(2,1)S(1)}, bf16[320,1024]{1,0:T(8,128)(2,1)S(1)}, u32[]{:S(2)}, u32[]{:S(2)}) collective-permute-start(bf16[320,1024]{1,0:T(8,128)(2,1)S(1)} %collective-permute-done.6.refs_2_), channel_id=1, source_target_pairs={{0,24},{1,7},{2,26},{3,1},{4,28},{5,3},{6,30},{7,5},{8,0},{9,15},{... | collective-permute-start | bytes 1966088 | tf_op jit(solution)/shard_map/ppermute | solution.py:290
  39.8 41.5 %collective-permute-start.10 = (bf16[320,1024]{1,0:T(8,128)(2,1)}, bf16[320,1024]{1,0:T(8,128)(2,1)}, u32[]{:S(2)}, u32[]{:S(2)}) collective-permute-start(bf16[320,1024]{1,0:T(8,128)(2,1)} %collective-permute-done.3.refs_3_), channel_id=1, source_target_pairs={{0,8},{1,3},{2,10},{3,5},{4,12},{5,7},{6,14},{7,1},{8,16},{9,11},{... | collective-permute-start | bytes 1966088 | tf_op jit(solution)/shard_map/ppermute | solution.py:290
  46.7 36.1 %collective-permute-start.8 = (bf16[320,1024]{1,0:T(8,128)(2,1)}, bf16[320,1024]{1,0:T(8,128)(2,1)}, u32[]{:S(2)}, u32[]{:S(2)}) collective-permute-start(bf16[320,1024]{1,0:T(8,128)(2,1)} %collective-permute-done.1.refs_1_), channel_id=1, source_target_pairs={{0,24},{1,7},{2,26},{3,1},{4,28},{5,3},{6,30},{7,5},{8,0},{9,15},{... | collective-permute-start | bytes 1966088 | tf_op jit(solution)/shard_map/ppermute | solution.py:290
  55.0 28.7 %collective-permute-start.11 = (bf16[320,1024]{1,0:T(8,128)(2,1)S(1)}, bf16[320,1024]{1,0:T(8,128)(2,1)}, u32[]{:S(2)}, u32[]{:S(2)}) collective-permute-start(bf16[320,1024]{1,0:T(8,128)(2,1)S(1)} %collective-permute-done.6.refs_2_), channel_id=1, source_target_pairs={{0,8},{1,3},{2,10},{3,5},{4,12},{5,7},{6,14},{7,1},{8,16},{9,11},{... | collective-permute-start | bytes 1966088 | tf_op jit(solution)/shard_map/ppermute | solution.py:290
  61.1 28.0 %collective-permute-start.13 = (bf16[320,1024]{1,0:T(8,128)(2,1)}, bf16[320,1024]{1,0:T(8,128)(2,1)S(1)}, u32[]{:S(2)}, u32[]{:S(2)}) collective-permute-start(bf16[320,1024]{1,0:T(8,128)(2,1)} %get-tuple-element.34), channel_id=1, source_target_pairs={{0,8},{1,3},{2,10},{3,5},{4,12},{5,7},{6,14},{7,1},{8,16},{9,11},{... | collective-permute-start | bytes 1966088 | tf_op jit(solution)/shard_map/ppermute | solution.py:290
  61.1 28.4 %collective-permute-start.15 = (bf16[320,1024]{1,0:T(8,128)(2,1)S(1)}, bf16[320,1024]{1,0:T(8,128)(2,1)S(1)}, u32[]{:S(2)}, u32[]{:S(2)}) collective-permute-start(bf16[320,1024]{1,0:T(8,128)(2,1)S(1)} %collective-permute-done.12.refs_0_), channel_id=1, source_target_pairs={{0,24},{1,7},{2,26},{3,1},{4,28},{5,3},{6,30},{7,5},{8,0},{9,15},{... | collective-permute-start | bytes 1966088 | tf_op jit(solution)/shard_map/ppermute | solution.py:290
  82.7 13.4 %collective-permute-start.16 = (f32[2560,128]{1,0:T(8,128)}, f32[2560,128]{1,0:T(8,128)}, u32[]{:S(2)}, u32[]{:S(2)}) collective-permute-start(f32[2560,128]{1,0:T(8,128)} %get-tuple-element.37), channel_id=1, source_target_pairs={{0,1},{1,0},{2,3},{3,2},{4,5},{5,4},{6,7},{7,6},{8,9},{9,8},{10,11... | collective-permute-start | bytes 3932168 | tf_op jit(solution)/shard_map/ppermute | solution.py:289
  83.7 12.4 %collective-permute-start.17 = (f32[2560,128]{1,0:T(8,128)}, f32[2560,128]{1,0:T(8,128)}, u32[]{:S(2)}, u32[]{:S(2)}) collective-permute-start(f32[2560,128]{1,0:T(8,128)} %get-tuple-element.38), channel_id=1, source_target_pairs={{0,1},{1,0},{2,3},{3,2},{4,5},{5,4},{6,7},{7,6},{8,9},{9,8},{10,11... | collective-permute-start | bytes 3932168 | tf_op jit(solution)/shard_map/ppermute | solution.py:289
  96.1 40.8 %collective-permute-start.22 = (bf16[4,160,1280]{2,1,0:T(8,128)(2,1)}, bf16[4,160,1280]{2,1,0:T(8,128)(2,1)}, u32[]{:S(2)}, u32[]{:S(2)}) collective-permute-start(bf16[4,160,1280]{2,1,0:T(8,128)(2,1)} %get-tuple-element.44), channel_id=1, source_target_pairs={{0,1},{1,0},{2,3},{3,2},{4,5},{5,4},{6,7},{7,6},{8,9},{9,8},{10,11... | collective-permute-start | bytes 4915208 | tf_op jit(solution)/shard_map/ppermute | solution.py:289
  109.0 15.3 %collective-permute-start.26 = (bf16[80,1280]{1,0:T(8,128)(2,1)S(1)}, bf16[80,1280]{1,0:T(8,128)(2,1)S(1)}, u32[]{:S(2)}, u32[]{:S(2)}) collective-permute-start(bf16[80,1280]{1,0:T(8,128)(2,1)S(1)} %get-tuple-element.57), channel_id=1, source_target_pairs={{0,224},{32,0},{64,32},{96,64},{128,96},{160,128},{192,160},{224,1... | collective-permute-start | bytes 614408 | tf_op jit(solution)/shard_map/ppermute | solution.py:323
  124.4 20.0 %collective-permute-start.21 = (bf16[160,1280]{1,0:T(8,128)(2,1)}, bf16[160,1280]{1,0:T(8,128)(2,1)}, u32[]{:S(2)}, u32[]{:S(2)}) collective-permute-start(bf16[160,1280]{1,0:T(8,128)(2,1)} %hop_sum.6), channel_id=1, source_target_pairs={{0,32},{32,64},{64,96},{96,128},{128,160},{160,192},{192,224},{224... | collective-permute-start | bytes 1228808 | tf_op jit(solution)/shard_map/ppermute | solution.py:322
  125.2 20.4 %collective-permute-start.27 = (bf16[160,1280]{1,0:T(8,128)(2,1)}, bf16[160,1280]{1,0:T(8,128)(2,1)}, u32[]{:S(2)}, u32[]{:S(2)}) collective-permute-start(bf16[160,1280]{1,0:T(8,128)(2,1)} %hop_sum.9), channel_id=1, source_target_pairs={{0,224},{32,0},{64,32},{96,64},{128,96},{160,128},{192,160},{224,1... | collective-permute-start | bytes 1228808 | tf_op jit(solution)/shard_map/ppermute | solution.py:323
  145.5 13.7 %collective-permute-start.24 = (bf16[160,1280]{1,0:T(8,128)(2,1)S(1)}, bf16[160,1280]{1,0:T(8,128)(2,1)S(1)}, u32[]{:S(2)}, u32[]{:S(2)}) collective-permute-start(bf16[160,1280]{1,0:T(8,128)(2,1)S(1)} %hop_sum.7), channel_id=1, source_target_pairs={{0,32},{32,64},{64,96},{96,128},{128,160},{160,192},{192,224},{224... | collective-permute-start | bytes 1228808 | tf_op jit(solution)/shard_map/ppermute | solution.py:322
  146.8 12.7 %collective-permute-start.28 = (bf16[160,1280]{1,0:T(8,128)(2,1)S(1)}, bf16[160,1280]{1,0:T(8,128)(2,1)S(1)}, u32[]{:S(2)}, u32[]{:S(2)}) collective-permute-start(bf16[160,1280]{1,0:T(8,128)(2,1)S(1)} %hop_sum.10), channel_id=1, source_target_pairs={{0,224},{32,0},{64,32},{96,64},{128,96},{160,128},{192,160},{224,1... | collective-permute-start | bytes 1228808 | tf_op jit(solution)/shard_map/ppermute | solution.py:323
  (51 other events, 344.3 us)
Sparse Core Ops, SparseCore 0:
  9.8 50.0 all-gather.2

commit v6 on v5

--- a/solution.py
+++ b/solution.py
@@ -269,6 +269,28 @@
         cost_estimate=pl.CostEstimate(flops=1_300_000_000, bytes_accessed=8_000_000, transcendentals=0),
         name="weight_term",
     )(mine, theirs, *pieces, *totals, *after)
+
+
+def bias_kernel(order_ref, mine_ref, theirs_ref, out_ref, held, ordered):
+    held[0:16, :] = mine_ref[...]
+    held[16:32, :] = theirs_ref[...]
+    for device in range(N_TEXT):
+        ordered[device:device + 1, :] = held[pl.ds(order_ref[device], 1), :]
+    out_ref[...] = jnp.sum(ordered[...], axis=0, keepdims=True)
+
+
+def bias_sum(order, mine, theirs):
+    vmem = pl.BlockSpec(memory_space=pltpu.VMEM)
+    return pl.pallas_call(
+        bias_kernel,
+        out_shape=jax.ShapeDtypeStruct((1, WIDTH), F32),
+        in_specs=[pl.BlockSpec(memory_space=pltpu.SMEM), vmem, vmem],
+        out_specs=vmem,
+        scratch_shapes=[pltpu.VMEM((N_TEXT, WIDTH), F32)] * 2,
+        compiler_params=pltpu.CompilerParams(vmem_limit_bytes=2 * 2**20),
+        cost_estimate=pl.CostEstimate(flops=0, bytes_accessed=1_000_000, transcendentals=0),
+        name="bias_sum",
+    )(order, mine, theirs)[0]
 
 
 def gelu_parts(pre):
@@ -327,16 +349,15 @@
     arrived = [rise]
     totals = weight_term(0, act_mine, act_theirs, groups[0], [], [])
     totals = weight_term(1, act_mine, act_theirs, groups[1], totals, [])
-    sums = jnp.concatenate(sums, axis=0)
-    sums = jnp.concatenate([sums, swap(sums)], axis=0)
-    grad_bias = jnp.sum(sums[piece_of], axis=0)
-    rise, fall = up(hop(2, None, middle, rise, [totals[0], grad_bias])), down(hop(3, None, middle, fall))
+    rise, fall = up(hop(2, None, middle, rise, totals[:1])), down(hop(3, None, middle, fall))
     arrived.append(rise)
     rise, fall = up(hop(0, None, nearest, rise)), down(hop(1, None, nearest, fall))
     grad_pre = (nearest[2] + rise.astype(F32) + fall.astype(F32)) * lax.optimization_barrier(slope)
     for g in range(2, GROUPS):
         totals = weight_term(g, act_mine, act_theirs, groups[g], totals, arrived[1:] if g == 2 else [])
     grad_w = totals[0] + swap(totals[1])
+    sums = jnp.concatenate(sums, axis=0)
+    grad_bias = bias_sum(piece_of, sums, swap(sums))
     return grad_pre.T, grad_w, grad_bias
 
 

time: 181 us -> 171 us (0.945)
  local copies, waits for them, and re-layouts: 17 us -> 9.29 us
    pallas_call x6, Pallas kernels: 4.01 us -> 0.49 us  [hop(): pl.pallas_call(functools.partial(hop_kernel, which, fresh), out_shape=jax...]
    concatenate x1 -> x0, local copies, waits for them, and re-layouts: 3.46 us -> none  [body(): sums = jnp.concatenate([sums, swap(sums)], axis=0)]
    gather x1 -> x0, local copies, waits for them, and re-layouts: 2.33 us -> none  [body(): grad_bias = jnp.sum(sums[piece_of], axis=0)]
    unnamed x87 -> x67, local copies, waits for them, and re-layouts: 11.2 us -> 9.24 us
  transfers between devices with their start and end apart: 32 -> 32, of which waited for: 7 -> 6; matrix products, arithmetic and copies ran while one was open for 5% -> 1% of each run, Pallas kernels for 39% -> 41%
where the time goes in v6:
time: 171 us; the launch traced here: 170 us
  Pallas kernels  69.3 us (41%)
  starting transfers between devices  39.3 us (23%)
  waiting for transfers between devices  33.2 us (19%)
  between operations  14.6 us (9%)
  local copies, waits for them, and re-layouts  9.29 us (5%)
  other arithmetic  4.55 us (3%)
    ppermute x15, waiting for transfers between devices, body(): send = lambda value, perm: lax.ppermute(value, 'text', perm)  25.7 us
    pallas_call x3, Pallas kernels, to_slot_order(): pl.pallas_call(functools.partial(slot_kernel, count, not whole, keep), ou...  24.3 us
    ppermute x15, starting transfers between devices, body(): send = lambda value, perm: lax.ppermute(value, 'text', perm)  17.3 us
    pallas_call x4, Pallas kernels, products_of(): pl.pallas_call(functools.partial(product_kernel, hand_on), out_shape=out...  16.9 us
    pallas_call x1, Pallas kernels, act_in_arrival_order(): pl.pallas_call(act_kernel, out_shape=[jax.ShapeDtypeStruct((GROUPS, HID,...  15.5 us
    ppermute x4, starting transfers between devices, body(): down = lambda value: lax.ppermute(value.astype(BF16), 'tile', TILE_DOWN)  13.9 us
    pallas_call x4, Pallas kernels, weight_term(): pl.pallas_call(functools.partial(weight_kernel, group, not totals), out_s...  10.9 us
    unnamed x67, local copies, waits for them, and re-layouts  9.24 us
  transfers between devices with their start and end apart: 32, of which 6 were waited for; matrix products, arithmetic and copies ran while one was open for 1% of the time, Pallas kernels for 41%

profile of v6, /device:TPU:1, one launch (start us, length us, event | category | flops | bytes accessed | tf_op | source)
XLA Modules:
  0.0 170.3 jit_solution(18070068159853204097)
XLA Ops:
  16.2 9.7 %collective-permute-done.1.refs_1_ = bf16[320,1024]{1,0:T(8,128)(2,1)} collective-permute-done((bf16[320,1024]{1,0:T(8,128)(2,1)}, bf16[320,1024]{1,0:T(8,128)(2,1)}, u32[]{:S(2)}, u32[]{:S(2)}) %collective-permute-start.1) | collective-permute-done | bytes 655392 | tf_op jit(solution)/shard_map/ppermute | solution.py:312
  26.3 3.3 %collective-permute-start.4 = (bf16[320,1024]{1,0:T(8,128)(2,1)}, bf16[320,1024]{1,0:T(8,128)(2,1)S(1)}, u32[]{:S(2)}, u32[]{:S(2)}) collective-permute-start(bf16[320,1024]{1,0:T(8,128)(2,1)} %refs_0_.3), channel_id=1, source_target_pairs={{0,24},{1,7},{2,26},{3,1},{4,28},{5,3},{6,30},{7,5},{8,0},{9,15},{... | collective-permute-start | bytes 1966088 | tf_op jit(solution)/shard_map/ppermute | solution.py:312
  29.7 4.5 %products.4 = (f32[2560,128]{1,0:T(8,128)S(1)}, f32[2560,128]{1,0:T(8,128)}, f32[4,1024]{1,0:T(4,128)S(1)}, bf16[320,1024]{1,0:T(8,128)(2,1)}) custom-call(bf16[320,1024]{1,0:T(8,128)(2,1)S(1)} %constant_dynamic-update-slice_fusion.weight_ref, bf16[320,1024]{1,0:T(8,128)(2,1)} %refs_0_.3, bf16[320,1024]{1,0:T(8,128)(2,1)} %collective-permute-done.1.refs_1_, ...), custom_call_target="tpu_custom_call" | custom-call | flops 1300000000 | bytes 8000000 | tf_op jit(solution)/shard_map/products/pallas_call | solution.py:145
  39.9 6.8 %collective-permute-done.5.refs_1_ = bf16[320,1024]{1,0:T(8,128)(2,1)S(1)} collective-permute-done((bf16[320,1024]{1,0:T(8,128)(2,1)}, bf16[320,1024]{1,0:T(8,128)(2,1)S(1)}, u32[]{:S(2)}, u32[]{:S(2)}) %collective-permute-start.5) | collective-permute-done | bytes 655392 | tf_op jit(solution)/shard_map/ppermute | solution.py:312
  46.7 8.4 %collective-permute-done.7.refs_3_ = bf16[320,1024]{1,0:T(8,128)(2,1)} collective-permute-done((bf16[320,1024]{1,0:T(8,128)(2,1)}, bf16[320,1024]{1,0:T(8,128)(2,1)}, u32[]{:S(2)}, u32[]{:S(2)}) %collective-permute-start.7) | collective-permute-done | bytes 655392 | tf_op jit(solution)/shard_map/ppermute | solution.py:312
  56.1 4.0 %products.5 = (f32[2560,128]{1,0:T(8,128)S(1)}, f32[2560,128]{1,0:T(8,128)}, f32[4,1024]{1,0:T(4,128)S(1)}, bf16[320,1024]{1,0:T(8,128)(2,1)}) custom-call(bf16[320,1024]{1,0:T(8,128)(2,1)S(1)} %copy-done.22, bf16[320,1024]{1,0:T(8,128)(2,1)S(1)} %collective-permute-done.4.refs_0_, bf16[320,1024]{1,0:T(8,128)(2,1)S(1)} %collective-permute-done.5.refs_1_, ...), custom_call_target="tpu_custom_call" | custom-call | flops 1300000000 | bytes 8000000 | tf_op jit(solution)/shard_map/products/pallas_call | solution.py:145
  61.2 2.8 %collective-permute-start.15 = (bf16[320,1024]{1,0:T(8,128)(2,1)S(1)}, bf16[320,1024]{1,0:T(8,128)(2,1)}, u32[]{:S(2)}, u32[]{:S(2)}) collective-permute-start(bf16[320,1024]{1,0:T(8,128)(2,1)S(1)} %collective-permute-done.12.refs_0_), channel_id=1, source_target_pairs={{0,24},{1,7},{2,26},{3,1},{4,28},{5,3},{6,30},{7,5},{8,0},{9,15},{... | collective-permute-start | bytes 1966088 | tf_op jit(solution)/shard_map/ppermute | solution.py:312
  65.9 15.5 %act_rows.1 = (bf16[4,160,1280]{2,1,0:T(8,128)(2,1)S(1)}, bf16[4,160,1280]{2,1,0:T(8,128)(2,1)}, bf16[320,1024]{1,0:T(8,128)(2,1)S(1)}) custom-call(s32[10240]{0:T(1024)S(1)} %fusion.13.place_ref, bf16[8,160,1280]{2,1,0:T(8,128)(2,1)S(1)} %bitcast.35, bf16[320,1024]{1,0:T(8,128)(2,1)S(1)} %collective-permute-done.9.refs_1_.piece_ref), custom_call_target="tpu_custom_call" | custom-call | bytes 70000000 | tf_op jit(solution)/shard_map/act_rows/pallas_call | solution.py:98
  84.1 4.2 %products.6 = (f32[2560,128]{1,0:T(8,128)S(1)}, f32[2560,128]{1,0:T(8,128)}, f32[4,1024]{1,0:T(4,128)S(1)}) custom-call(bf16[320,1024]{1,0:T(8,128)(2,1)S(1)} %copy-done.23, bf16[320,1024]{1,0:T(8,128)(2,1)} %collective-permute-done.8.refs_0_, bf16[320,1024]{1,0:T(8,128)(2,1)S(1)} %collective-permute-done.9.refs_1_.piece_ref, ...), custom_call_target="tpu_custom_call" | custom-call | flops 1300000000 | bytes 8000000 | tf_op jit(solution)/shard_map/products/pallas_call | solution.py:145
  91.2 4.2 %products.7 = (f32[2560,128]{1,0:T(8,128)S(1)}, f32[2560,128]{1,0:T(8,128)}, f32[4,1024]{1,0:T(4,128)S(1)}) custom-call(bf16[320,1024]{1,0:T(8,128)(2,1)S(1)} %copy-done.23, bf16[320,1024]{1,0:T(8,128)(2,1)S(1)} %collective-permute-done.12.refs_0_, bf16[320,1024]{1,0:T(8,128)(2,1)} %collective-permute-done.13.refs_1_, ...), custom_call_target="tpu_custom_call" | custom-call | flops 1300000000 | bytes 8000000 | tf_op jit(solution)/shard_map/products/pallas_call | solution.py:145
  98.5 4.8 %collective-permute-done.19.refs_7_ = f32[2560,128]{1,0:T(8,128)} collective-permute-done((f32[2560,128]{1,0:T(8,128)}, f32[2560,128]{1,0:T(8,128)}, u32[]{:S(2)}, u32[]{:S(2)}) %collective-permute-start.19) | collective-permute-done | bytes 1310752 | tf_op jit(solution)/shard_map/ppermute | solution.py:311
  103.3 7.0 %slot_rows.3 = (f32[20480,128]{1,0:T(8,128)S(1)}, f32[1,160,1280]{2,1,0:T(8,128)S(1)}) custom-call(s32[10240]{0:T(1024)} %copy-done.8, s32[1]{0:T(128)S(6)} %select_n.73.blocks_ref, f32[2560,128]{1,0:T(8,128)} %copy-done, f32[2560,128]{1,0:T(8,128)} %copy-done.2, f32[2560,128]{1,0:T(8,128)} %copy-done.3, f32[2560,128]{1,0:T(8,128)} %copy-done.4, ...), custom_call_target="tpu_custom_call" | custom-call | bytes 8000000 | tf_op jit(solution)/shard_map/slot_rows/pallas_call | solution.py:199
  110.4 5.7 %collective-permute-start.25 = (bf16[80,1280]{1,0:T(8,128)(2,1)S(1)}, bf16[80,1280]{1,0:T(8,128)(2,1)S(1)}, u32[]{:S(2)}, u32[]{:S(2)}) collective-permute-start(bf16[80,1280]{1,0:T(8,128)(2,1)S(1)} %get-tuple-element.57), channel_id=1, source_target_pairs={{0,224},{32,0},{64,32},{96,64},{128,96},{160,128},{192,160},{224,1... | collective-permute-start | bytes 614408 | tf_op jit(solution)/shard_map/ppermute | solution.py:345
  116.2 7.6 %slot_rows.5.terms_ref = f32[4,160,1280]{2,1,0:T(8,128)S(1)} custom-call(s32[10240]{0:T(1024)S(1)} %copy-done.9, s32[4]{0:T(128)S(1)} %and_select_fusion.blocks_ref, f32[20480,128]{1,0:T(8,128)S(1)} %get-tuple-element.42.refs_0_, f32[1,160,1280]{2,1,0:T(8,128)S(1)} %get-tuple-element.41.refs_1_), custom_call_target="tpu_custom_call" | custom-call | bytes 32000000 | tf_op jit(solution)/shard_map/slot_rows/pallas_call | solution.py:199
  124.5 2.7 %collective-permute-start.26 = (bf16[160,1280]{1,0:T(8,128)(2,1)S(1)}, bf16[160,1280]{1,0:T(8,128)(2,1)S(1)}, u32[]{:S(2)}, u32[]{:S(2)}) collective-permute-start(bf16[160,1280]{1,0:T(8,128)(2,1)S(1)} %hop_sum.9), channel_id=1, source_target_pairs={{0,224},{32,0},{64,32},{96,64},{128,96},{160,128},{192,160},{224,1... | collective-permute-start | bytes 1228808 | tf_op jit(solution)/shard_map/ppermute | solution.py:345
  127.3 2.8 %weight_term.4 = (f32[160,1024]{1,0:T(8,128)S(1)}, f32[160,1024]{1,0:T(8,128)S(1)}) custom-call(bf16[4,160,1280]{2,1,0:T(8,128)(2,1)S(1)} %get-tuple-element.43.mine_ref, bf16[4,160,1280]{2,1,0:T(8,128)(2,1)S(1)} %collective-permute-done.22.theirs_ref, bf16[320,1024]{1,0:T(8,128)(2,1)} %refs_0_.3, bf16[320,1024]{1,0:T(8,128)(2,1)} %collective-permute-done.1.refs_1_, ...), custom_call_target="tpu_custom_call" | custom-call | flops 1300000000 | bytes 8000000 | tf_op jit(solution)/shard_map/weight_term/pallas_call | solution.py:258
  130.1 2.8 %weight_term.5 = (f32[160,1024]{1,0:T(8,128)S(1)}, f32[160,1024]{1,0:T(8,128)S(1)}) custom-call(bf16[4,160,1280]{2,1,0:T(8,128)(2,1)S(1)} %get-tuple-element.43.mine_ref, bf16[4,160,1280]{2,1,0:T(8,128)(2,1)S(1)} %collective-permute-done.22.theirs_ref, bf16[320,1024]{1,0:T(8,128)(2,1)S(1)} %copy-done.16, bf16[320,1024]{1,0:T(8,128)(2,1)S(1)} %copy-done.18, ...), custom_call_target="tpu_custom_call" | custom-call | flops 1300000000 | bytes 8000000 | tf_op jit(solution)/shard_map/weight_term/pallas_call | solution.py:258
  132.9 2.6 %collective-permute-done.21.come_ref = bf16[160,1280]{1,0:T(8,128)(2,1)S(1)} collective-permute-done((bf16[160,1280]{1,0:T(8,128)(2,1)S(1)}, bf16[160,1280]{1,0:T(8,128)(2,1)S(1)}, u32[]{:S(2)}, u32[]{:S(2)}) %collective-permute-start.21) | collective-permute-done | bytes 409632 | tf_op jit(solution)/shard_map/ppermute | solution.py:344
  135.9 2.7 %collective-permute-start.27 = (bf16[160,1280]{1,0:T(8,128)(2,1)S(1)}, bf16[160,1280]{1,0:T(8,128)(2,1)S(1)}, u32[]{:S(2)}, u32[]{:S(2)}) collective-permute-start(bf16[160,1280]{1,0:T(8,128)(2,1)S(1)} %hop_sum.10), channel_id=1, source_target_pairs={{0,224},{32,0},{64,32},{96,64},{128,96},{160,128},{192,160},{224,1... | collective-permute-start | bytes 1228808 | tf_op jit(solution)/shard_map/ppermute | solution.py:345
  138.7 9.8 %slot_rows.4.terms_ref = f32[3,160,1280]{2,1,0:T(8,128)S(1)} custom-call(s32[10240]{0:T(1024)S(1)} %copy-done.10, s32[3]{0:T(128)S(1)} %and_select_fusion.1.blocks_ref, f32[2560,128]{1,0:T(8,128)S(1)} %copy-done.1, f32[2560,128]{1,0:T(8,128)} %copy-done.2, f32[2560,128]{1,0:T(8,128)} %copy-done.3, f32[2560,128]{1,0:T(8,128)} %copy-done.4, ...), custom_call_target="tpu_custom_call" | custom-call | bytes 24000000 | tf_op jit(solution)/shard_map/slot_rows/pallas_call | solution.py:199
  148.8 2.7 %collective-permute-start.28 = (bf16[160,1280]{1,0:T(8,128)(2,1)S(1)}, bf16[160,1280]{1,0:T(8,128)(2,1)S(1)}, u32[]{:S(2)}, u32[]{:S(2)}) collective-permute-start(bf16[160,1280]{1,0:T(8,128)(2,1)S(1)} %hop_sum.11), channel_id=1, source_target_pairs={{0,224},{32,0},{64,32},{96,64},{128,96},{160,128},{192,160},{224,1... | collective-permute-start | bytes 1228808 | tf_op jit(solution)/shard_map/ppermute | solution.py:345
  151.5 3.2 %collective-permute-start.30 = (f32[16,1024]{1,0:T(8,128)S(1)}, f32[16,1024]{1,0:T(8,128)S(1)}, u32[]{:S(2)}, u32[]{:S(2)}) collective-permute-start(f32[16,1024]{1,0:T(8,128)S(1)} %pad_maximum_fusion.mine_ref), channel_id=1, source_target_pairs={{0,1},{1,0},{2,3},{3,2},{4,5},{5,4},{6,7},{7,6},{8,9},{9,8},{10,11... | collective-permute-start | bytes 196616 | tf_op jit(solution)/shard_map/ppermute | solution.py:311
  154.7 2.7 %weight_term.6 = (f32[160,1024]{1,0:T(8,128)S(1)}, f32[160,1024]{1,0:T(8,128)S(1)}) custom-call(bf16[4,160,1280]{2,1,0:T(8,128)(2,1)S(1)} %get-tuple-element.43.mine_ref, bf16[4,160,1280]{2,1,0:T(8,128)(2,1)S(1)} %collective-permute-done.22.theirs_ref, bf16[320,1024]{1,0:T(8,128)(2,1)} %collective-permute-done.8.refs_0_, bf16[320,1024]{1,0:T(8,128)(2,1)S(1)} %copy-done.7, ...), custom_call_target="tpu_custom_call" | custom-call | flops 1300000000 | bytes 8000000 | tf_op jit(solution)/shard_map/weight_term/pallas_call | solution.py:258
  157.5 2.6 %weight_term.7 = (f32[160,1024]{1,0:T(8,128)S(1)}, f32[160,1024]{1,0:T(8,128)S(1)}) custom-call(bf16[4,160,1280]{2,1,0:T(8,128)(2,1)S(1)} %get-tuple-element.43.mine_ref, bf16[4,160,1280]{2,1,0:T(8,128)(2,1)S(1)} %collective-permute-done.22.theirs_ref, bf16[320,1024]{1,0:T(8,128)(2,1)S(1)} %copy-done.14, bf16[320,1024]{1,0:T(8,128)(2,1)} %collective-permute-done.13.refs_1_, ...), custom_call_target="tpu_custom_call" | custom-call | flops 1300000000 | bytes 8000000 | tf_op jit(solution)/shard_map/weight_term/pallas_call | solution.py:258
  (138 shorter events, 32.6 us)
Async XLA Ops:
  7.2 56.8 %all-gather.3.cloned.1.call-start = ((), (), s32[]{:S(2)}) async-start(), calls=%async_computation | async-start | bytes 3686400 | tf_op jit(solution)/shard_map/all_gather | solution.py:310
  9.7 16.3 %collective-permute-start.1 = (bf16[320,1024]{1,0:T(8,128)(2,1)}, bf16[320,1024]{1,0:T(8,128)(2,1)}, u32[]{:S(2)}, u32[]{:S(2)}) collective-permute-start(bf16[320,1024]{1,0:T(8,128)(2,1)} %refs_0_.3), channel_id=1, source_target_pairs={{0,2},{1,9},{2,4},{3,11},{4,6},{5,13},{6,0},{7,15},{8,10},{9,17},{... | collective-permute-start | bytes 1966088 | tf_op jit(solution)/shard_map/ppermute | solution.py:312
  11.9 17.9 %collective-permute-start.3 = (bf16[320,1024]{1,0:T(8,128)(2,1)}, bf16[320,1024]{1,0:T(8,128)(2,1)}, u32[]{:S(2)}, u32[]{:S(2)}) collective-permute-start(bf16[320,1024]{1,0:T(8,128)(2,1)} %refs_0_.3), channel_id=1, source_target_pairs={{0,8},{1,3},{2,10},{3,5},{4,12},{5,7},{6,14},{7,1},{8,16},{9,11},{... | collective-permute-start | bytes 1966088 | tf_op jit(solution)/shard_map/ppermute | solution.py:312
  13.1 16.7 %collective-permute-start.2 = (bf16[320,1024]{1,0:T(8,128)(2,1)}, bf16[320,1024]{1,0:T(8,128)(2,1)}, u32[]{:S(2)}, u32[]{:S(2)}) collective-permute-start(bf16[320,1024]{1,0:T(8,128)(2,1)} %refs_0_.3), channel_id=1, source_target_pairs={{0,6},{1,25},{2,0},{3,27},{4,2},{5,29},{6,4},{7,31},{8,14},{9,1},{... | collective-permute-start | bytes 1966088 | tf_op jit(solution)/shard_map/ppermute | solution.py:312
  14.6 15.0 %collective-permute-start = (bf16[160,1024]{1,0:T(8,128)(2,1)S(1)}, bf16[160,1024]{1,0:T(8,128)(2,1)S(1)}, u32[]{:S(2)}, u32[]{:S(2)}) collective-permute-start(bf16[160,1024]{1,0:T(8,128)(2,1)S(1)} %copy-done.29), channel_id=1, source_target_pairs={{0,1},{1,0},{2,3},{3,2},{4,5},{5,4},{6,7},{7,6},{8,9},{9,8},{10,11... | collective-permute-start | bytes 983048 | tf_op jit(solution)/shard_map/ppermute | solution.py:311
  26.0 12.1 %collective-permute-start.6 = (bf16[320,1024]{1,0:T(8,128)(2,1)}, bf16[320,1024]{1,0:T(8,128)(2,1)}, u32[]{:S(2)}, u32[]{:S(2)}) collective-permute-start(bf16[320,1024]{1,0:T(8,128)(2,1)} %collective-permute-done.1.refs_1_), channel_id=1, source_target_pairs={{0,2},{1,9},{2,4},{3,11},{4,6},{5,13},{6,0},{7,15},{8,10},{9,17},{... | collective-permute-start | bytes 1966088 | tf_op jit(solution)/shard_map/ppermute | solution.py:312
  26.3 13.5 %collective-permute-start.4 = (bf16[320,1024]{1,0:T(8,128)(2,1)}, bf16[320,1024]{1,0:T(8,128)(2,1)S(1)}, u32[]{:S(2)}, u32[]{:S(2)}) collective-permute-start(bf16[320,1024]{1,0:T(8,128)(2,1)} %refs_0_.3), channel_id=1, source_target_pairs={{0,24},{1,7},{2,26},{3,1},{4,28},{5,3},{6,30},{7,5},{8,0},{9,15},{... | collective-permute-start | bytes 1966088 | tf_op jit(solution)/shard_map/ppermute | solution.py:312
  29.6 17.0 %collective-permute-start.5 = (bf16[320,1024]{1,0:T(8,128)(2,1)}, bf16[320,1024]{1,0:T(8,128)(2,1)S(1)}, u32[]{:S(2)}, u32[]{:S(2)}) collective-permute-start(bf16[320,1024]{1,0:T(8,128)(2,1)} %collective-permute-done.1.refs_1_), channel_id=1, source_target_pairs={{0,8},{1,3},{2,10},{3,5},{4,12},{5,7},{6,14},{7,1},{8,16},{9,11},{... | collective-permute-start | bytes 1966088 | tf_op jit(solution)/shard_map/ppermute | solution.py:312
  35.3 19.7 %collective-permute-start.7 = (bf16[320,1024]{1,0:T(8,128)(2,1)}, bf16[320,1024]{1,0:T(8,128)(2,1)}, u32[]{:S(2)}, u32[]{:S(2)}) collective-permute-start(bf16[320,1024]{1,0:T(8,128)(2,1)} %get-tuple-element.31), channel_id=1, source_target_pairs={{0,8},{1,3},{2,10},{3,5},{4,12},{5,7},{6,14},{7,1},{8,16},{9,11},{... | collective-permute-start | bytes 1966088 | tf_op jit(solution)/shard_map/ppermute | solution.py:312
  35.5 25.7 %collective-permute-start.9 = (bf16[320,1024]{1,0:T(8,128)(2,1)}, bf16[320,1024]{1,0:T(8,128)(2,1)S(1)}, u32[]{:S(2)}, u32[]{:S(2)}) collective-permute-start(bf16[320,1024]{1,0:T(8,128)(2,1)} %collective-permute-done.2.refs_2_), channel_id=1, source_target_pairs={{0,24},{1,7},{2,26},{3,1},{4,28},{5,3},{6,30},{7,5},{8,0},{9,15},{... | collective-permute-start | bytes 1966088 | tf_op jit(solution)/shard_map/ppermute | solution.py:312
  38.0 23.2 %collective-permute-start.12 = (bf16[320,1024]{1,0:T(8,128)(2,1)}, bf16[320,1024]{1,0:T(8,128)(2,1)S(1)}, u32[]{:S(2)}, u32[]{:S(2)}) collective-permute-start(bf16[320,1024]{1,0:T(8,128)(2,1)} %collective-permute-done.6.refs_2_), channel_id=1, source_target_pairs={{0,24},{1,7},{2,26},{3,1},{4,28},{5,3},{6,30},{7,5},{8,0},{9,15},{... | collective-permute-start | bytes 1966088 | tf_op jit(solution)/shard_map/ppermute | solution.py:312
  39.8 41.7 %collective-permute-start.10 = (bf16[320,1024]{1,0:T(8,128)(2,1)}, bf16[320,1024]{1,0:T(8,128)(2,1)}, u32[]{:S(2)}, u32[]{:S(2)}) collective-permute-start(bf16[320,1024]{1,0:T(8,128)(2,1)} %collective-permute-done.3.refs_3_), channel_id=1, source_target_pairs={{0,8},{1,3},{2,10},{3,5},{4,12},{5,7},{6,14},{7,1},{8,16},{9,11},{... | collective-permute-start | bytes 1966088 | tf_op jit(solution)/shard_map/ppermute | solution.py:312
  46.7 36.2 %collective-permute-start.8 = (bf16[320,1024]{1,0:T(8,128)(2,1)}, bf16[320,1024]{1,0:T(8,128)(2,1)}, u32[]{:S(2)}, u32[]{:S(2)}) collective-permute-start(bf16[320,1024]{1,0:T(8,128)(2,1)} %collective-permute-done.1.refs_1_), channel_id=1, source_target_pairs={{0,24},{1,7},{2,26},{3,1},{4,28},{5,3},{6,30},{7,5},{8,0},{9,15},{... | collective-permute-start | bytes 1966088 | tf_op jit(solution)/shard_map/ppermute | solution.py:312
  55.0 28.9 %collective-permute-start.11 = (bf16[320,1024]{1,0:T(8,128)(2,1)}, bf16[320,1024]{1,0:T(8,128)(2,1)}, u32[]{:S(2)}, u32[]{:S(2)}) collective-permute-start(bf16[320,1024]{1,0:T(8,128)(2,1)} %collective-permute-done.6.refs_2_), channel_id=1, source_target_pairs={{0,8},{1,3},{2,10},{3,5},{4,12},{5,7},{6,14},{7,1},{8,16},{9,11},{... | collective-permute-start | bytes 1966088 | tf_op jit(solution)/shard_map/ppermute | solution.py:312
  61.2 28.7 %collective-permute-start.13 = (bf16[320,1024]{1,0:T(8,128)(2,1)}, bf16[320,1024]{1,0:T(8,128)(2,1)}, u32[]{:S(2)}, u32[]{:S(2)}) collective-permute-start(bf16[320,1024]{1,0:T(8,128)(2,1)} %get-tuple-element.34), channel_id=1, source_target_pairs={{0,8},{1,3},{2,10},{3,5},{4,12},{5,7},{6,14},{7,1},{8,16},{9,11},{... | collective-permute-start | bytes 1966088 | tf_op jit(solution)/shard_map/ppermute | solution.py:312
  61.2 29.1 %collective-permute-start.15 = (bf16[320,1024]{1,0:T(8,128)(2,1)S(1)}, bf16[320,1024]{1,0:T(8,128)(2,1)}, u32[]{:S(2)}, u32[]{:S(2)}) collective-permute-start(bf16[320,1024]{1,0:T(8,128)(2,1)S(1)} %collective-permute-done.12.refs_0_), channel_id=1, source_target_pairs={{0,24},{1,7},{2,26},{3,1},{4,28},{5,3},{6,30},{7,5},{8,0},{9,15},{... | collective-permute-start | bytes 1966088 | tf_op jit(solution)/shard_map/ppermute | solution.py:312
  82.9 15.6 %collective-permute-start.16 = (f32[2560,128]{1,0:T(8,128)}, f32[2560,128]{1,0:T(8,128)}, u32[]{:S(2)}, u32[]{:S(2)}) collective-permute-start(f32[2560,128]{1,0:T(8,128)} %get-tuple-element.37), channel_id=1, source_target_pairs={{0,1},{1,0},{2,3},{3,2},{4,5},{5,4},{6,7},{7,6},{8,9},{9,8},{10,11... | collective-permute-start | bytes 3932168 | tf_op jit(solution)/shard_map/ppermute | solution.py:311
  84.0 14.5 %collective-permute-start.17 = (f32[2560,128]{1,0:T(8,128)}, f32[2560,128]{1,0:T(8,128)}, u32[]{:S(2)}, u32[]{:S(2)}) collective-permute-start(f32[2560,128]{1,0:T(8,128)} %get-tuple-element.38), channel_id=1, source_target_pairs={{0,1},{1,0},{2,3},{3,2},{4,5},{5,4},{6,7},{7,6},{8,9},{9,8},{10,11... | collective-permute-start | bytes 3932168 | tf_op jit(solution)/shard_map/ppermute | solution.py:311
  98.5 28.8 %collective-permute-start.22 = (bf16[4,160,1280]{2,1,0:T(8,128)(2,1)}, bf16[4,160,1280]{2,1,0:T(8,128)(2,1)S(1)}, u32[]{:S(2)}, u32[]{:S(2)}) collective-permute-start(bf16[4,160,1280]{2,1,0:T(8,128)(2,1)} %get-tuple-element.44), channel_id=1, source_target_pairs={{0,1},{1,0},{2,3},{3,2},{4,5},{5,4},{6,7},{7,6},{8,9},{9,8},{10,11... | collective-permute-start | bytes 4915208 | tf_op jit(solution)/shard_map/ppermute | solution.py:311
  110.4 14.0 %collective-permute-start.25 = (bf16[80,1280]{1,0:T(8,128)(2,1)S(1)}, bf16[80,1280]{1,0:T(8,128)(2,1)S(1)}, u32[]{:S(2)}, u32[]{:S(2)}) collective-permute-start(bf16[80,1280]{1,0:T(8,128)(2,1)S(1)} %get-tuple-element.57), channel_id=1, source_target_pairs={{0,224},{32,0},{64,32},{96,64},{128,96},{160,128},{192,160},{224,1... | collective-permute-start | bytes 614408 | tf_op jit(solution)/shard_map/ppermute | solution.py:345
  135.7 12.8 %collective-permute-start.23 = (bf16[160,1280]{1,0:T(8,128)(2,1)S(1)}, bf16[160,1280]{1,0:T(8,128)(2,1)S(1)}, u32[]{:S(2)}, u32[]{:S(2)}) collective-permute-start(bf16[160,1280]{1,0:T(8,128)(2,1)S(1)} %hop_sum.7), channel_id=1, source_target_pairs={{0,32},{32,64},{64,96},{96,128},{128,160},{160,192},{192,224},{224... | collective-permute-start | bytes 1228808 | tf_op jit(solution)/shard_map/ppermute | solution.py:344
  135.9 12.8 %collective-permute-start.27 = (bf16[160,1280]{1,0:T(8,128)(2,1)S(1)}, bf16[160,1280]{1,0:T(8,128)(2,1)S(1)}, u32[]{:S(2)}, u32[]{:S(2)}) collective-permute-start(bf16[160,1280]{1,0:T(8,128)(2,1)S(1)} %hop_sum.10), channel_id=1, source_target_pairs={{0,224},{32,0},{64,32},{96,64},{128,96},{160,128},{192,160},{224,1... | collective-permute-start | bytes 1228808 | tf_op jit(solution)/shard_map/ppermute | solution.py:345
  148.6 12.9 %collective-permute-start.24 = (bf16[160,1280]{1,0:T(8,128)(2,1)S(1)}, bf16[160,1280]{1,0:T(8,128)(2,1)S(1)}, u32[]{:S(2)}, u32[]{:S(2)}) collective-permute-start(bf16[160,1280]{1,0:T(8,128)(2,1)S(1)} %hop_sum.8), channel_id=1, source_target_pairs={{0,32},{32,64},{64,96},{96,128},{128,160},{160,192},{192,224},{224... | collective-permute-start | bytes 1228808 | tf_op jit(solution)/shard_map/ppermute | solution.py:344
  148.8 12.8 %collective-permute-start.28 = (bf16[160,1280]{1,0:T(8,128)(2,1)S(1)}, bf16[160,1280]{1,0:T(8,128)(2,1)S(1)}, u32[]{:S(2)}, u32[]{:S(2)}) collective-permute-start(bf16[160,1280]{1,0:T(8,128)(2,1)S(1)} %hop_sum.11), channel_id=1, source_target_pairs={{0,224},{32,0},{64,32},{96,64},{128,96},{160,128},{192,160},{224,1... | collective-permute-start | bytes 1228808 | tf_op jit(solution)/shard_map/ppermute | solution.py:345
  (41 other events, 281.1 us)
Sparse Core Ops, SparseCore 0:
  9.8 50.0 all-gather.2

commit v7 on v6

--- a/solution.py
+++ b/solution.py
@@ -325,7 +325,9 @@
     mine, theirs, sums = [], [], []
     for g in range(GROUPS):
         pieces = [got[key] for key in ARRIVAL[4 * g:4 * g + 4]]
-        kept, sent, part, *handed = first_products if g == 0 else products_of(weight, pieces, [], 1 if g == 1 else None)
+        kept, sent, part, *handed = first_products if g == 0 else products_of(
+            weight, pieces, [act_theirs] if g == GROUPS - 1 else [], 1 if g == 1 else None
+        )
         if g == 1:
             got[1, 2] = send(handed[0], SECOND_UP)
             got[3, 2], got[2, 2] = send(late_piece, SECOND_DOWN), send(got[2, 3], SECOND_DOWN)

time: 171 us -> 191 us (1.12)
  waiting for transfers between devices: 33.2 us -> 60.1 us
  Pallas kernels: 69.3 us -> 64.4 us
    all_gather x1, waiting for transfers between devices: 0.01 us -> 27.5 us  [body(): act_all = lax.all_gather(activated.astype(BF16), 'tile', axis=0)]
    ppermute x4, starting transfers between devices: 13.9 us -> 9.08 us  [body(): down = lambda value: lax.ppermute(value.astype(BF16), 'tile', TILE_DOWN)]
    pallas_call x4, Pallas kernels: 16.9 us -> 14.2 us  [products_of(): pl.pallas_call(functools.partial(product_kernel, hand_on), out_shape=out...]
    ppermute x8, starting transfers between devices: 7.93 us -> 10.2 us  [body(): swap = lambda value: lax.ppermute(value, 'text', SWAP)]
    unnamed x67 -> x87, local copies, waits for them, and re-layouts: 9.24 us -> 7.17 us
  transfers between devices with their start and end apart: 32 -> 32, of which waited for: 6 -> 10; matrix products, arithmetic and copies ran while one was open for 1% -> 2% of each run, Pallas kernels for 41% -> 30%
where the time goes in v7:
time: 191 us; the launch traced here: 190 us
  Pallas kernels  64.4 us (34%)
  waiting for transfers between devices  60.1 us (31%)
  starting transfers between devices  38.4 us (20%)
  between operations  14.6 us (8%)
  local copies, waits for them, and re-layouts  8.19 us (4%)
  other arithmetic  4.55 us (2%)
    all_gather x1, waiting for transfers between devices, body(): act_all = lax.all_gather(activated.astype(BF16), 'tile', axis=0)  27.5 us
    ppermute x15, waiting for transfers between devices, body(): send = lambda value, perm: lax.ppermute(value, 'text', perm)  26.4 us
    pallas_call x3, Pallas kernels, to_slot_order(): pl.pallas_call(functools.partial(slot_kernel, count, not whole, keep), ou...  24.3 us
    ppermute x15, starting transfers between devices, body(): send = lambda value, perm: lax.ppermute(value, 'text', perm)  18 us
    pallas_call x1, Pallas kernels, act_in_arrival_order(): pl.pallas_call(act_kernel, out_shape=[jax.ShapeDtypeStruct((GROUPS, HID,...  14.3 us
    pallas_call x4, Pallas kernels, products_of(): pl.pallas_call(functools.partial(product_kernel, hand_on), out_shape=out...  14.2 us
    ppermute x8, starting transfers between devices, body(): swap = lambda value: lax.ppermute(value, 'text', SWAP)  10.2 us
    pallas_call x4, Pallas kernels, weight_term(): pl.pallas_call(functools.partial(weight_kernel, group, not totals), out_s...  9.84 us
  transfers between devices with their start and end apart: 32, of which 10 were waited for; matrix products, arithmetic and copies ran while one was open for 2% of the time, Pallas kernels for 30%

profile of v7, /device:TPU:1, one launch (start us, length us, event | category | flops | bytes accessed | tf_op | source)
XLA Modules:
  0.0 190.3 jit_solution(10412292438088539663)
XLA Ops:
  9.7 3.6 %collective-permute-start.2 = (bf16[320,1024]{1,0:T(8,128)(2,1)}, bf16[320,1024]{1,0:T(8,128)(2,1)S(1)}, u32[]{:S(2)}, u32[]{:S(2)}) collective-permute-start(bf16[320,1024]{1,0:T(8,128)(2,1)} %refs_0_.3), channel_id=1, source_target_pairs={{0,6},{1,25},{2,0},{3,27},{4,2},{5,29},{6,4},{7,31},{8,14},{9,1},{... | collective-permute-start | bytes 1966088 | tf_op jit(solution)/shard_map/ppermute | solution.py:312
  13.3 7.8 %collective-permute-done.2.refs_2_ = bf16[320,1024]{1,0:T(8,128)(2,1)S(1)} collective-permute-done((bf16[320,1024]{1,0:T(8,128)(2,1)}, bf16[320,1024]{1,0:T(8,128)(2,1)S(1)}, u32[]{:S(2)}, u32[]{:S(2)}) %collective-permute-start.2) | collective-permute-done | bytes 655392 | tf_op jit(solution)/shard_map/ppermute | solution.py:312
  21.2 2.5 %collective-permute-start.9 = (bf16[320,1024]{1,0:T(8,128)(2,1)S(1)}, bf16[320,1024]{1,0:T(8,128)(2,1)S(1)}, u32[]{:S(2)}, u32[]{:S(2)}) collective-permute-start(bf16[320,1024]{1,0:T(8,128)(2,1)S(1)} %collective-permute-done.2.refs_2_), channel_id=1, source_target_pairs={{0,24},{1,7},{2,26},{3,1},{4,28},{5,3},{6,30},{7,5},{8,0},{9,15},{... | collective-permute-start | bytes 1966088 | tf_op jit(solution)/shard_map/ppermute | solution.py:312
  23.7 2.7 %collective-permute-start.4 = (bf16[320,1024]{1,0:T(8,128)(2,1)}, bf16[320,1024]{1,0:T(8,128)(2,1)}, u32[]{:S(2)}, u32[]{:S(2)}) collective-permute-start(bf16[320,1024]{1,0:T(8,128)(2,1)} %refs_0_.3), channel_id=1, source_target_pairs={{0,24},{1,7},{2,26},{3,1},{4,28},{5,3},{6,30},{7,5},{8,0},{9,15},{... | collective-permute-start | bytes 1966088 | tf_op jit(solution)/shard_map/ppermute | solution.py:312
  32.3 27.5 %all-gather.3.cloned.1.call-done = bf16[1280,1280]{1,0:T(8,128)(2,1)} async-done(((bf16[160,1280]{1,0:T(8,128)(2,1)}), bf16[1280,1280]{1,0:T(8,128)(2,1)}) %all-gather.3.cloned.1.call-update) | async-done | bytes 3276816 | tf_op jit(solution)/shard_map/all_gather | solution.py:310
  61.8 14.3 %act_rows.1 = (bf16[4,160,1280]{2,1,0:T(8,128)(2,1)S(1)}, bf16[4,160,1280]{2,1,0:T(8,128)(2,1)S(1)}, bf16[320,1024]{1,0:T(8,128)(2,1)S(1)}) custom-call(s32[10240]{0:T(1024)S(1)} %fusion.13.place_ref, bf16[8,160,1280]{2,1,0:T(8,128)(2,1)S(1)} %bitcast.35, bf16[320,1024]{1,0:T(8,128)(2,1)S(1)} %collective-permute-done.9.refs_1_.piece_ref), custom_call_target="tpu_custom_call" | custom-call | bytes 70000000 | tf_op jit(solution)/shard_map/act_rows/pallas_call | solution.py:98
  77.9 4.4 %products.4 = (f32[2560,128]{1,0:T(8,128)S(1)}, f32[2560,128]{1,0:T(8,128)}, f32[4,1024]{1,0:T(4,128)S(1)}, bf16[320,1024]{1,0:T(8,128)(2,1)S(1)}) custom-call(bf16[320,1024]{1,0:T(8,128)(2,1)S(1)} %constant_dynamic-update-slice_fusion.weight_ref, bf16[320,1024]{1,0:T(8,128)(2,1)} %refs_0_.3, bf16[320,1024]{1,0:T(8,128)(2,1)} %collective-permute-done.1.refs_1_, ...), custom_call_target="tpu_custom_call" | custom-call | flops 1300000000 | bytes 8000000 | tf_op jit(solution)/shard_map/products/pallas_call | solution.py:145
  87.5 6.8 %collective-permute-done.7.refs_3_ = bf16[320,1024]{1,0:T(8,128)(2,1)S(1)} collective-permute-done((bf16[320,1024]{1,0:T(8,128)(2,1)S(1)}, bf16[320,1024]{1,0:T(8,128)(2,1)S(1)}, u32[]{:S(2)}, u32[]{:S(2)}) %collective-permute-start.7) | collective-permute-done | bytes 655392 | tf_op jit(solution)/shard_map/ppermute | solution.py:312
  94.3 4.6 %products.5 = (f32[2560,128]{1,0:T(8,128)S(1)}, f32[2560,128]{1,0:T(8,128)}, f32[4,1024]{1,0:T(4,128)S(1)}, bf16[320,1024]{1,0:T(8,128)(2,1)S(1)}) custom-call(bf16[320,1024]{1,0:T(8,128)(2,1)S(1)} %constant_dynamic-update-slice_fusion.weight_ref, bf16[320,1024]{1,0:T(8,128)(2,1)} %collective-permute-done.4.refs_0_, ...), custom_call_target="tpu_custom_call" | custom-call | flops 1300000000 | bytes 8000000 | tf_op jit(solution)/shard_map/products/pallas_call | solution.py:145
  101.3 2.7 %collective-permute-start.15 = (bf16[320,1024]{1,0:T(8,128)(2,1)S(1)}, bf16[320,1024]{1,0:T(8,128)(2,1)S(1)}, u32[]{:S(2)}, u32[]{:S(2)}) collective-permute-start(bf16[320,1024]{1,0:T(8,128)(2,1)S(1)} %collective-permute-done.12.refs_0_), channel_id=1, source_target_pairs={{0,24},{1,7},{2,26},{3,1},{4,28},{5,3},{6,30},{7,5},{8,0},{9,15},{... | collective-permute-start | bytes 1966088 | tf_op jit(solution)/shard_map/ppermute | solution.py:312
  105.4 2.9 %collective-permute-done.11.refs_3_ = bf16[320,1024]{1,0:T(8,128)(2,1)S(1)} collective-permute-done((bf16[320,1024]{1,0:T(8,128)(2,1)}, bf16[320,1024]{1,0:T(8,128)(2,1)S(1)}, u32[]{:S(2)}, u32[]{:S(2)}) %collective-permute-start.11) | collective-permute-done | bytes 655392 | tf_op jit(solution)/shard_map/ppermute | solution.py:312
  109.2 2.7 %products.6 = (f32[2560,128]{1,0:T(8,128)S(1)}, f32[2560,128]{1,0:T(8,128)}, f32[4,1024]{1,0:T(4,128)S(1)}) custom-call(bf16[320,1024]{1,0:T(8,128)(2,1)S(1)} %constant_dynamic-update-slice_fusion.weight_ref, bf16[320,1024]{1,0:T(8,128)(2,1)S(1)} %collective-permute-done.8.refs_0_, bf16[320,1024]{1,0:T(8,128)(2,1)S(1)} %copy-done.15, ...), custom_call_target="tpu_custom_call" | custom-call | flops 1300000000 | bytes 8000000 | tf_op jit(solution)/shard_map/products/pallas_call | solution.py:145
  111.9 3.5 %collective-permute-done.13.refs_1_ = bf16[320,1024]{1,0:T(8,128)(2,1)S(1)} collective-permute-done((bf16[320,1024]{1,0:T(8,128)(2,1)S(1)}, bf16[320,1024]{1,0:T(8,128)(2,1)S(1)}, u32[]{:S(2)}, u32[]{:S(2)}) %collective-permute-start.13) | collective-permute-done | bytes 655392 | tf_op jit(solution)/shard_map/ppermute | solution.py:312
  118.5 2.7 %products.7 = (f32[2560,128]{1,0:T(8,128)S(1)}, f32[2560,128]{1,0:T(8,128)}, f32[4,1024]{1,0:T(4,128)S(1)}) custom-call(bf16[320,1024]{1,0:T(8,128)(2,1)S(1)} %constant_dynamic-update-slice_fusion.weight_ref, bf16[320,1024]{1,0:T(8,128)(2,1)S(1)} %collective-permute-done.12.refs_0_, bf16[320,1024]{1,0:T(8,128)(2,1)S(1)} %collective-permute-done.13.refs_1_, ...), custom_call_target="tpu_custom_call" | custom-call | flops 1300000000 | bytes 8000000 | tf_op jit(solution)/shard_map/products/pallas_call | solution.py:145
  124.9 3.0 %collective-permute-done.20.refs_7_ = f32[2560,128]{1,0:T(8,128)} collective-permute-done((f32[2560,128]{1,0:T(8,128)}, f32[2560,128]{1,0:T(8,128)}, u32[]{:S(2)}, u32[]{:S(2)}) %collective-permute-start.20) | collective-permute-done | bytes 1310752 | tf_op jit(solution)/shard_map/ppermute | solution.py:311
  127.9 7.0 %slot_rows.3 = (f32[20480,128]{1,0:T(8,128)S(1)}, f32[1,160,1280]{2,1,0:T(8,128)S(1)}) custom-call(s32[10240]{0:T(1024)} %copy-done.18, s32[1]{0:T(128)S(6)} %select_n.73.blocks_ref, f32[2560,128]{1,0:T(8,128)} %copy-done, f32[2560,128]{1,0:T(8,128)} %copy-done.2, f32[2560,128]{1,0:T(8,128)} %copy-done.3, f32[2560,128]{1,0:T(8,128)} %copy-done.4, ...), custom_call_target="tpu_custom_call" | custom-call | bytes 8000000 | tf_op jit(solution)/shard_map/slot_rows/pallas_call | solution.py:199
  136.7 7.6 %slot_rows.5.terms_ref = f32[4,160,1280]{2,1,0:T(8,128)S(1)} custom-call(s32[10240]{0:T(1024)S(1)} %copy-done.19, s32[4]{0:T(128)S(1)} %and_select_fusion.blocks_ref, f32[20480,128]{1,0:T(8,128)S(1)} %get-tuple-element.43.refs_0_, f32[1,160,1280]{2,1,0:T(8,128)S(1)} %get-tuple-element.42.refs_1_), custom_call_target="tpu_custom_call" | custom-call | bytes 32000000 | tf_op jit(solution)/shard_map/slot_rows/pallas_call | solution.py:199
  147.8 2.7 %weight_term.4 = (f32[160,1024]{1,0:T(8,128)S(1)}, f32[160,1024]{1,0:T(8,128)S(1)}) custom-call(bf16[4,160,1280]{2,1,0:T(8,128)(2,1)S(1)} %get-tuple-element.44.mine_ref, bf16[4,160,1280]{2,1,0:T(8,128)(2,1)S(1)} %collective-permute-done.16.refs_4_.theirs_ref, bf16[320,1024]{1,0:T(8,128)(2,1)} %refs_0_.3, bf16[320,1024]{1,0:T(8,128)(2,1)} %collective-permute-done.1.refs_1_, ...), custom_call_target="tpu_custom_call" | custom-call | flops 1300000000 | bytes 8000000 | tf_op jit(solution)/shard_map/weight_term/pallas_call | solution.py:258
  150.5 2.6 %weight_term.5 = (f32[160,1024]{1,0:T(8,128)S(1)}, f32[160,1024]{1,0:T(8,128)S(1)}) custom-call(bf16[4,160,1280]{2,1,0:T(8,128)(2,1)S(1)} %get-tuple-element.44.mine_ref, bf16[4,160,1280]{2,1,0:T(8,128)(2,1)S(1)} %collective-permute-done.16.refs_4_.theirs_ref, bf16[320,1024]{1,0:T(8,128)(2,1)} %collective-permute-done.4.refs_0_, ...), custom_call_target="tpu_custom_call" | custom-call | flops 1300000000 | bytes 8000000 | tf_op jit(solution)/shard_map/weight_term/pallas_call | solution.py:258
  153.1 3.2 %collective-permute-done.22.come_ref = bf16[160,1280]{1,0:T(8,128)(2,1)S(1)} collective-permute-done((bf16[160,1280]{1,0:T(8,128)(2,1)S(1)}, bf16[160,1280]{1,0:T(8,128)(2,1)S(1)}, u32[]{:S(2)}, u32[]{:S(2)}) %collective-permute-start.22) | collective-permute-done | bytes 409632 | tf_op jit(solution)/shard_map/ppermute | solution.py:346
  156.6 2.7 %collective-permute-start.27 = (bf16[160,1280]{1,0:T(8,128)(2,1)S(1)}, bf16[160,1280]{1,0:T(8,128)(2,1)S(1)}, u32[]{:S(2)}, u32[]{:S(2)}) collective-permute-start(bf16[160,1280]{1,0:T(8,128)(2,1)S(1)} %hop_sum.10), channel_id=1, source_target_pairs={{0,224},{32,0},{64,32},{96,64},{128,96},{160,128},{192,160},{224,1... | collective-permute-start | bytes 1228808 | tf_op jit(solution)/shard_map/ppermute | solution.py:347
  159.4 9.8 %slot_rows.4.terms_ref = f32[3,160,1280]{2,1,0:T(8,128)S(1)} custom-call(s32[10240]{0:T(1024)S(1)} %copy-done.20, s32[3]{0:T(128)S(1)} %and_select_fusion.1.blocks_ref, f32[2560,128]{1,0:T(8,128)S(1)} %copy-done.1, f32[2560,128]{1,0:T(8,128)} %copy-done.2, f32[2560,128]{1,0:T(8,128)} %copy-done.3, f32[2560,128]{1,0:T(8,128)} %copy-done.4, ...), custom_call_target="tpu_custom_call" | custom-call | bytes 24000000 | tf_op jit(solution)/shard_map/slot_rows/pallas_call | solution.py:199
  169.5 2.7 %collective-permute-start.28 = (bf16[160,1280]{1,0:T(8,128)(2,1)S(1)}, bf16[160,1280]{1,0:T(8,128)(2,1)S(1)}, u32[]{:S(2)}, u32[]{:S(2)}) collective-permute-start(bf16[160,1280]{1,0:T(8,128)(2,1)S(1)} %hop_sum.11), channel_id=1, source_target_pairs={{0,224},{32,0},{64,32},{96,64},{128,96},{160,128},{192,160},{224,1... | collective-permute-start | bytes 1228808 | tf_op jit(solution)/shard_map/ppermute | solution.py:347
  172.3 3.1 %collective-permute-start.30 = (f32[16,1024]{1,0:T(8,128)S(1)}, f32[16,1024]{1,0:T(8,128)S(1)}, u32[]{:S(2)}, u32[]{:S(2)}) collective-permute-start(f32[16,1024]{1,0:T(8,128)S(1)} %pad_maximum_fusion.mine_ref), channel_id=1, source_target_pairs={{0,1},{1,0},{2,3},{3,2},{4,5},{5,4},{6,7},{7,6},{8,9},{9,8},{10,11... | collective-permute-start | bytes 196616 | tf_op jit(solution)/shard_map/ppermute | solution.py:311
  (158 shorter events, 42.9 us)
Async XLA Ops:
  7.2 52.7 %all-gather.3.cloned.1.call-start = ((), (), s32[]{:S(2)}) async-start(), calls=%async_computation | async-start | bytes 3686400 | tf_op jit(solution)/shard_map/all_gather | solution.py:310
  9.7 11.5 %collective-permute-start.2 = (bf16[320,1024]{1,0:T(8,128)(2,1)}, bf16[320,1024]{1,0:T(8,128)(2,1)S(1)}, u32[]{:S(2)}, u32[]{:S(2)}) collective-permute-start(bf16[320,1024]{1,0:T(8,128)(2,1)} %refs_0_.3), channel_id=1, source_target_pairs={{0,6},{1,25},{2,0},{3,27},{4,2},{5,29},{6,4},{7,31},{8,14},{9,1},{... | collective-permute-start | bytes 1966088 | tf_op jit(solution)/shard_map/ppermute | solution.py:312
  13.3 16.1 %collective-permute-start.1 = (bf16[320,1024]{1,0:T(8,128)(2,1)}, bf16[320,1024]{1,0:T(8,128)(2,1)}, u32[]{:S(2)}, u32[]{:S(2)}) collective-permute-start(bf16[320,1024]{1,0:T(8,128)(2,1)} %refs_0_.3), channel_id=1, source_target_pairs={{0,2},{1,9},{2,4},{3,11},{4,6},{5,13},{6,0},{7,15},{8,10},{9,17},{... | collective-permute-start | bytes 1966088 | tf_op jit(solution)/shard_map/ppermute | solution.py:312
  23.6 54.2 %collective-permute-start.3 = (bf16[320,1024]{1,0:T(8,128)(2,1)}, bf16[320,1024]{1,0:T(8,128)(2,1)}, u32[]{:S(2)}, u32[]{:S(2)}) collective-permute-start(bf16[320,1024]{1,0:T(8,128)(2,1)} %refs_0_.3), channel_id=1, source_target_pairs={{0,8},{1,3},{2,10},{3,5},{4,12},{5,7},{6,14},{7,1},{8,16},{9,11},{... | collective-permute-start | bytes 1966088 | tf_op jit(solution)/shard_map/ppermute | solution.py:312
  23.7 60.9 %collective-permute-start.4 = (bf16[320,1024]{1,0:T(8,128)(2,1)}, bf16[320,1024]{1,0:T(8,128)(2,1)}, u32[]{:S(2)}, u32[]{:S(2)}) collective-permute-start(bf16[320,1024]{1,0:T(8,128)(2,1)} %refs_0_.3), channel_id=1, source_target_pairs={{0,24},{1,7},{2,26},{3,1},{4,28},{5,3},{6,30},{7,5},{8,0},{9,15},{... | collective-permute-start | bytes 1966088 | tf_op jit(solution)/shard_map/ppermute | solution.py:312
  26.3 49.8 %collective-permute-start = (bf16[160,1024]{1,0:T(8,128)(2,1)S(1)}, bf16[160,1024]{1,0:T(8,128)(2,1)}, u32[]{:S(2)}, u32[]{:S(2)}) collective-permute-start(bf16[160,1024]{1,0:T(8,128)(2,1)S(1)} %copy-done.39), channel_id=1, source_target_pairs={{0,1},{1,0},{2,3},{3,2},{4,5},{5,4},{6,7},{7,6},{8,9},{9,8},{10,11... | collective-permute-start | bytes 983048 | tf_op jit(solution)/shard_map/ppermute | solution.py:311
  29.4 56.3 %collective-permute-start.6 = (bf16[320,1024]{1,0:T(8,128)(2,1)}, bf16[320,1024]{1,0:T(8,128)(2,1)}, u32[]{:S(2)}, u32[]{:S(2)}) collective-permute-start(bf16[320,1024]{1,0:T(8,128)(2,1)} %collective-permute-done.1.refs_1_), channel_id=1, source_target_pairs={{0,2},{1,9},{2,4},{3,11},{4,6},{5,13},{6,0},{7,15},{8,10},{9,17},{... | collective-permute-start | bytes 1966088 | tf_op jit(solution)/shard_map/ppermute | solution.py:312
  31.2 56.0 %collective-permute-start.5 = (bf16[320,1024]{1,0:T(8,128)(2,1)}, bf16[320,1024]{1,0:T(8,128)(2,1)}, u32[]{:S(2)}, u32[]{:S(2)}) collective-permute-start(bf16[320,1024]{1,0:T(8,128)(2,1)} %collective-permute-done.1.refs_1_), channel_id=1, source_target_pairs={{0,8},{1,3},{2,10},{3,5},{4,12},{5,7},{6,14},{7,1},{8,16},{9,11},{... | collective-permute-start | bytes 1966088 | tf_op jit(solution)/shard_map/ppermute | solution.py:312
  76.1 42.4 %collective-permute-start.16 = (bf16[4,160,1280]{2,1,0:T(8,128)(2,1)S(1)}, bf16[4,160,1280]{2,1,0:T(8,128)(2,1)S(1)}, u32[]{:S(2)}, u32[]{:S(2)}) collective-permute-start(bf16[4,160,1280]{2,1,0:T(8,128)(2,1)S(1)} %get-tuple-element.36), channel_id=1, source_target_pairs={{0,1},{1,0},{2,3},{3,2},{4,5},{5,4},{6,7},{7,6},{8,9},{9,8},{10,11... | collective-permute-start | bytes 4915208 | tf_op jit(solution)/shard_map/ppermute | solution.py:311
  83.3 10.9 %collective-permute-start.7 = (bf16[320,1024]{1,0:T(8,128)(2,1)S(1)}, bf16[320,1024]{1,0:T(8,128)(2,1)S(1)}, u32[]{:S(2)}, u32[]{:S(2)}) collective-permute-start(bf16[320,1024]{1,0:T(8,128)(2,1)S(1)} %get-tuple-element.31), channel_id=1, source_target_pairs={{0,8},{1,3},{2,10},{3,5},{4,12},{5,7},{6,14},{7,1},{8,16},{9,11},{... | collective-permute-start | bytes 1966088 | tf_op jit(solution)/shard_map/ppermute | solution.py:312
  84.5 16.8 %collective-permute-start.10 = (bf16[320,1024]{1,0:T(8,128)(2,1)}, bf16[320,1024]{1,0:T(8,128)(2,1)S(1)}, u32[]{:S(2)}, u32[]{:S(2)}) collective-permute-start(bf16[320,1024]{1,0:T(8,128)(2,1)} %collective-permute-done.3.refs_3_), channel_id=1, source_target_pairs={{0,8},{1,3},{2,10},{3,5},{4,12},{5,7},{6,14},{7,1},{8,16},{9,11},{... | collective-permute-start | bytes 1966088 | tf_op jit(solution)/shard_map/ppermute | solution.py:312
  85.7 15.6 %collective-permute-start.12 = (bf16[320,1024]{1,0:T(8,128)(2,1)}, bf16[320,1024]{1,0:T(8,128)(2,1)S(1)}, u32[]{:S(2)}, u32[]{:S(2)}) collective-permute-start(bf16[320,1024]{1,0:T(8,128)(2,1)} %collective-permute-done.6.refs_2_), channel_id=1, source_target_pairs={{0,24},{1,7},{2,26},{3,1},{4,28},{5,3},{6,30},{7,5},{8,0},{9,15},{... | collective-permute-start | bytes 1966088 | tf_op jit(solution)/shard_map/ppermute | solution.py:312
  87.2 16.8 %collective-permute-start.8 = (bf16[320,1024]{1,0:T(8,128)(2,1)}, bf16[320,1024]{1,0:T(8,128)(2,1)S(1)}, u32[]{:S(2)}, u32[]{:S(2)}) collective-permute-start(bf16[320,1024]{1,0:T(8,128)(2,1)} %collective-permute-done.1.refs_1_), channel_id=1, source_target_pairs={{0,24},{1,7},{2,26},{3,1},{4,28},{5,3},{6,30},{7,5},{8,0},{9,15},{... | collective-permute-start | bytes 1966088 | tf_op jit(solution)/shard_map/ppermute | solution.py:312
  94.3 14.0 %collective-permute-start.11 = (bf16[320,1024]{1,0:T(8,128)(2,1)}, bf16[320,1024]{1,0:T(8,128)(2,1)S(1)}, u32[]{:S(2)}, u32[]{:S(2)}) collective-permute-start(bf16[320,1024]{1,0:T(8,128)(2,1)} %collective-permute-done.6.refs_2_), channel_id=1, source_target_pairs={{0,8},{1,3},{2,10},{3,5},{4,12},{5,7},{6,14},{7,1},{8,16},{9,11},{... | collective-permute-start | bytes 1966088 | tf_op jit(solution)/shard_map/ppermute | solution.py:312
  101.3 14.0 %collective-permute-start.13 = (bf16[320,1024]{1,0:T(8,128)(2,1)S(1)}, bf16[320,1024]{1,0:T(8,128)(2,1)S(1)}, u32[]{:S(2)}, u32[]{:S(2)}) collective-permute-start(bf16[320,1024]{1,0:T(8,128)(2,1)S(1)} %get-tuple-element.34), channel_id=1, source_target_pairs={{0,8},{1,3},{2,10},{3,5},{4,12},{5,7},{6,14},{7,1},{8,16},{9,11},{... | collective-permute-start | bytes 1966088 | tf_op jit(solution)/shard_map/ppermute | solution.py:312
  101.3 14.9 %collective-permute-start.15 = (bf16[320,1024]{1,0:T(8,128)(2,1)S(1)}, bf16[320,1024]{1,0:T(8,128)(2,1)S(1)}, u32[]{:S(2)}, u32[]{:S(2)}) collective-permute-start(bf16[320,1024]{1,0:T(8,128)(2,1)S(1)} %collective-permute-done.12.refs_0_), channel_id=1, source_target_pairs={{0,24},{1,7},{2,26},{3,1},{4,28},{5,3},{6,30},{7,5},{8,0},{9,15},{... | collective-permute-start | bytes 1966088 | tf_op jit(solution)/shard_map/ppermute | solution.py:312
  104.0 14.5 %collective-permute-start.14 = (bf16[320,1024]{1,0:T(8,128)(2,1)S(1)}, bf16[320,1024]{1,0:T(8,128)(2,1)S(1)}, u32[]{:S(2)}, u32[]{:S(2)}) collective-permute-start(bf16[320,1024]{1,0:T(8,128)(2,1)S(1)} %get-tuple-element.35), channel_id=1, source_target_pairs={{0,24},{1,7},{2,26},{3,1},{4,28},{5,3},{6,30},{7,5},{8,0},{9,15},{... | collective-permute-start | bytes 1966088 | tf_op jit(solution)/shard_map/ppermute | solution.py:312
  108.3 16.6 %collective-permute-start.17 = (f32[2560,128]{1,0:T(8,128)}, f32[2560,128]{1,0:T(8,128)}, u32[]{:S(2)}, u32[]{:S(2)}) collective-permute-start(f32[2560,128]{1,0:T(8,128)} %get-tuple-element.38), channel_id=1, source_target_pairs={{0,1},{1,0},{2,3},{3,2},{4,5},{5,4},{6,7},{7,6},{8,9},{9,8},{10,11... | collective-permute-start | bytes 3932168 | tf_op jit(solution)/shard_map/ppermute | solution.py:311
  145.0 11.2 %collective-permute-start.22 = (bf16[160,1280]{1,0:T(8,128)(2,1)S(1)}, bf16[160,1280]{1,0:T(8,128)(2,1)S(1)}, u32[]{:S(2)}, u32[]{:S(2)}) collective-permute-start(bf16[160,1280]{1,0:T(8,128)(2,1)S(1)} %hop_sum.6), channel_id=1, source_target_pairs={{0,32},{32,64},{64,96},{96,128},{128,160},{160,192},{192,224},{224... | collective-permute-start | bytes 1228808 | tf_op jit(solution)/shard_map/ppermute | solution.py:346
  145.7 10.8 %collective-permute-start.26 = (bf16[160,1280]{1,0:T(8,128)(2,1)S(1)}, bf16[160,1280]{1,0:T(8,128)(2,1)S(1)}, u32[]{:S(2)}, u32[]{:S(2)}) collective-permute-start(bf16[160,1280]{1,0:T(8,128)(2,1)S(1)} %hop_sum.9), channel_id=1, source_target_pairs={{0,224},{32,0},{64,32},{96,64},{128,96},{160,128},{192,160},{224,1... | collective-permute-start | bytes 1228808 | tf_op jit(solution)/shard_map/ppermute | solution.py:347
  156.4 12.8 %collective-permute-start.23 = (bf16[160,1280]{1,0:T(8,128)(2,1)S(1)}, bf16[160,1280]{1,0:T(8,128)(2,1)S(1)}, u32[]{:S(2)}, u32[]{:S(2)}) collective-permute-start(bf16[160,1280]{1,0:T(8,128)(2,1)S(1)} %hop_sum.7), channel_id=1, source_target_pairs={{0,32},{32,64},{64,96},{96,128},{128,160},{160,192},{192,224},{224... | collective-permute-start | bytes 1228808 | tf_op jit(solution)/shard_map/ppermute | solution.py:346
  156.6 12.8 %collective-permute-start.27 = (bf16[160,1280]{1,0:T(8,128)(2,1)S(1)}, bf16[160,1280]{1,0:T(8,128)(2,1)S(1)}, u32[]{:S(2)}, u32[]{:S(2)}) collective-permute-start(bf16[160,1280]{1,0:T(8,128)(2,1)S(1)} %hop_sum.10), channel_id=1, source_target_pairs={{0,224},{32,0},{64,32},{96,64},{128,96},{160,128},{192,160},{224,1... | collective-permute-start | bytes 1228808 | tf_op jit(solution)/shard_map/ppermute | solution.py:347
  169.3 12.1 %collective-permute-start.24 = (bf16[160,1280]{1,0:T(8,128)(2,1)S(1)}, bf16[160,1280]{1,0:T(8,128)(2,1)S(1)}, u32[]{:S(2)}, u32[]{:S(2)}) collective-permute-start(bf16[160,1280]{1,0:T(8,128)(2,1)S(1)} %hop_sum.8), channel_id=1, source_target_pairs={{0,32},{32,64},{64,96},{96,128},{128,160},{160,192},{192,224},{224... | collective-permute-start | bytes 1228808 | tf_op jit(solution)/shard_map/ppermute | solution.py:346
  169.5 11.9 %collective-permute-start.28 = (bf16[160,1280]{1,0:T(8,128)(2,1)S(1)}, bf16[160,1280]{1,0:T(8,128)(2,1)S(1)}, u32[]{:S(2)}, u32[]{:S(2)}) collective-permute-start(bf16[160,1280]{1,0:T(8,128)(2,1)S(1)} %hop_sum.11), channel_id=1, source_target_pairs={{0,224},{32,0},{64,32},{96,64},{128,96},{160,128},{192,160},{224,1... | collective-permute-start | bytes 1228808 | tf_op jit(solution)/shard_map/ppermute | solution.py:347
  (51 other events, 408.9 us)
Sparse Core Ops, SparseCore 0:
  9.8 50.0 all-gather.2
